TPU v7x, 512 devices: a whole 4x4x16 slice. The times are simulated.
512 devices in a mesh: dom: 128 (over x, z, core), tile: 4 (over y).
Axes of the slice: x: 4, y: 4, z: 16, core: 2. Of those that a mesh axis runs over, the one named last changes fastest.
Arguments:
- pumping: float32 [8192, 4096], P(('dom', 'tile')), may hold values from -36 to 36
- coupling: float32 [8192, 4096], P(('dom', 'tile')), may hold values from -0.75 to 0.75
- storage: float32 [8192, 64], P(('dom', 'tile')), may hold values from 0.2 to 2
- tile_order: int32 [512, 1024], P(('dom', 'tile')), may hold values from 0 to 1023, each once within a row
- kriging: bfloat16 [8192, 1024], P(('dom', 'tile')), may hold values from -0.75 to 0.75
Outputs:
- sensitivity: float32 [8192, 64], P(('dom', 'tile'))
- residual_gram: float32 [64, 64], replicated
All inputs are finite; a program needn't handle non-finite values.
Results may differ from a plain program's by a relative error of at most 0.00105.
Values may be sent and summed in bfloat16 or wider, within the bound.
No kernel may reach another device: no remote copies, remote signals or barrier semaphores. Data moves between devices by JAX's collectives and lax.ppermute only.
A program may use at most 64 MiB of HBM per device.

v0:
```python
import jax
import jax.numpy as jnp
from jax import lax
from jax.sharding import PartitionSpec as P

FX = 8
FY = 2
ITERS = 2


PRECISE = lax.Precision.HIGHEST


def padded_2(shard, sides, width):
    for axis, dim in sides:
        devices, length = (lax.axis_size(axis), shard.shape[dim])
        up = [(i, (i + 1) % devices) for i in range(devices - 1)]
        down = [(j, i) for i, j in up]
        last = lax.slice_in_dim(shard, length - width, length, axis=dim)
        initial = lax.slice_in_dim(shard, 0, width, axis=dim)
        before = lax.ppermute(last, axis, up)
        after = lax.ppermute(initial, axis, down)
        shard = jnp.concatenate([before, shard, after], axis=dim)
    return shard


def symmetric(matrix):
    return 0.5 * (matrix + matrix.T)


def gram_matrix(left, right):
    return jnp.einsum("brc,bsc->rs", left, right, precision=PRECISE)


def mix_rows(weights, values):
    return jnp.einsum("rs,brc->bsc", weights, values, precision=PRECISE)


def solve_definite(matrix, target):
    factor = jnp.linalg.cholesky(matrix)
    lower_part = lax.linalg.triangular_solve(factor, target, left_side=True, lower=True)
    return lax.linalg.triangular_solve(
        factor, lower_part, left_side=True, lower=True, transpose_a=True
    )


def total_squares(residual):
    return symmetric(lax.psum(gram_matrix(residual, residual), ("dom", "tile")))


def apply_operator(values, matrices, capacity):
    spread = jnp.einsum("brc,bce->bre", values, matrices, precision=PRECISE)
    patch_grid = spread.reshape(FX, FY, -1)
    padded = padded_2(patch_grid.astype(jnp.bfloat16), (("dom", 0), ("tile", 1)), 1).astype(
        patch_grid.dtype
    )
    beside = padded[:-2, 1:-1] + padded[2:, 1:-1] + padded[1:-1, :-2] + padded[1:-1, 2:]
    pulled = (4.0 * patch_grid - beside).reshape(values.shape)
    return capacity[:, None, :] * values + jnp.einsum(
        "bre,bce->brc", pulled, matrices, precision=PRECISE
    )


def shards(pumping, coupling, storage, tile_order, kriging):
    blocks = storage.shape[0]
    width_block = storage.shape[1]
    test_count = pumping.shape[1] // width_block
    groups = lax.axis_size("dom")
    matrices = coupling.reshape(blocks, width_block, width_block)
    residual = pumping.reshape(blocks, test_count, width_block)
    direction = residual
    solution = jnp.zeros_like(residual)
    residual_gram = total_squares(residual)
    for iteration in range(ITERS):
        applied = apply_operator(direction, matrices, storage)
        curvature = symmetric(lax.psum(gram_matrix(direction, applied), ("dom", "tile")))
        step_size = solve_definite(curvature, residual_gram)
        solution = solution + mix_rows(step_size, direction)
        residual = residual - mix_rows(step_size, applied)
        next_gram = total_squares(residual)
        if iteration + 1 < ITERS:
            direction = residual + mix_rows(solve_definite(residual_gram, next_gram), direction)
        residual_gram = next_gram
    head_table = jnp.transpose(solution, (1, 0, 2)).reshape(test_count, -1)
    ordered = jnp.take(head_table, tile_order[0], axis=1).reshape(test_count, groups, -1)
    arrived = lax.all_to_all(ordered, "dom", split_axis=1, concat_axis=1, tiled=True).reshape(
        test_count, -1
    )
    sensitivity = lax.dot_general(
        kriging.astype(jnp.float32), arrived, (((1,), (1,)), ((), ())), precision=PRECISE
    )
    cell_total = blocks * width_block * groups * lax.axis_size("tile")
    return (sensitivity, residual_gram / cell_total)


def solution(mesh):
    in_specs = (
        P(("dom", "tile"), None),
        P(("dom", "tile"), None),
        P(("dom", "tile"), None),
        P(("dom", "tile"), None),
        P(("dom", "tile"), None),
    )
    out_specs = (P(("dom", "tile"), None), P())
    return jax.shard_map(shards, mesh=mesh, in_specs=in_specs, out_specs=out_specs, check_vma=False)
```

profile of v0, /device:TPU:1, one launch (start us, length us, event | category | flops | bytes accessed | tf_op | source)
XLA Modules:
  0.0 525.7 jit_solution(12580467156202745954)
XLA Ops:
  0.7 1.2 reshape.93
  2.9 4.9 collective-permute-start
  7.9 5.1 collective-permute-start.1
  15.3 1.3 collective-permute-start.3
  16.6 4.0 collective-permute-start.2
  21.2 1.9 collective-permute-done.3
  23.1 1.4 collective-permute-done.2
  26.0 1.0 convolution_add_fusion.1
  27.6 109.2 %all-reduce = (f32[64,64]{1,0:T(8,128)S(1)}, f32[64,64]{1,0:T(8,128)S(1)}) all-reduce(f32[64,64]{1,0:T(8,128)S(1)} %convolution_bitcast_fusion.9, f32[64,64]{1,0:T(8,128)S(1)} %convolution_bitcast_fusion.10), channel_id=1, replica_groups=mesh['dom'=128,'tile'=4] {'dom','tile'}, use_global_device_ids=true, to_apply=%region_3.0 | all-reduce | flops 8192 | bytes 65536 | tf_op jit(solution)/shard_map/psum | solution.py:48
  137.0 5.8 %cholesky.59 = f32[64,64]{1,0:T(8,128)S(1)} custom-call(f32[64,64]{1,0:T(8,128)S(1)} %fusion.24), custom_call_target="Cholesky" | custom-call | tf_op jit(solution)/shard_map/jit(cholesky)/cholesky | solution.py:40
  144.2 4.9 custom-call.13
  150.3 5.8 %cholesky.70 = f32[64,64]{1,0:T(8,128)S(1)} custom-call(f32[64,64]{1,0:T(8,128)S(1)} %fusion.19), custom_call_target="Cholesky" | custom-call | tf_op jit(solution)/shard_map/jit(cholesky)/cholesky | solution.py:40
  157.5 4.9 custom-call.15
  162.9 99.0 %psum.37 = f32[64,64]{1,0:T(8,128)S(1)} all-reduce(f32[64,64]{1,0:T(8,128)S(1)} %convolution_bitcast_fusion.7), channel_id=1, replica_groups=mesh['dom'=128,'tile'=4] {'dom','tile'}, use_global_device_ids=true, to_apply=%region_4.8 | all-reduce | flops 4096 | bytes 32768 | tf_op jit(solution)/shard_map/psum | solution.py:48
  263.8 4.2 collective-permute-start.4
  268.4 1.9 collective-permute-start.5
  270.5 3.0 collective-permute-done.5
  273.5 1.0 fusion.34
  274.6 1.3 collective-permute-start.7
  275.9 4.7 collective-permute-start.6
  281.4 1.5 collective-permute-done.6
  282.9 1.5 maximum_convert_fusion.1
  285.1 1.0 convolution_add_fusion
  286.7 101.5 %psum.38 = f32[64,64]{1,0:T(8,128)S(1)} all-reduce(f32[64,64]{1,0:T(8,128)S(1)} %convolution_bitcast_fusion.5), channel_id=1, replica_groups=mesh['dom'=128,'tile'=4] {'dom','tile'}, use_global_device_ids=true, to_apply=%region_5.9 | all-reduce | flops 4096 | bytes 32768 | tf_op jit(solution)/shard_map/psum | solution.py:76
  388.4 5.8 %cholesky.81 = f32[64,64]{1,0:T(8,128)S(1)} custom-call(f32[64,64]{1,0:T(8,128)S(1)} %fusion.13), custom_call_target="Cholesky" | custom-call | tf_op jit(solution)/shard_map/jit(cholesky)/cholesky | solution.py:40
  395.6 4.9 custom-call.17
  401.7 2.8 gather_fusion
  404.8 1.0 reshape.146
  405.8 10.6 %all-to-all-start = ((f32[128,1,512]{2,1,0:T(1,128)}), f32[128,1,512]{2,1,0:T(1,128)S(1)}, u32[]{:S(2)}, u32[]{:S(2)}) async-start(f32[128,1,512]{2,1,0:T(1,128)} %reshape.146), calls=%async_computation | async-start | bytes 524288 | tf_op jit(solution)/shard_map/all_to_all | solution.py:86
  417.6 104.6 %psum.39 = f32[64,64]{1,0:T(8,128)S(1)} all-reduce(f32[64,64]{1,0:T(8,128)S(1)} %convolution_bitcast_fusion.3), channel_id=1, replica_groups=mesh['dom'=128,'tile'=4] {'dom','tile'}, use_global_device_ids=true, to_apply=%region_6.10 | all-reduce | flops 4096 | bytes 32768 | tf_op jit(solution)/shard_map/psum | solution.py:48
  523.4 1.3 reduce.8
  524.8 0.9 convolution_bitcast_fusion.11
  (87 shorter events, 20.4 us)
Async XLA Ops:
  0.6 524.2 %copy-start = (bf16[16,1024]{1,0:T(8,128)(2,1)S(1)}, bf16[16,1024]{1,0:T(8,128)(2,1)}, u32[]{:S(2)}) copy-start(bf16[16,1024]{1,0:T(8,128)(2,1)} %param.14) | copy-start | bytes 98308
  0.6 1.2 copy-start.1
  2.9 12.0 %collective-permute-start = (bf16[1,2,4096]{2,1,0:T(2,128)(2,1)S(1)}, bf16[1,2,4096]{2,1,0:T(2,128)(2,1)S(1)}, u32[]{:S(2)}, u32[]{:S(2)}) collective-permute-start(bf16[1,2,4096]{2,1,0:T(2,128)(2,1)S(1)} %slice.69), channel_id=1, source_target_pairs={{0,4},{4,8},{8,12},{12,16},{16,20},{20,24},{24,28},{28,32},{32,36}... | collective-permute-start | bytes 49160 | tf_op jit(solution)/shard_map/ppermute | solution.py:21
  7.8 5.8 %copy-start.3 = (s32[1,1024]{1,0:T(1,128)S(1)}, s32[1,1024]{1,0:T(1,128)}, u32[]{:S(2)}) copy-start(s32[1,1024]{1,0:T(1,128)} %param.13) | copy-start | bytes 12292
  7.9 7.1 %collective-permute-start.1 = (bf16[1,2,4096]{2,1,0:T(2,128)(2,1)S(1)}, bf16[1,2,4096]{2,1,0:T(2,128)(2,1)S(1)}, u32[]{:S(2)}, u32[]{:S(2)}) collective-permute-start(bf16[1,2,4096]{2,1,0:T(2,128)(2,1)S(1)} %slice.71), channel_id=1, source_target_pairs={{4,0},{8,4},{12,8},{16,12},{20,16},{24,20},{28,24},{32,28},{36,32}... | collective-permute-start | bytes 49160 | tf_op jit(solution)/shard_map/ppermute | solution.py:22
  15.3 7.8 %collective-permute-start.3 = (bf16[10,1,4096]{2,1,0:T(2,128)(2,1)S(1)}, bf16[10,1,4096]{2,1,0:T(2,128)(2,1)S(1)}, u32[]{:S(2)}, u32[]{:S(2)}) collective-permute-start(bf16[10,1,4096]{2,1,0:T(2,128)(2,1)S(1)} %get-tuple-element.18), channel_id=1, source_target_pairs={{1,0},{2,1},{3,2},{5,4},{6,5},{7,6},{9,8},{10,9},{11,10},{13,12},{... | collective-permute-start | bytes 245768 | tf_op jit(solution)/shard_map/ppermute | solution.py:22
  16.6 7.9 %collective-permute-start.2 = (bf16[10,1,4096]{2,1,0:T(2,128)(2,1)S(1)}, bf16[10,1,4096]{2,1,0:T(2,128)(2,1)S(1)}, u32[]{:S(2)}, u32[]{:S(2)}) collective-permute-start(bf16[10,1,4096]{2,1,0:T(2,128)(2,1)S(1)} %get-tuple-element.17), channel_id=1, source_target_pairs={{0,1},{1,2},{2,3},{4,5},{5,6},{6,7},{8,9},{9,10},{10,11},{12,13},{... | collective-permute-start | bytes 245768 | tf_op jit(solution)/shard_map/ppermute | solution.py:21
  25.3 0.7 copy-start.2
  263.8 6.5 %collective-permute-start.4 = (bf16[1,2,4096]{2,1,0:T(2,128)(2,1)S(1)}, bf16[1,2,4096]{2,1,0:T(2,128)(2,1)S(1)}, u32[]{:S(2)}, u32[]{:S(2)}) collective-permute-start(bf16[1,2,4096]{2,1,0:T(2,128)(2,1)S(1)} %slice.79), channel_id=1, source_target_pairs={{0,4},{4,8},{8,12},{12,16},{16,20},{20,24},{24,28},{28,32},{32,36}... | collective-permute-start | bytes 49160 | tf_op jit(solution)/shard_map/ppermute | solution.py:21
  268.4 5.1 collective-permute-start.5
  274.6 6.8 %collective-permute-start.7 = (bf16[10,1,4096]{2,1,0:T(2,128)(2,1)}, bf16[10,1,4096]{2,1,0:T(2,128)(2,1)}, u32[]{:S(2)}, u32[]{:S(2)}) collective-permute-start(bf16[10,1,4096]{2,1,0:T(2,128)(2,1)} %get-tuple-element.16), channel_id=1, source_target_pairs={{1,0},{2,1},{3,2},{5,4},{6,5},{7,6},{9,8},{10,9},{11,10},{13,12},{... | collective-permute-start | bytes 245768 | tf_op jit(solution)/shard_map/ppermute | solution.py:22
  275.9 7.1 %collective-permute-start.6 = (bf16[10,1,4096]{2,1,0:T(2,128)(2,1)}, bf16[10,1,4096]{2,1,0:T(2,128)(2,1)}, u32[]{:S(2)}, u32[]{:S(2)}) collective-permute-start(bf16[10,1,4096]{2,1,0:T(2,128)(2,1)} %get-tuple-element.15), channel_id=1, source_target_pairs={{0,1},{1,2},{2,3},{4,5},{5,6},{6,7},{8,9},{9,10},{10,11},{12,13},{... | collective-permute-start | bytes 245768 | tf_op jit(solution)/shard_map/ppermute | solution.py:21
  405.8 117.1 %all-to-all-start = ((f32[128,1,512]{2,1,0:T(1,128)}), f32[128,1,512]{2,1,0:T(1,128)S(1)}, u32[]{:S(2)}, u32[]{:S(2)}) async-start(f32[128,1,512]{2,1,0:T(1,128)} %reshape.146), calls=%async_computation | async-start | bytes 524288 | tf_op jit(solution)/shard_map/all_to_all | solution.py:86
where the time goes:
time: 527 us; the launch traced here: 526 us
  blocking collectives  414 us (79%)
  other arithmetic  41.7 us (8%)
  starting transfers between devices  38.1 us (7%)
  local copies, waits for them, and re-layouts  11.3 us (2%)
  matrix products  11.3 us (2%)
  waiting for transfers between devices  7.81 us (1%)
    psum x3, blocking collectives, total_squares(): return symmetric(lax.psum(gram_matrix(residual, residual), ('dom', 'tile')))  313 us
    psum x1, blocking collectives, shards(): lax.psum(gram_matrix(direction, applied), ('dom', 'tile'))  102 us
    another operation x9, other arithmetic, solve_definite(): factor = jnp.linalg.cholesky(matrix)  19.6 us
    ppermute x4, starting transfers between devices, padded_2(): before = lax.ppermute(last, axis, up)  17.8 us
    another operation x6, other arithmetic, solve_definite(): lax.linalg.triangular_solve(factor, lower_part, left_side=True, lower=Tru...  16.6 us
    all_to_all x1, starting transfers between devices, shards(): lax.all_to_all(ordered, 'dom', split_axis=1, concat_axis=1, tiled=True)  10.6 us
  transfers between devices with their start and end apart: 9, of which 4 were waited for; matrix products, arithmetic and copies ran while one was open for 1% of the time, Pallas kernels for 0%

commit v1 on v0

v1 whole, which is shorter than its diff:
```python
import jax
import jax.numpy as jnp
from jax import lax
from jax.experimental import pallas as pl
from jax.experimental.pallas import tpu as pltpu
from jax.sharding import PartitionSpec as P

RHS = 64
CB = 64
FX = 8
LANE = 128
ROWS = FX * RHS
F32 = jnp.float32
BF16 = jnp.bfloat16
HIGHEST = lax.Precision.HIGHEST
PARAMS = pltpu.CompilerParams(vmem_limit_bytes=40 * 1024 * 1024)
NN = (((1,), (0,)), ((), ()))
NT = (((1,), (1,)), ((), ()))


def split(value):
    high = value.astype(BF16)
    return high, (value - high.astype(F32)).astype(BF16)


def dot(left, right, dims):
    return lax.dot_general(left, right, dims, preferred_element_type=F32)


def dot3(left, right, dims):
    (lh, ll), (rh, rl) = left, right
    return dot(lh, rh, dims) + (dot(ll, rh, dims) + dot(lh, rl, dims))


def exact(left, right, dims=NN):
    return lax.dot_general(left, right, dims, precision=HIGHEST, preferred_element_type=F32)


def low_lanes(rows):
    return lax.broadcasted_iota(jnp.int32, (rows, LANE), 1) < CB


def swap(value):
    return pltpu.roll(value, CB, 1)


def part(x):
    return pl.ds(x * RHS, RHS)


def write_edges(spread, dl, dr, tl, tr):
    low = low_lanes(RHS)
    dl[...] = spread[0].astype(BF16)
    dr[...] = spread[FX - 1].astype(BF16)
    for i in range(FX // 2):
        even, odd = spread[2 * i], spread[2 * i + 1]
        tl[part(i), :] = jnp.where(low, even, swap(odd)).astype(BF16)
        tr[part(i), :] = jnp.where(low, swap(even), odd).astype(BF16)


def first_kernel(pump, coup, p_out, sh_out, sl_out, u_out, dl, dr, tl, tr, rows_p, rows_s, mats):
    for k in range(RHS // 2):
        chunk = slice(k * LANE, (k + 1) * LANE)
        rows_p[pl.ds(k, 16, stride=32), :] = pump[:, chunk]
        rows_s[pl.ds(k, 16, stride=32), :] = coup[:, chunk]
    low = low_lanes(32)
    zero = jnp.zeros((32, LANE), F32)
    for x in range(FX):
        a0, a1 = rows_p[pl.ds(x * 64, 32), :], rows_p[pl.ds(x * 64 + 32, 32), :]
        p_out[pl.ds(x * 64, 32, stride=2), :] = jnp.where(low, a0, swap(a1))
        p_out[pl.ds(x * 64 + 1, 32, stride=2), :] = jnp.where(low, swap(a0), a1)
        s0, s1 = rows_s[pl.ds(x * 64, 32), :], rows_s[pl.ds(x * 64 + 32, 32), :]
        mats[pl.ds(x * 128, 32, stride=2), :] = jnp.where(low, s0, zero)
        mats[pl.ds(x * 128 + 1, 32, stride=2), :] = jnp.where(low, swap(s0), zero)
        mats[pl.ds(x * 128 + 64, 32, stride=2), :] = jnp.where(low, zero, swap(s1))
        mats[pl.ds(x * 128 + 65, 32, stride=2), :] = jnp.where(low, zero, s1)
    spread = []
    for x in range(FX):
        block = pl.ds(x * LANE, LANE)
        high, rest = split(mats[block, :])
        sh_out[block, :] = high
        sl_out[block, :] = rest
        u = dot3(split(p_out[part(x), :]), (high, rest), NN)
        u_out[part(x), :] = u
        spread.append(u)
    write_edges(spread, dl, dr, tl, tr)


def operator(v, u, sh, sl, stor, before, after, left, right):
    low = low_lanes(RHS)
    spread = [u[part(x), :] for x in range(FX)]
    ends = [before[...].astype(F32)] + spread + [after[...].astype(F32)]
    applied = []
    for x in range(FX):
        from_left = left[part(x // 2), :].astype(F32)
        from_right = right[part(x // 2), :].astype(F32)
        if x % 2 == 0:
            outside = jnp.where(low, from_left, swap(from_right))
        else:
            outside = jnp.where(low, swap(from_left), from_right)
        pulled = 4.0 * spread[x] - (ends[x] + ends[x + 2] + swap(spread[x]) + outside)
        block = pl.ds(x * LANE, LANE)
        capacity = jnp.concatenate([stor[2 * x : 2 * x + 1, :], stor[2 * x + 1 : 2 * x + 2, :]], axis=1)
        applied.append(
            capacity * v[part(x), :] + dot3(split(pulled), (sh[block, :], sl[block, :]), NT)
        )
    return applied


def second_kernel(v, u, sh, sl, stor, before, after, left, right, ap_out, u_out, dl, dr, tl, tr):
    applied = operator(v, u, sh, sl, stor, before, after, left, right)
    spread = []
    for x in range(FX):
        ap_out[part(x), :] = applied[x]
        block = pl.ds(x * LANE, LANE)
        s = dot3(split(applied[x]), (sh[block, :], sl[block, :]), NN)
        u_out[part(x), :] = s
        spread.append(s)
    write_edges(spread, dl, dr, tl, tr)


def order_kernel(order, v, ap, cells, grams, table):
    total = jnp.zeros((2 * RHS, 2 * RHS), F32)
    for x in range(FX):
        high, rest = split(jnp.concatenate([v[part(x), :], ap[part(x), :]], axis=0))
        table[: 2 * RHS, x * LANE : (x + 1) * LANE] = high
        table[2 * RHS :, x * LANE : (x + 1) * LANE] = rest
        total += dot3((high, rest), (high, rest), NT)
    grams[...] = total
    lane = lax.broadcasted_iota(jnp.int32, (LANE, LANE), 1)
    for g in range(FX):
        row = jnp.broadcast_to(order[:, g * LANE : (g + 1) * LANE], (LANE, LANE))
        wanted = jnp.transpose(row)
        picks = [
            jnp.where(wanted == lane + l * LANE, 1.0, 0.0).astype(BF16) for l in range(FX)
        ]
        cells[pl.ds(g * LANE, LANE), :] = dot(
            jnp.concatenate(picks, axis=1), table[...], NT
        ).astype(BF16)


def third_kernel(v, u, sh, sl, stor, before, after, left, right, grams, packed):
    applied = operator(v, u, sh, sl, stor, before, after, left, right)
    total = jnp.zeros((2 * RHS, RHS), F32)
    for x in range(FX):
        high, rest = split(jnp.concatenate([v[part(x), :], applied[x]], axis=0))
        total += dot3((high, rest), (high[RHS:], rest[RHS:]), NT)
    packed[0:128, :] = grams[...]
    packed[128:192, :] = jnp.concatenate([total[:RHS], total[RHS:]], axis=1)
    packed[192:256, :] = jnp.zeros((64, LANE), F32)


def eliminate(joined):
    order = joined.shape[0]
    row_index = lax.broadcasted_iota(jnp.int32, (order, 1), 0)
    column_index = lax.broadcasted_iota(jnp.int32, (order, order), 1)
    row_full = lax.broadcasted_iota(jnp.int32, (order, order), 0)
    for k in range(order):
        row = joined[k : k + 1, :]
        factor = joined[:, k : k + 1] / row[:, k : k + 1]
        factor = jnp.where(row_index == k, 0.0, factor)
        joined = joined - factor * row
    diagonal = jnp.sum(
        jnp.where(row_full == column_index, joined[:, :order], 0.0), axis=1, keepdims=True
    )
    return joined[:, order:] / diagonal


def symmetric(matrix):
    return 0.5 * (matrix + jnp.transpose(matrix))


def final_kernel(cell_total, packed, kriging, cells, sens, gram):
    m0 = symmetric(packed[0:64, 0:64])
    m1 = 0.5 * (packed[0:64, 64:128] + packed[64:128, 0:64])
    m2 = symmetric(packed[64:128, 64:128])
    m3 = symmetric(packed[128:192, 0:64])
    m4 = symmetric(packed[128:192, 64:128])
    weighted = dot(kriging[...], cells[...], NN)
    weighted = weighted[:, :LANE] + weighted[:, LANE:]
    first = eliminate(jnp.concatenate([m1, m0, m2], axis=1))
    alpha, shift = first[:, :RHS], first[:, RHS:]
    curved = symmetric(m3 - exact(m2, shift))
    target = m1 - exact(m2, alpha)
    gamma = eliminate(jnp.concatenate([curved, target], axis=1))
    mixed = alpha - exact(shift, gamma)
    rest = exact(m4, gamma) + exact(m3, mixed) - m2
    gram[...] = symmetric(exact(jnp.transpose(gamma), rest)) * (1.0 / cell_total)
    sens[...] = exact(weighted, jnp.concatenate([mixed, gamma], axis=0))


def call(kernel, shapes, *operands, scratch=(), flops=1000000):
    return pl.pallas_call(
        kernel,
        out_shape=[jax.ShapeDtypeStruct(shape, kind) for shape, kind in shapes],
        in_specs=[pl.BlockSpec(memory_space=pltpu.VMEM)] * len(operands),
        out_specs=[pl.BlockSpec(memory_space=pltpu.VMEM)] * len(shapes),
        scratch_shapes=list(scratch),
        compiler_params=PARAMS,
        cost_estimate=pl.CostEstimate(flops=flops, bytes_accessed=1 << 20, transcendentals=0),
    )(*operands)


EDGES = (((RHS, LANE), BF16), ((RHS, LANE), BF16), ((ROWS // 2, LANE), BF16), ((ROWS // 2, LANE), BF16))
FIELD = ((ROWS, LANE), F32)


def exchange(dl, dr, tl, tr):
    def along(axis, first, last):
        devices = lax.axis_size(axis)
        up = [(i, i + 1) for i in range(devices - 1)]
        down = [(i + 1, i) for i in range(devices - 1)]
        return lax.ppermute(last, axis, up), lax.ppermute(first, axis, down)

    return along("dom", dl, dr) + along("tile", tl, tr)


def member_groups(sizes, together):
    strides, total = [], 1
    for size in reversed(sizes):
        strides.insert(0, total)
        total *= size

    def numbers(axes):
        values = [0]
        for axis in axes:
            values = [v + i * strides[axis] for v in values for i in range(sizes[axis])]
        return values

    apart = [axis for axis in range(len(sizes)) if axis not in together]
    return [[base + v for v in numbers(together)] for base in numbers(apart)]


def reduce_all(packed):
    axes = ("dom", "tile")
    sizes = (4, 16, 2, 4)
    near = member_groups(sizes, (0, 2, 3))
    far = member_groups(sizes, (1,))

    def trade(array, groups):
        return lax.all_to_all(array, axes, 0, 0, axis_index_groups=groups, tiled=True)

    n, m = len(near[0]), len(far[0])
    mine = jnp.sum(trade(packed.reshape(n, -1, LANE), near), axis=0)
    mine = jnp.sum(trade(jnp.broadcast_to(mine[None], (m,) + mine.shape), far), axis=0)
    return trade(jnp.broadcast_to(mine[None], (n,) + mine.shape), near).reshape(packed.shape)


def shards(pumping, coupling, storage, tile_order, kriging):
    groups = lax.axis_size("dom")
    cell_total = storage.shape[0] * CB * groups * lax.axis_size("tile")
    scratch = lambda rows: pltpu.VMEM((rows, LANE), F32)
    p, sh, sl, u, *edges = call(
        first_kernel,
        (FIELD, ((FX * LANE, LANE), BF16), ((FX * LANE, LANE), BF16), FIELD) + EDGES,
        pumping,
        coupling,
        scratch=(scratch(ROWS), scratch(ROWS), scratch(FX * LANE)),
    )
    ap, u, *edges = call(
        second_kernel, (FIELD, FIELD) + EDGES, p, u, sh, sl, storage, *exchange(*edges)
    )
    halo = exchange(*edges)
    cells, grams = call(
        order_kernel,
        (((FX * LANE, 4 * RHS), BF16), ((2 * RHS, 2 * RHS), F32)),
        tile_order,
        p,
        ap,
        scratch=(pltpu.VMEM((4 * RHS, FX * LANE), BF16),),
    )
    cells = lax.all_to_all(cells.reshape(groups, -1, 4 * RHS), "dom", 0, 0, tiled=True)
    (packed,) = call(
        third_kernel, (((256, LANE), F32),), ap, u, sh, sl, storage, *halo, grams
    )
    packed = reduce_all(packed)
    sens, gram = call(
        lambda *refs: final_kernel(cell_total, *refs),
        (((kriging.shape[0], RHS), F32), ((RHS, RHS), F32)),
        packed,
        kriging,
        cells.reshape(-1, 4 * RHS),
    )
    return sens, gram


def solution(mesh):
    spec = P(("dom", "tile"), None)
    return jax.shard_map(
        shards, mesh=mesh, in_specs=(spec,) * 5, out_specs=(spec, P()), check_vma=False
    )
```

time: 527 us -> 141 us (0.27)
  blocking collectives: 414 us -> 94.8 us
  other arithmetic: 41.7 us -> 0.05 us
  Pallas kernels: 0 us -> 17.7 us
  starting transfers between devices: 38.1 us -> 22.5 us
  matrix products: 11.3 us -> 0 us
  local copies, waits for them, and re-layouts: 11.3 us -> 1.93 us
    psum x4 -> x0, blocking collectives: 414 us -> none  [the longest x3 313 us: total_squares(): return symmetric(lax.psum(gram_matrix(residual, residual), ('dom', 'tile')))]
    all_to_all x0 -> x4, blocking collectives: none -> 94.8 us  [the longest x3 56.2 us: trade(): lax.all_to_all(array, axes, 0, 0, axis_index_groups=groups, tiled=True)]
    another operation x15 -> x0, other arithmetic: 36.2 us -> none  [the longest x9 19.6 us: solve_definite(): factor = jnp.linalg.cholesky(matrix)]
    pallas_call x0 -> x5, Pallas kernels: none -> 17.7 us  [call(): pl.pallas_call(kernel, out_shape=[jax.ShapeDtypeStruct(shape, kind) for s...]
    all_to_all x1 -> x0, starting transfers between devices: 10.6 us -> none  [shards(): lax.all_to_all(ordered, 'dom', split_axis=1, concat_axis=1, tiled=True)]
    dot_general x15 -> x0, matrix products: 10 us -> none  [the longest x5 3.05 us: mix_rows(): return jnp.einsum('rs,brc->bsc', weights, values, precision=PRECISE)]
  transfers between devices with their start and end apart: 9 -> 8, of which waited for: 4 -> 2; matrix products, arithmetic and copies ran while one was open for 1% -> 0% of each run, Pallas kernels for 0% -> 1%
where the time goes in v1:
time: 141 us
  blocking collectives  94.8 us (67%)
  starting transfers between devices  22.5 us (16%)
  Pallas kernels  17.7 us (13%)
  waiting for transfers between devices  3.04 us (2%)
  local copies, waits for them, and re-layouts  1.93 us (1%)
    all_to_all x3, blocking collectives, trade(): lax.all_to_all(array, axes, 0, 0, axis_index_groups=groups, tiled=True)  56.2 us
    all_to_all x1, blocking collectives, shards(): lax.all_to_all(cells.reshape(groups, -1, 4 * RHS), 'dom', 0, 0, tiled=True)  38.6 us
    ppermute x8, starting transfers between devices, along(): return (lax.ppermute(last, axis, up), lax.ppermute(first, axis, down))  22.5 us
    pallas_call x5, Pallas kernels, call(): pl.pallas_call(kernel, out_shape=[jax.ShapeDtypeStruct(shape, kind) for s...  17.7 us
    ppermute x8, waiting for transfers between devices, along(): return (lax.ppermute(last, axis, up), lax.ppermute(first, axis, down))  3.04 us
  transfers between devices with their start and end apart: 8, of which 2 were waited for; matrix products, arithmetic and copies ran while one was open for 0% of the time, Pallas kernels for 1%

profile of v1, /device:TPU:1, one launch (start us, length us, event | category | flops | bytes accessed | tf_op | source)
XLA Modules:
  0.0 140.8 jit_solution(6415639524490124880)
XLA Ops:
  0.6 0.0 copy-start
  0.6 0.9 copy-done
  1.6 0.9 copy-done.1
  2.5 0.8 shard_map.68
  3.3 0.0 copy-start.2
  3.3 4.0 %collective-permute-start.2 = (bf16[256,128]{1,0:T(8,128)(2,1)S(1)}, bf16[256,128]{1,0:T(8,128)(2,1)S(1)}, u32[]{:S(2)}, u32[]{:S(2)}) collective-permute-start(bf16[256,128]{1,0:T(8,128)(2,1)S(1)} %get-tuple-element.24), channel_id=1, source_target_pairs={{0,1},{1,2},{2,3},{4,5},{5,6},{6,7},{8,9},{9,10},{10,11},{12,13},{... | collective-permute-start | bytes 196616 | tf_op jit(solution)/shard_map/ppermute | solution.py:213
  7.4 1.3 collective-permute-start.3
  8.7 4.4 %collective-permute-start = (bf16[64,128]{1,0:T(8,128)(2,1)S(1)}, bf16[64,128]{1,0:T(8,128)(2,1)S(1)}, u32[]{:S(2)}, u32[]{:S(2)}) collective-permute-start(bf16[64,128]{1,0:T(8,128)(2,1)S(1)} %get-tuple-element.22), channel_id=1, source_target_pairs={{0,4},{4,8},{8,12},{12,16},{16,20},{20,24},{24,28},{28,32},{32,36}... | collective-permute-start | bytes 49160 | tf_op jit(solution)/shard_map/ppermute | solution.py:213
  13.1 3.0 %collective-permute-start.1 = (bf16[64,128]{1,0:T(8,128)(2,1)S(1)}, bf16[64,128]{1,0:T(8,128)(2,1)S(1)}, u32[]{:S(2)}, u32[]{:S(2)}) collective-permute-start(bf16[64,128]{1,0:T(8,128)(2,1)S(1)} %get-tuple-element.23), channel_id=1, source_target_pairs={{4,0},{8,4},{12,8},{16,12},{20,16},{24,20},{28,24},{32,28},{36,32}... | collective-permute-start | bytes 49160 | tf_op jit(solution)/shard_map/ppermute | solution.py:213
  16.0 0.0 collective-permute-done.before
  16.0 2.1 %collective-permute-done.1.after = bf16[64,128]{1,0:T(8,128)(2,1)S(1)} collective-permute-done((bf16[64,128]{1,0:T(8,128)(2,1)S(1)}, bf16[64,128]{1,0:T(8,128)(2,1)S(1)}, u32[]{:S(2)}, u32[]{:S(2)}) %collective-permute-start.1) | collective-permute-done | bytes 16416 | tf_op jit(solution)/shard_map/ppermute | solution.py:213
  18.1 0.0 collective-permute-done.2.left
  18.1 0.0 collective-permute-done.3.right
  18.1 0.0 copy-done.2
  18.1 1.0 shard_map.69
  19.1 0.0 copy-start.4
  19.1 4.3 %collective-permute-start.6 = (bf16[256,128]{1,0:T(8,128)(2,1)S(1)}, bf16[256,128]{1,0:T(8,128)(2,1)S(1)}, u32[]{:S(2)}, u32[]{:S(2)}) collective-permute-start(bf16[256,128]{1,0:T(8,128)(2,1)S(1)} %get-tuple-element.30), channel_id=1, source_target_pairs={{0,1},{1,2},{2,3},{4,5},{5,6},{6,7},{8,9},{9,10},{10,11},{12,13},{... | collective-permute-start | bytes 196616 | tf_op jit(solution)/shard_map/ppermute | solution.py:213
  23.4 1.3 collective-permute-start.7
  24.7 2.2 %collective-permute-start.4 = (bf16[64,128]{1,0:T(8,128)(2,1)S(1)}, bf16[64,128]{1,0:T(8,128)(2,1)S(1)}, u32[]{:S(2)}, u32[]{:S(2)}) collective-permute-start(bf16[64,128]{1,0:T(8,128)(2,1)S(1)} %get-tuple-element.28), channel_id=1, source_target_pairs={{0,4},{4,8},{8,12},{12,16},{16,20},{20,24},{24,28},{28,32},{32,36}... | collective-permute-start | bytes 49160 | tf_op jit(solution)/shard_map/ppermute | solution.py:213
  26.9 2.1 %collective-permute-start.5 = (bf16[64,128]{1,0:T(8,128)(2,1)S(1)}, bf16[64,128]{1,0:T(8,128)(2,1)S(1)}, u32[]{:S(2)}, u32[]{:S(2)}) collective-permute-start(bf16[64,128]{1,0:T(8,128)(2,1)S(1)} %get-tuple-element.29), channel_id=1, source_target_pairs={{4,0},{8,4},{12,8},{16,12},{20,16},{24,20},{28,24},{32,28},{36,32}... | collective-permute-start | bytes 49160 | tf_op jit(solution)/shard_map/ppermute | solution.py:213
  29.1 0.0 copy-done.4
  29.1 2.0 %shard_map.70 = (bf16[1024,256]{1,0:T(8,128)(2,1)S(1)}, f32[128,128]{1,0:T(8,128)S(1)}) custom-call(s32[1,1024]{1,0:T(1,128)S(1)} %copy-done.4, f32[512,128]{1,0:T(8,128)S(1)} %get-tuple-element.18.v, f32[512,128]{1,0:T(8,128)S(1)} %get-tuple-element.26.ap.v), custom_call_target="tpu_custom_call" | custom-call | flops 1000000 | bytes 1048576 | tf_op jit(solution)/shard_map/pallas_call | solution.py:193
  31.1 0.0 collective-permute-done.4.before
  31.1 0.9 collective-permute-done.5.after
  32.0 0.0 collective-permute-done.6.left
  32.0 0.0 collective-permute-done.7.right
  32.0 1.1 shard_map.71
  33.1 23.4 %all_to_all.20 = f32[32,8,128]{2,1,0:T(8,128)S(1)} all-to-all(f32[32,8,128]{2,1,0:T(8,128)S(1)} %bitcast.7), channel_id=1, replica_groups={{0,1,2,3,4,5,6,7,128,129,130,131,132,133,134,135,256,257,258,259,260,26..., dimensions={0} | all-to-all | bytes 262144 | tf_op jit(solution)/shard_map/all_to_all | solution.py:241
  56.5 20.0 %all_to_all.21 = f32[16,8,128]{2,1,0:T(8,128)S(1)} all-to-all(f32[16,8,128]{2,1,0:T(8,128)S(1)} %broadcast_in_dim.4), channel_id=1, replica_groups={{0,8,16,24,32,40,48,56,64,72,80,88,96,104,112,120},{1,9,17,25,33,41,49,..., dimensions={0} | all-to-all | bytes 131072 | tf_op jit(solution)/shard_map/all_to_all | solution.py:241
  76.5 12.9 %all_to_all.22 = f32[32,8,128]{2,1,0:T(8,128)S(1)} all-to-all(f32[32,8,128]{2,1,0:T(8,128)S(1)} %broadcast_in_dim.5), channel_id=1, replica_groups={{0,1,2,3,4,5,6,7,128,129,130,131,132,133,134,135,256,257,258,259,260,26..., dimensions={0} | all-to-all | bytes 262144 | tf_op jit(solution)/shard_map/all_to_all | solution.py:241
  89.4 38.6 %all_to_all.23 = bf16[128,8,256]{2,1,0:T(8,128)(2,1)S(1)} all-to-all(bf16[128,8,256]{2,1,0:T(8,128)(2,1)S(1)} %bitcast.5), channel_id=1, replica_groups=mesh['dom'=128,'tile'=4] {'dom'}, dimensions={0} | all-to-all | bytes 1048576 | tf_op jit(solution)/shard_map/all_to_all | solution.py:272
  127.9 12.9 %shard_map.72 = (f32[16,64]{1,0:T(8,128)}, f32[64,64]{1,0:T(8,128)}) custom-call(f32[256,128]{1,0:T(8,128)S(1)} %bitcast.6, bf16[16,1024]{1,0:T(8,128)(2,1)S(1)} %copy-done.3, bf16[1024,256]{1,0:T(8,128)(2,1)S(1)} %bitcast.4), custom_call_target="tpu_custom_call" | custom-call | flops 1000000 | bytes 1048576 | tf_op jit(solution)/shard_map/pallas_call | solution.py:193
  (7 shorter events, 0.1 us)
Async XLA Ops:
  0.6 1.0 copy-start
  1.6 0.9 copy-start.1
  3.3 14.8 %copy-start.2 = (f32[16,64]{1,0:T(8,128)S(1)}, f32[16,64]{1,0:T(8,128)}, u32[]{:S(2)}) copy-start(f32[16,64]{1,0:T(8,128)} %stor.3) | copy-start | bytes 12292
  3.3 14.8 %collective-permute-start.2 = (bf16[256,128]{1,0:T(8,128)(2,1)S(1)}, bf16[256,128]{1,0:T(8,128)(2,1)S(1)}, u32[]{:S(2)}, u32[]{:S(2)}) collective-permute-start(bf16[256,128]{1,0:T(8,128)(2,1)S(1)} %get-tuple-element.24), channel_id=1, source_target_pairs={{0,1},{1,2},{2,3},{4,5},{5,6},{6,7},{8,9},{9,10},{10,11},{12,13},{... | collective-permute-start | bytes 196616 | tf_op jit(solution)/shard_map/ppermute | solution.py:213
  7.4 10.8 %collective-permute-start.3 = (bf16[256,128]{1,0:T(8,128)(2,1)S(1)}, bf16[256,128]{1,0:T(8,128)(2,1)S(1)}, u32[]{:S(2)}, u32[]{:S(2)}) collective-permute-start(bf16[256,128]{1,0:T(8,128)(2,1)S(1)} %get-tuple-element.25), channel_id=1, source_target_pairs={{1,0},{2,1},{3,2},{5,4},{6,5},{7,6},{9,8},{10,9},{11,10},{13,12},{... | collective-permute-start | bytes 196616 | tf_op jit(solution)/shard_map/ppermute | solution.py:213
  8.7 7.4 %collective-permute-start = (bf16[64,128]{1,0:T(8,128)(2,1)S(1)}, bf16[64,128]{1,0:T(8,128)(2,1)S(1)}, u32[]{:S(2)}, u32[]{:S(2)}) collective-permute-start(bf16[64,128]{1,0:T(8,128)(2,1)S(1)} %get-tuple-element.22), channel_id=1, source_target_pairs={{0,4},{4,8},{8,12},{12,16},{16,20},{20,24},{24,28},{28,32},{32,36}... | collective-permute-start | bytes 49160 | tf_op jit(solution)/shard_map/ppermute | solution.py:213
  13.1 5.1 %collective-permute-start.1 = (bf16[64,128]{1,0:T(8,128)(2,1)S(1)}, bf16[64,128]{1,0:T(8,128)(2,1)S(1)}, u32[]{:S(2)}, u32[]{:S(2)}) collective-permute-start(bf16[64,128]{1,0:T(8,128)(2,1)S(1)} %get-tuple-element.23), channel_id=1, source_target_pairs={{4,0},{8,4},{12,8},{16,12},{20,16},{24,20},{28,24},{32,28},{36,32}... | collective-permute-start | bytes 49160 | tf_op jit(solution)/shard_map/ppermute | solution.py:213
  19.1 9.9 %copy-start.4 = (s32[1,1024]{1,0:T(1,128)S(1)}, s32[1,1024]{1,0:T(1,128)}, u32[]{:S(2)}) copy-start(s32[1,1024]{1,0:T(1,128)} %order.1) | copy-start | bytes 12292
  19.1 12.9 %collective-permute-start.6 = (bf16[256,128]{1,0:T(8,128)(2,1)S(1)}, bf16[256,128]{1,0:T(8,128)(2,1)S(1)}, u32[]{:S(2)}, u32[]{:S(2)}) collective-permute-start(bf16[256,128]{1,0:T(8,128)(2,1)S(1)} %get-tuple-element.30), channel_id=1, source_target_pairs={{0,1},{1,2},{2,3},{4,5},{5,6},{6,7},{8,9},{9,10},{10,11},{12,13},{... | collective-permute-start | bytes 196616 | tf_op jit(solution)/shard_map/ppermute | solution.py:213
  23.4 8.6 %collective-permute-start.7 = (bf16[256,128]{1,0:T(8,128)(2,1)S(1)}, bf16[256,128]{1,0:T(8,128)(2,1)S(1)}, u32[]{:S(2)}, u32[]{:S(2)}) collective-permute-start(bf16[256,128]{1,0:T(8,128)(2,1)S(1)} %get-tuple-element.31), channel_id=1, source_target_pairs={{1,0},{2,1},{3,2},{5,4},{6,5},{7,6},{9,8},{10,9},{11,10},{13,12},{... | collective-permute-start | bytes 196616 | tf_op jit(solution)/shard_map/ppermute | solution.py:213
  24.7 6.3 %collective-permute-start.4 = (bf16[64,128]{1,0:T(8,128)(2,1)S(1)}, bf16[64,128]{1,0:T(8,128)(2,1)S(1)}, u32[]{:S(2)}, u32[]{:S(2)}) collective-permute-start(bf16[64,128]{1,0:T(8,128)(2,1)S(1)} %get-tuple-element.28), channel_id=1, source_target_pairs={{0,4},{4,8},{8,12},{12,16},{16,20},{20,24},{24,28},{28,32},{32,36}... | collective-permute-start | bytes 49160 | tf_op jit(solution)/shard_map/ppermute | solution.py:213
  26.9 5.1 %collective-permute-start.5 = (bf16[64,128]{1,0:T(8,128)(2,1)S(1)}, bf16[64,128]{1,0:T(8,128)(2,1)S(1)}, u32[]{:S(2)}, u32[]{:S(2)}) collective-permute-start(bf16[64,128]{1,0:T(8,128)(2,1)S(1)} %get-tuple-element.29), channel_id=1, source_target_pairs={{4,0},{8,4},{12,8},{16,12},{20,16},{24,20},{28,24},{32,28},{36,32}... | collective-permute-start | bytes 49160 | tf_op jit(solution)/shard_map/ppermute | solution.py:213
  89.4 38.6 %copy-start.3 = (bf16[16,1024]{1,0:T(8,128)(2,1)S(1)}, bf16[16,1024]{1,0:T(8,128)(2,1)}, u32[]{:S(2)}) copy-start(bf16[16,1024]{1,0:T(8,128)(2,1)} %refs_1_.1) | copy-start | bytes 98308

commit v2 on v1

--- a/solution.py
+++ b/solution.py
@@ -139,7 +139,9 @@
         ).astype(BF16)
 
 
-def third_kernel(v, u, sh, sl, stor, before, after, left, right, grams, packed):
+def third_kernel(v, u, sh, sl, stor, before, after, left, right, grams, kriging, cells, packed, weighted):
+    product = dot(kriging[...], cells[...], NN)
+    weighted[...] = product[:, :LANE] + product[:, LANE:]
     applied = operator(v, u, sh, sl, stor, before, after, left, right)
     total = jnp.zeros((2 * RHS, RHS), F32)
     for x in range(FX):
@@ -170,14 +172,12 @@
     return 0.5 * (matrix + jnp.transpose(matrix))
 
 
-def final_kernel(cell_total, packed, kriging, cells, sens, gram):
+def final_kernel(cell_total, packed, weighted, sens, gram):
     m0 = symmetric(packed[0:64, 0:64])
     m1 = 0.5 * (packed[0:64, 64:128] + packed[64:128, 0:64])
     m2 = symmetric(packed[64:128, 64:128])
     m3 = symmetric(packed[128:192, 0:64])
     m4 = symmetric(packed[128:192, 64:128])
-    weighted = dot(kriging[...], cells[...], NN)
-    weighted = weighted[:, :LANE] + weighted[:, LANE:]
     first = eliminate(jnp.concatenate([m1, m0, m2], axis=1))
     alpha, shift = first[:, :RHS], first[:, RHS:]
     curved = symmetric(m3 - exact(m2, shift))
@@ -186,7 +186,7 @@
     mixed = alpha - exact(shift, gamma)
     rest = exact(m4, gamma) + exact(m3, mixed) - m2
     gram[...] = symmetric(exact(jnp.transpose(gamma), rest)) * (1.0 / cell_total)
-    sens[...] = exact(weighted, jnp.concatenate([mixed, gamma], axis=0))
+    sens[...] = exact(weighted[...], jnp.concatenate([mixed, gamma], axis=0))
 
 
 def call(kernel, shapes, *operands, scratch=(), flops=1000000):
@@ -270,16 +270,17 @@
         scratch=(pltpu.VMEM((4 * RHS, FX * LANE), BF16),),
     )
     cells = lax.all_to_all(cells.reshape(groups, -1, 4 * RHS), "dom", 0, 0, tiled=True)
-    (packed,) = call(
-        third_kernel, (((256, LANE), F32),), ap, u, sh, sl, storage, *halo, grams
+    packed, weighted = call(
+        third_kernel,
+        (((256, LANE), F32), ((kriging.shape[0], LANE), F32)),
+        *(ap, u, sh, sl, storage, *halo, grams, kriging, cells.reshape(-1, 4 * RHS)),
     )
     packed = reduce_all(packed)
     sens, gram = call(
         lambda *refs: final_kernel(cell_total, *refs),
         (((kriging.shape[0], RHS), F32), ((RHS, RHS), F32)),
         packed,
-        kriging,
-        cells.reshape(-1, 4 * RHS),
+        weighted,
     )
     return sens, gram
 

time: 141 us -> 132 us (0.936)
  blocking collectives: 94.8 us -> 43.3 us
  waiting for transfers between devices: 3.04 us -> 24 us
  starting transfers between devices: 22.5 us -> 43 us
    all_to_all x1 -> x0, blocking collectives: 38.6 us -> none  [shards(): lax.all_to_all(cells.reshape(groups, -1, 4 * RHS), 'dom', 0, 0, tiled=True)]
    all_to_all x0 -> x1, starting transfers between devices: none -> 19 us  [shards(): lax.all_to_all(cells.reshape(groups, -1, 4 * RHS), 'dom', 0, 0, tiled=True)]
    all_to_all x3, blocking collectives: 56.2 us -> 43.3 us  [trade(): lax.all_to_all(array, axes, 0, 0, axis_index_groups=groups, tiled=True)]
    ppermute x8, waiting for transfers between devices: 3.04 us -> 14.1 us  [along(): return (lax.ppermute(last, axis, up), lax.ppermute(first, axis, down))]
    all_to_all x0 -> x1, waiting for transfers between devices: none -> 9.91 us  [shards(): lax.all_to_all(cells.reshape(groups, -1, 4 * RHS), 'dom', 0, 0, tiled=True)]
    ppermute x8, starting transfers between devices: 22.5 us -> 24 us  [along(): return (lax.ppermute(last, axis, up), lax.ppermute(first, axis, down))]
  transfers between devices with their start and end apart: 8 -> 9, of which waited for: 2 -> 4; matrix products, arithmetic and copies ran while one was open for 0% -> 0% of each run, Pallas kernels for 1% -> 0%
where the time goes in v2:
time: 132 us
  blocking collectives  43.3 us (33%)
  starting transfers between devices  43 us (33%)
  waiting for transfers between devices  24 us (18%)
  Pallas kernels  18.6 us (14%)
  local copies, waits for them, and re-layouts  1.93 us (1%)
    all_to_all x3, blocking collectives, trade(): lax.all_to_all(array, axes, 0, 0, axis_index_groups=groups, tiled=True)  43.3 us
    ppermute x8, starting transfers between devices, along(): return (lax.ppermute(last, axis, up), lax.ppermute(first, axis, down))  24 us
    all_to_all x1, starting transfers between devices, shards(): lax.all_to_all(cells.reshape(groups, -1, 4 * RHS), 'dom', 0, 0, tiled=True)  19 us
    pallas_call x5, Pallas kernels, call(): pl.pallas_call(kernel, out_shape=[jax.ShapeDtypeStruct(shape, kind) for s...  18.6 us
    ppermute x8, waiting for transfers between devices, along(): return (lax.ppermute(last, axis, up), lax.ppermute(first, axis, down))  14.1 us
    all_to_all x1, waiting for transfers between devices, shards(): lax.all_to_all(cells.reshape(groups, -1, 4 * RHS), 'dom', 0, 0, tiled=True)  9.91 us
  transfers between devices with their start and end apart: 9, of which 4 were waited for; matrix products, arithmetic and copies ran while one was open for 0% of the time, Pallas kernels for 0%

profile of v2, /device:TPU:1, one launch (start us, length us, event | category | flops | bytes accessed | tf_op | source)
XLA Modules:
  0.0 131.6 jit_solution(6292047677160836508)
XLA Ops:
  0.6 0.9 copy-done
  1.6 0.9 copy-done.1
  2.5 0.8 shard_map.68
  3.3 0.0 copy-start.3
  3.3 4.0 %collective-permute-start.2 = (bf16[256,128]{1,0:T(8,128)(2,1)S(1)}, bf16[256,128]{1,0:T(8,128)(2,1)S(1)}, u32[]{:S(2)}, u32[]{:S(2)}) collective-permute-start(bf16[256,128]{1,0:T(8,128)(2,1)S(1)} %get-tuple-element.26), channel_id=1, source_target_pairs={{0,1},{1,2},{2,3},{4,5},{5,6},{6,7},{8,9},{9,10},{10,11},{12,13},{... | collective-permute-start | bytes 196616 | tf_op jit(solution)/shard_map/ppermute | solution.py:213
  7.4 1.3 collective-permute-start.3
  8.7 4.4 %collective-permute-start = (bf16[64,128]{1,0:T(8,128)(2,1)S(1)}, bf16[64,128]{1,0:T(8,128)(2,1)S(1)}, u32[]{:S(2)}, u32[]{:S(2)}) collective-permute-start(bf16[64,128]{1,0:T(8,128)(2,1)S(1)} %get-tuple-element.24), channel_id=1, source_target_pairs={{0,4},{4,8},{8,12},{12,16},{16,20},{20,24},{24,28},{28,32},{32,36}... | collective-permute-start | bytes 49160 | tf_op jit(solution)/shard_map/ppermute | solution.py:213
  13.1 3.0 %collective-permute-start.1 = (bf16[64,128]{1,0:T(8,128)(2,1)S(1)}, bf16[64,128]{1,0:T(8,128)(2,1)S(1)}, u32[]{:S(2)}, u32[]{:S(2)}) collective-permute-start(bf16[64,128]{1,0:T(8,128)(2,1)S(1)} %get-tuple-element.25), channel_id=1, source_target_pairs={{4,0},{8,4},{12,8},{16,12},{20,16},{24,20},{28,24},{32,28},{36,32}... | collective-permute-start | bytes 49160 | tf_op jit(solution)/shard_map/ppermute | solution.py:213
  16.0 0.0 collective-permute-done.before
  16.0 2.1 %collective-permute-done.1.after = bf16[64,128]{1,0:T(8,128)(2,1)S(1)} collective-permute-done((bf16[64,128]{1,0:T(8,128)(2,1)S(1)}, bf16[64,128]{1,0:T(8,128)(2,1)S(1)}, u32[]{:S(2)}, u32[]{:S(2)}) %collective-permute-start.1) | collective-permute-done | bytes 16416 | tf_op jit(solution)/shard_map/ppermute | solution.py:213
  18.1 0.0 collective-permute-done.2.left
  18.1 0.0 collective-permute-done.3.right
  18.1 0.0 copy-done.3
  18.1 0.0 copy-start.4
  18.1 1.0 shard_map.69
  19.1 0.0 copy-done.4
  19.1 2.8 %shard_map.70 = (bf16[1024,256]{1,0:T(8,128)(2,1)}, f32[128,128]{1,0:T(8,128)S(1)}) custom-call(s32[1,1024]{1,0:T(1,128)S(1)} %copy-done.4, f32[512,128]{1,0:T(8,128)S(1)} %get-tuple-element.20.v, f32[512,128]{1,0:T(8,128)S(1)} %get-tuple-element.28.ap.v), custom_call_target="tpu_custom_call" | custom-call | flops 1000000 | bytes 1048576 | tf_op jit(solution)/shard_map/pallas_call | solution.py:193
  21.9 19.0 %all-to-all-start = ((bf16[128,8,256]{2,1,0:T(8,128)(2,1)}), bf16[128,8,256]{2,1,0:T(8,128)(2,1)S(1)}, u32[]{:S(2)}, u32[]{:S(2)}) async-start(bf16[128,8,256]{2,1,0:T(8,128)(2,1)} %bitcast), calls=%async_computation | async-start | bytes 1048576 | tf_op jit(solution)/shard_map/all_to_all | solution.py:272
  40.9 4.3 %collective-permute-start.6 = (bf16[256,128]{1,0:T(8,128)(2,1)S(1)}, bf16[256,128]{1,0:T(8,128)(2,1)S(1)}, u32[]{:S(2)}, u32[]{:S(2)}) collective-permute-start(bf16[256,128]{1,0:T(8,128)(2,1)S(1)} %get-tuple-element.32), channel_id=1, source_target_pairs={{0,1},{1,2},{2,3},{4,5},{5,6},{6,7},{8,9},{9,10},{10,11},{12,13},{... | collective-permute-start | bytes 196616 | tf_op jit(solution)/shard_map/ppermute | solution.py:213
  45.2 1.3 collective-permute-start.7
  46.5 3.8 %collective-permute-start.4 = (bf16[64,128]{1,0:T(8,128)(2,1)S(1)}, bf16[64,128]{1,0:T(8,128)(2,1)S(1)}, u32[]{:S(2)}, u32[]{:S(2)}) collective-permute-start(bf16[64,128]{1,0:T(8,128)(2,1)S(1)} %get-tuple-element.30), channel_id=1, source_target_pairs={{0,4},{4,8},{8,12},{12,16},{16,20},{20,24},{24,28},{28,32},{32,36}... | collective-permute-start | bytes 49160 | tf_op jit(solution)/shard_map/ppermute | solution.py:213
  50.3 1.9 %collective-permute-start.5 = (bf16[64,128]{1,0:T(8,128)(2,1)S(1)}, bf16[64,128]{1,0:T(8,128)(2,1)S(1)}, u32[]{:S(2)}, u32[]{:S(2)}) collective-permute-start(bf16[64,128]{1,0:T(8,128)(2,1)S(1)} %get-tuple-element.31), channel_id=1, source_target_pairs={{4,0},{8,4},{12,8},{16,12},{20,16},{24,20},{28,24},{32,28},{36,32}... | collective-permute-start | bytes 49160 | tf_op jit(solution)/shard_map/ppermute | solution.py:213
  52.3 3.2 %collective-permute-done.4.before = bf16[64,128]{1,0:T(8,128)(2,1)S(1)} collective-permute-done((bf16[64,128]{1,0:T(8,128)(2,1)S(1)}, bf16[64,128]{1,0:T(8,128)(2,1)S(1)}, u32[]{:S(2)}, u32[]{:S(2)}) %collective-permute-start.4) | collective-permute-done | bytes 16416 | tf_op jit(solution)/shard_map/ppermute | solution.py:213
  55.5 8.7 %collective-permute-done.5.after = bf16[64,128]{1,0:T(8,128)(2,1)S(1)} collective-permute-done((bf16[64,128]{1,0:T(8,128)(2,1)S(1)}, bf16[64,128]{1,0:T(8,128)(2,1)S(1)}, u32[]{:S(2)}, u32[]{:S(2)}) %collective-permute-start.5) | collective-permute-done | bytes 16416 | tf_op jit(solution)/shard_map/ppermute | solution.py:213
  64.2 0.0 collective-permute-done.6.left
  64.2 0.0 collective-permute-done.7.right
  64.2 9.9 %all-to-all-done = bf16[128,8,256]{2,1,0:T(8,128)(2,1)S(1)} async-done(((bf16[128,8,256]{2,1,0:T(8,128)(2,1)}), bf16[128,8,256]{2,1,0:T(8,128)(2,1)S(1)}, u32[]{:S(2)}, u32[]{:S(2)}) %all-to-all-start) | async-done | bytes 524320 | tf_op jit(solution)/shard_map/all_to_all | solution.py:272
  74.1 1.1 shard_map.71
  75.3 16.6 %all_to_all.20 = f32[32,8,128]{2,1,0:T(8,128)S(1)} all-to-all(f32[32,8,128]{2,1,0:T(8,128)S(1)} %bitcast.6), channel_id=1, replica_groups={{0,1,2,3,4,5,6,7,128,129,130,131,132,133,134,135,256,257,258,259,260,26..., dimensions={0} | all-to-all | bytes 262144 | tf_op jit(solution)/shard_map/all_to_all | solution.py:241
  91.9 14.2 %all_to_all.21 = f32[16,8,128]{2,1,0:T(8,128)S(1)} all-to-all(f32[16,8,128]{2,1,0:T(8,128)S(1)} %broadcast_in_dim.4), channel_id=1, replica_groups={{0,8,16,24,32,40,48,56,64,72,80,88,96,104,112,120},{1,9,17,25,33,41,49,..., dimensions={0} | all-to-all | bytes 131072 | tf_op jit(solution)/shard_map/all_to_all | solution.py:241
  106.2 12.5 %all_to_all.22 = f32[32,8,128]{2,1,0:T(8,128)S(1)} all-to-all(f32[32,8,128]{2,1,0:T(8,128)S(1)} %broadcast_in_dim.5), channel_id=1, replica_groups={{0,1,2,3,4,5,6,7,128,129,130,131,132,133,134,135,256,257,258,259,260,26..., dimensions={0} | all-to-all | bytes 262144 | tf_op jit(solution)/shard_map/all_to_all | solution.py:241
  118.7 12.9 %shard_map.72 = (f32[16,64]{1,0:T(8,128)}, f32[64,64]{1,0:T(8,128)}) custom-call(f32[256,128]{1,0:T(8,128)S(1)} %bitcast.5, f32[16,128]{1,0:T(8,128)S(1)} %get-tuple-element.37.refs_1_), custom_call_target="tpu_custom_call" | custom-call | flops 1000000 | bytes 1048576 | tf_op jit(solution)/shard_map/pallas_call | solution.py:193
  (8 shorter events, 0.1 us)
Async XLA Ops:
  0.6 1.0 copy-start
  1.6 0.9 copy-start.1
  3.3 14.8 %copy-start.3 = (f32[16,64]{1,0:T(8,128)S(1)}, f32[16,64]{1,0:T(8,128)}, u32[]{:S(2)}) copy-start(f32[16,64]{1,0:T(8,128)} %stor.3) | copy-start | bytes 12292
  3.3 14.8 %collective-permute-start.2 = (bf16[256,128]{1,0:T(8,128)(2,1)S(1)}, bf16[256,128]{1,0:T(8,128)(2,1)S(1)}, u32[]{:S(2)}, u32[]{:S(2)}) collective-permute-start(bf16[256,128]{1,0:T(8,128)(2,1)S(1)} %get-tuple-element.26), channel_id=1, source_target_pairs={{0,1},{1,2},{2,3},{4,5},{5,6},{6,7},{8,9},{9,10},{10,11},{12,13},{... | collective-permute-start | bytes 196616 | tf_op jit(solution)/shard_map/ppermute | solution.py:213
  7.4 10.8 %collective-permute-start.3 = (bf16[256,128]{1,0:T(8,128)(2,1)S(1)}, bf16[256,128]{1,0:T(8,128)(2,1)S(1)}, u32[]{:S(2)}, u32[]{:S(2)}) collective-permute-start(bf16[256,128]{1,0:T(8,128)(2,1)S(1)} %get-tuple-element.27), channel_id=1, source_target_pairs={{1,0},{2,1},{3,2},{5,4},{6,5},{7,6},{9,8},{10,9},{11,10},{13,12},{... | collective-permute-start | bytes 196616 | tf_op jit(solution)/shard_map/ppermute | solution.py:213
  8.7 7.4 %collective-permute-start = (bf16[64,128]{1,0:T(8,128)(2,1)S(1)}, bf16[64,128]{1,0:T(8,128)(2,1)S(1)}, u32[]{:S(2)}, u32[]{:S(2)}) collective-permute-start(bf16[64,128]{1,0:T(8,128)(2,1)S(1)} %get-tuple-element.24), channel_id=1, source_target_pairs={{0,4},{4,8},{8,12},{12,16},{16,20},{20,24},{24,28},{28,32},{32,36}... | collective-permute-start | bytes 49160 | tf_op jit(solution)/shard_map/ppermute | solution.py:213
  13.1 5.1 %collective-permute-start.1 = (bf16[64,128]{1,0:T(8,128)(2,1)S(1)}, bf16[64,128]{1,0:T(8,128)(2,1)S(1)}, u32[]{:S(2)}, u32[]{:S(2)}) collective-permute-start(bf16[64,128]{1,0:T(8,128)(2,1)S(1)} %get-tuple-element.25), channel_id=1, source_target_pairs={{4,0},{8,4},{12,8},{16,12},{20,16},{24,20},{28,24},{32,28},{36,32}... | collective-permute-start | bytes 49160 | tf_op jit(solution)/shard_map/ppermute | solution.py:213
  18.1 1.0 copy-start.4
  21.9 52.2 %copy-start.2 = (bf16[16,1024]{1,0:T(8,128)(2,1)S(1)}, bf16[16,1024]{1,0:T(8,128)(2,1)}, u32[]{:S(2)}) copy-start(bf16[16,1024]{1,0:T(8,128)(2,1)} %kriging.1) | copy-start | bytes 98308
  21.9 52.2 %all-to-all-start = ((bf16[128,8,256]{2,1,0:T(8,128)(2,1)}), bf16[128,8,256]{2,1,0:T(8,128)(2,1)S(1)}, u32[]{:S(2)}, u32[]{:S(2)}) async-start(bf16[128,8,256]{2,1,0:T(8,128)(2,1)} %bitcast), calls=%async_computation | async-start | bytes 1048576 | tf_op jit(solution)/shard_map/all_to_all | solution.py:272
  40.9 23.3 %collective-permute-start.6 = (bf16[256,128]{1,0:T(8,128)(2,1)S(1)}, bf16[256,128]{1,0:T(8,128)(2,1)S(1)}, u32[]{:S(2)}, u32[]{:S(2)}) collective-permute-start(bf16[256,128]{1,0:T(8,128)(2,1)S(1)} %get-tuple-element.32), channel_id=1, source_target_pairs={{0,1},{1,2},{2,3},{4,5},{5,6},{6,7},{8,9},{9,10},{10,11},{12,13},{... | collective-permute-start | bytes 196616 | tf_op jit(solution)/shard_map/ppermute | solution.py:213
  45.2 19.0 %collective-permute-start.7 = (bf16[256,128]{1,0:T(8,128)(2,1)S(1)}, bf16[256,128]{1,0:T(8,128)(2,1)S(1)}, u32[]{:S(2)}, u32[]{:S(2)}) collective-permute-start(bf16[256,128]{1,0:T(8,128)(2,1)S(1)} %get-tuple-element.33), channel_id=1, source_target_pairs={{1,0},{2,1},{3,2},{5,4},{6,5},{7,6},{9,8},{10,9},{11,10},{13,12},{... | collective-permute-start | bytes 196616 | tf_op jit(solution)/shard_map/ppermute | solution.py:213
  46.5 9.0 %collective-permute-start.4 = (bf16[64,128]{1,0:T(8,128)(2,1)S(1)}, bf16[64,128]{1,0:T(8,128)(2,1)S(1)}, u32[]{:S(2)}, u32[]{:S(2)}) collective-permute-start(bf16[64,128]{1,0:T(8,128)(2,1)S(1)} %get-tuple-element.30), channel_id=1, source_target_pairs={{0,4},{4,8},{8,12},{12,16},{16,20},{20,24},{24,28},{28,32},{32,36}... | collective-permute-start | bytes 49160 | tf_op jit(solution)/shard_map/ppermute | solution.py:213
  50.3 13.9 %collective-permute-start.5 = (bf16[64,128]{1,0:T(8,128)(2,1)S(1)}, bf16[64,128]{1,0:T(8,128)(2,1)S(1)}, u32[]{:S(2)}, u32[]{:S(2)}) collective-permute-start(bf16[64,128]{1,0:T(8,128)(2,1)S(1)} %get-tuple-element.31), channel_id=1, source_target_pairs={{4,0},{8,4},{12,8},{16,12},{20,16},{24,20},{28,24},{32,28},{36,32}... | collective-permute-start | bytes 49160 | tf_op jit(solution)/shard_map/ppermute | solution.py:213

commit v3 on v1

--- a/solution.py
+++ b/solution.py
@@ -14,6 +14,7 @@
 BF16 = jnp.bfloat16
 HIGHEST = lax.Precision.HIGHEST
 PARAMS = pltpu.CompilerParams(vmem_limit_bytes=40 * 1024 * 1024)
+LONG = 10**11
 NN = (((1,), (0,)), ((), ()))
 NT = (((1,), (1,)), ((), ()))
 
@@ -119,14 +120,11 @@
     write_edges(spread, dl, dr, tl, tr)
 
 
-def order_kernel(order, v, ap, cells, grams, table):
-    total = jnp.zeros((2 * RHS, 2 * RHS), F32)
-    for x in range(FX):
-        high, rest = split(jnp.concatenate([v[part(x), :], ap[part(x), :]], axis=0))
-        table[: 2 * RHS, x * LANE : (x + 1) * LANE] = high
-        table[2 * RHS :, x * LANE : (x + 1) * LANE] = rest
-        total += dot3((high, rest), (high, rest), NT)
-    grams[...] = total
+def deal(order, v, cells, table):
+    for x in range(FX):
+        high, rest = split(v[part(x), :])
+        table[:RHS, x * LANE : (x + 1) * LANE] = high
+        table[RHS:, x * LANE : (x + 1) * LANE] = rest
     lane = lax.broadcasted_iota(jnp.int32, (LANE, LANE), 1)
     for g in range(FX):
         row = jnp.broadcast_to(order[:, g * LANE : (g + 1) * LANE], (LANE, LANE))
@@ -139,45 +137,114 @@
         ).astype(BF16)
 
 
+def weigh(kriging, cells):
+    product = dot(kriging[...], cells[...], NN)
+    return product[:, :RHS] + product[:, RHS:]
+
+
+def deal_images(order, v, ap, kriging, arrived, cells, grams, weighted, table):
+    deal(order, ap, cells, table)
+    total = jnp.zeros((2 * RHS, 2 * RHS), F32)
+    for x in range(FX):
+        both = split(jnp.concatenate([v[part(x), :], ap[part(x), :]], axis=0))
+        total += dot3(both, both, NT)
+    grams[...] = total
+    weighted[...] = weigh(kriging, arrived)
+
+
 def third_kernel(v, u, sh, sl, stor, before, after, left, right, grams, packed):
     applied = operator(v, u, sh, sl, stor, before, after, left, right)
     total = jnp.zeros((2 * RHS, RHS), F32)
     for x in range(FX):
         high, rest = split(jnp.concatenate([v[part(x), :], applied[x]], axis=0))
         total += dot3((high, rest), (high[RHS:], rest[RHS:]), NT)
-    packed[0:128, :] = grams[...]
-    packed[128:192, :] = jnp.concatenate([total[:RHS], total[RHS:]], axis=1)
-    packed[192:256, :] = jnp.zeros((64, LANE), F32)
-
-
-def eliminate(joined):
-    order = joined.shape[0]
-    row_index = lax.broadcasted_iota(jnp.int32, (order, 1), 0)
-    column_index = lax.broadcasted_iota(jnp.int32, (order, order), 1)
-    row_full = lax.broadcasted_iota(jnp.int32, (order, order), 0)
-    for k in range(order):
-        row = joined[k : k + 1, :]
-        factor = joined[:, k : k + 1] / row[:, k : k + 1]
-        factor = jnp.where(row_index == k, 0.0, factor)
-        joined = joined - factor * row
-    diagonal = jnp.sum(
-        jnp.where(row_full == column_index, joined[:, :order], 0.0), axis=1, keepdims=True
-    )
-    return joined[:, order:] / diagonal
+    m0 = symmetric(grams[:RHS, :RHS])
+    m1 = 0.5 * (grams[:RHS, RHS:] + grams[RHS:, :RHS])
+    m2 = symmetric(grams[RHS:, RHS:])
+    m3 = symmetric(total[:RHS])
+    m4 = symmetric(total[RHS:])
+    row, column = square_index()
+    upper = row <= column
+    packed[:RHS, :] = jnp.concatenate([jnp.where(upper, m0, m2), jnp.where(upper, m1, m3)], axis=1)
+    ends = jnp.where(row == 0, diagonal(m2), jnp.where(row == 1, diagonal(m3), 0.0))
+    packed[RHS:, :] = jnp.concatenate([m4, ends], axis=1)
+
+
+def weigh_images(kriging, arrived, packed, weighted, packed_out):
+    weighted[...] = weigh(kriging, arrived)
+    packed_out[...] = packed[...]
+
+
+def square_index():
+    return [lax.broadcasted_iota(jnp.int32, (RHS, RHS), d) for d in (0, 1)]
+
+
+def diagonal(matrix):
+    row, column = square_index()
+    return jnp.sum(jnp.where(row == column, matrix, 0.0), axis=0, keepdims=True)
+
+
+def unpack_pair(matrix, ends):
+    row, column = square_index()
+    turned = jnp.transpose(matrix)
+    first = jnp.where(row <= column, matrix, turned)
+    second = jnp.where(row > column, matrix, jnp.where(row < column, turned, ends))
+    return first, second
+
+
+def eliminate(joined, panel=8):
+    order, width = joined.shape
+    parts = [joined[g : g + panel, :] for g in range(0, order, panel)]
+    index = lax.broadcasted_iota(jnp.int32, (panel, width), 0)
+
+    def wide(value):
+        pieces = [value] * (width // LANE)
+        if width % LANE:
+            pieces.append(value[:, : width % LANE])
+        return jnp.concatenate(pieces, axis=1) if len(pieces) > 1 else value
+
+    def apply(rows, at, c0, c1, inverse, where):
+        r0, r1 = rows[at : at + 1, :], rows[at + 1 : at + 2, :]
+        s0 = inverse[0] * r0 + inverse[1] * r1
+        s1 = inverse[2] * r0 + inverse[3] * r1
+        rest = rows - (c0 * s0 + c1 * s1)
+        return jnp.where(where == at, s0, jnp.where(where == at + 1, s1, rest))
+
+    for g in range(len(parts)):
+        rows = parts[g]
+        first = g * panel
+        columns = [
+            jnp.broadcast_to(rows[:, first + q : first + q + 1], (panel, LANE)) for q in range(panel)
+        ]
+        for at in range(0, panel, 2):
+            c0, c1 = columns[at], columns[at + 1]
+            a, c = c0[at : at + 1, :], c0[at + 1 : at + 2, :]
+            b, d = c1[at : at + 1, :], c1[at + 1 : at + 2, :]
+            scale = 1.0 / (a * d - b * c)
+            inverse = (d * scale, -b * scale, -c * scale, a * scale)
+            for q in range(at + 2, panel):
+                columns[q] = apply(columns[q], at, c0, c1, inverse, index[:, :LANE])
+            rows = apply(rows, at, wide(c0), wide(c1), [wide(v) for v in inverse], index)
+        parts[g] = rows
+        for h in range(len(parts)):
+            if h != g:
+                taken = None
+                for q in range(panel):
+                    column = jnp.broadcast_to(parts[h][:, first + q : first + q + 1], (panel, width))
+                    term = column * rows[q : q + 1, :]
+                    taken = term if taken is None else taken + term
+                parts[h] = parts[h] - taken
+    return jnp.concatenate(parts, axis=0)[:, order:]
 
 
 def symmetric(matrix):
     return 0.5 * (matrix + jnp.transpose(matrix))
 
 
-def final_kernel(cell_total, packed, kriging, cells, sens, gram):
-    m0 = symmetric(packed[0:64, 0:64])
-    m1 = 0.5 * (packed[0:64, 64:128] + packed[64:128, 0:64])
-    m2 = symmetric(packed[64:128, 64:128])
-    m3 = symmetric(packed[128:192, 0:64])
-    m4 = symmetric(packed[128:192, 64:128])
-    weighted = dot(kriging[...], cells[...], NN)
-    weighted = weighted[:, :LANE] + weighted[:, LANE:]
+def final_kernel(cell_total, packed, weighted_p, weighted_ap, sens, gram):
+    m0, m2 = unpack_pair(packed[:RHS, :RHS], packed[RHS : RHS + 1, RHS:])
+    m1, m3 = unpack_pair(packed[:RHS, RHS:], packed[RHS + 1 : RHS + 2, RHS:])
+    m4 = packed[RHS:, :RHS]
     first = eliminate(jnp.concatenate([m1, m0, m2], axis=1))
     alpha, shift = first[:, :RHS], first[:, RHS:]
     curved = symmetric(m3 - exact(m2, shift))
@@ -186,7 +253,7 @@
     mixed = alpha - exact(shift, gamma)
     rest = exact(m4, gamma) + exact(m3, mixed) - m2
     gram[...] = symmetric(exact(jnp.transpose(gamma), rest)) * (1.0 / cell_total)
-    sens[...] = exact(weighted, jnp.concatenate([mixed, gamma], axis=0))
+    sens[...] = exact(weighted_p[...], mixed) + exact(weighted_ap[...], gamma)
 
 
 def call(kernel, shapes, *operands, scratch=(), flops=1000000):
@@ -257,29 +324,40 @@
         coupling,
         scratch=(scratch(ROWS), scratch(ROWS), scratch(FX * LANE)),
     )
+    halo = exchange(*edges)
+    table = pltpu.VMEM((2 * RHS, FX * LANE), BF16)
+    cells = ((FX * LANE, 2 * RHS), BF16)
+    product = ((kriging.shape[0], RHS), F32)
+
+    def deliver(rows):
+        rows = rows.reshape(groups, -1, 2 * RHS)
+        return lax.all_to_all(rows, "dom", 0, 0, tiled=True).reshape(-1, 2 * RHS)
+
+    (dealt,) = call(deal, (cells,), tile_order, p, scratch=(table,))
+    arrived = deliver(dealt)
     ap, u, *edges = call(
-        second_kernel, (FIELD, FIELD) + EDGES, p, u, sh, sl, storage, *exchange(*edges)
+        second_kernel, (FIELD, FIELD) + EDGES, p, u, sh, sl, storage, *halo, flops=LONG
     )
     halo = exchange(*edges)
-    cells, grams = call(
-        order_kernel,
-        (((FX * LANE, 4 * RHS), BF16), ((2 * RHS, 2 * RHS), F32)),
-        tile_order,
-        p,
-        ap,
-        scratch=(pltpu.VMEM((4 * RHS, FX * LANE), BF16),),
-    )
-    cells = lax.all_to_all(cells.reshape(groups, -1, 4 * RHS), "dom", 0, 0, tiled=True)
+    dealt, grams, weighted_p = call(
+        deal_images,
+        (cells, ((2 * RHS, 2 * RHS), F32), product),
+        *(tile_order, p, ap, kriging, arrived),
+        scratch=(table,),
+    )
+    arrived = deliver(dealt)
+    moments = ((2 * RHS, LANE), F32)
     (packed,) = call(
-        third_kernel, (((256, LANE), F32),), ap, u, sh, sl, storage, *halo, grams
-    )
+        third_kernel, (moments,), *(ap, u, sh, sl, storage, *halo, grams), flops=LONG
+    )
+    weighted_ap, packed = call(weigh_images, (product, moments), kriging, arrived, packed)
     packed = reduce_all(packed)
     sens, gram = call(
         lambda *refs: final_kernel(cell_total, *refs),
         (((kriging.shape[0], RHS), F32), ((RHS, RHS), F32)),
         packed,
-        kriging,
-        cells.reshape(-1, 4 * RHS),
+        weighted_p,
+        weighted_ap,
     )
     return sens, gram
 

time: 141 us -> 140 us (level)
  blocking collectives: 94.8 us -> 42 us
  waiting for transfers between devices: 3.04 us -> 31.4 us
  starting transfers between devices: 22.5 us -> 50.8 us
  Pallas kernels: 17.7 us -> 12.5 us
    all_to_all x1 -> x0, blocking collectives: 38.6 us -> none  [shards(): lax.all_to_all(cells.reshape(groups, -1, 4 * RHS), 'dom', 0, 0, tiled=True)]
    all_to_all x0 -> x2, waiting for transfers between devices: none -> 31.4 us  [deliver(): return lax.all_to_all(rows, 'dom', 0, 0, tiled=True).reshape(-1, 2 * RHS)]
    all_to_all x0 -> x2, starting transfers between devices: none -> 26.8 us  [deliver(): return lax.all_to_all(rows, 'dom', 0, 0, tiled=True).reshape(-1, 2 * RHS)]
    all_to_all x3, blocking collectives: 56.2 us -> 42 us  [trade(): lax.all_to_all(array, axes, 0, 0, axis_index_groups=groups, tiled=True)]
    pallas_call x5 -> x7, Pallas kernels: 17.7 us -> 12.5 us  [call(): pl.pallas_call(kernel, out_shape=[jax.ShapeDtypeStruct(shape, kind) for s...]
    ppermute x8, waiting for transfers between devices: 3.04 us -> 0.02 us  [along(): return (lax.ppermute(last, axis, up), lax.ppermute(first, axis, down))]
    ppermute x8, starting transfers between devices: 22.5 us -> 24 us  [along(): return (lax.ppermute(last, axis, up), lax.ppermute(first, axis, down))]
  transfers between devices with their start and end apart: 8 -> 10, of which waited for: 2 -> 2; matrix products, arithmetic and copies ran while one was open for 0% -> 0% of each run, Pallas kernels for 1% -> 4%
where the time goes in v3:
time: 140 us; the launch traced here: 139 us
  starting transfers between devices  50.8 us (36%)
  blocking collectives  42 us (30%)
  waiting for transfers between devices  31.4 us (22%)
  Pallas kernels  12.5 us (9%)
  local copies, waits for them, and re-layouts  1.93 us (1%)
    all_to_all x3, blocking collectives, trade(): lax.all_to_all(array, axes, 0, 0, axis_index_groups=groups, tiled=True)  42 us
    all_to_all x2, waiting for transfers between devices, deliver(): return lax.all_to_all(rows, 'dom', 0, 0, tiled=True).reshape(-1, 2 * RHS)  31.4 us
    all_to_all x2, starting transfers between devices, deliver(): return lax.all_to_all(rows, 'dom', 0, 0, tiled=True).reshape(-1, 2 * RHS)  26.8 us
    ppermute x8, starting transfers between devices, along(): return (lax.ppermute(last, axis, up), lax.ppermute(first, axis, down))  24 us
    pallas_call x7, Pallas kernels, call(): pl.pallas_call(kernel, out_shape=[jax.ShapeDtypeStruct(shape, kind) for s...  12.5 us
  transfers between devices with their start and end apart: 10, of which 2 were waited for; matrix products, arithmetic and copies ran while one was open for 0% of the time, Pallas kernels for 4%

profile of v3, /device:TPU:1, one launch (start us, length us, event | category | flops | bytes accessed | tf_op | source)
XLA Modules:
  0.0 139.5 jit_solution(14753059111465027164)
XLA Ops:
  0.6 0.9 copy-done
  1.6 0.9 copy-done.1
  2.5 0.8 shard_map.68
  3.3 0.0 copy-start.3
  3.3 4.0 %collective-permute-start.2 = (bf16[256,128]{1,0:T(8,128)(2,1)S(1)}, bf16[256,128]{1,0:T(8,128)(2,1)S(1)}, u32[]{:S(2)}, u32[]{:S(2)}) collective-permute-start(bf16[256,128]{1,0:T(8,128)(2,1)S(1)} %get-tuple-element.27), channel_id=1, source_target_pairs={{0,1},{1,2},{2,3},{4,5},{5,6},{6,7},{8,9},{9,10},{10,11},{12,13},{... | collective-permute-start | bytes 196616 | tf_op jit(solution)/shard_map/ppermute | solution.py:280
  7.4 1.3 collective-permute-start.3
  8.7 4.4 %collective-permute-start = (bf16[64,128]{1,0:T(8,128)(2,1)S(1)}, bf16[64,128]{1,0:T(8,128)(2,1)S(1)}, u32[]{:S(2)}, u32[]{:S(2)}) collective-permute-start(bf16[64,128]{1,0:T(8,128)(2,1)S(1)} %get-tuple-element.25), channel_id=1, source_target_pairs={{0,4},{4,8},{8,12},{12,16},{16,20},{20,24},{24,28},{28,32},{32,36}... | collective-permute-start | bytes 49160 | tf_op jit(solution)/shard_map/ppermute | solution.py:280
  13.1 3.0 %collective-permute-start.1 = (bf16[64,128]{1,0:T(8,128)(2,1)S(1)}, bf16[64,128]{1,0:T(8,128)(2,1)S(1)}, u32[]{:S(2)}, u32[]{:S(2)}) collective-permute-start(bf16[64,128]{1,0:T(8,128)(2,1)S(1)} %get-tuple-element.26), channel_id=1, source_target_pairs={{4,0},{8,4},{12,8},{16,12},{20,16},{24,20},{28,24},{32,28},{36,32}... | collective-permute-start | bytes 49160 | tf_op jit(solution)/shard_map/ppermute | solution.py:280
  16.0 1.5 %shard_map.70 = bf16[1024,128]{1,0:T(8,128)(2,1)} custom-call(s32[1,1024]{1,0:T(1,128)S(1)} %copy-done.3, f32[512,128]{1,0:T(8,128)S(1)} %get-tuple-element.21.v), custom_call_target="tpu_custom_call" | custom-call | flops 1000000 | bytes 1048576 | tf_op jit(solution)/shard_map/pallas_call | solution.py:260
  17.5 19.4 %all-to-all-start = ((bf16[128,8,128]{2,1,0:T(8,128)(2,1)}), bf16[128,8,128]{2,1,0:T(8,128)(2,1)S(1)}, u32[]{:S(2)}, u32[]{:S(2)}) async-start(bf16[128,8,128]{2,1,0:T(8,128)(2,1)} %bitcast), calls=%async_computation | async-start | bytes 524288 | tf_op jit(solution)/shard_map/all_to_all | solution.py:334
  36.9 0.0 collective-permute-done.before
  36.9 0.0 collective-permute-done.1.after
  37.0 0.0 collective-permute-done.2.left
  37.0 0.0 collective-permute-done.3.right
  37.0 0.0 copy-start.2
  37.0 1.0 shard_map.69
  38.0 4.3 %collective-permute-start.6 = (bf16[256,128]{1,0:T(8,128)(2,1)S(1)}, bf16[256,128]{1,0:T(8,128)(2,1)S(1)}, u32[]{:S(2)}, u32[]{:S(2)}) collective-permute-start(bf16[256,128]{1,0:T(8,128)(2,1)S(1)} %get-tuple-element.34), channel_id=1, source_target_pairs={{0,1},{1,2},{2,3},{4,5},{5,6},{6,7},{8,9},{9,10},{10,11},{12,13},{... | collective-permute-start | bytes 196616 | tf_op jit(solution)/shard_map/ppermute | solution.py:280
  42.3 1.3 collective-permute-start.7
  43.6 3.8 %collective-permute-start.4 = (bf16[64,128]{1,0:T(8,128)(2,1)S(1)}, bf16[64,128]{1,0:T(8,128)(2,1)S(1)}, u32[]{:S(2)}, u32[]{:S(2)}) collective-permute-start(bf16[64,128]{1,0:T(8,128)(2,1)S(1)} %get-tuple-element.32), channel_id=1, source_target_pairs={{0,4},{4,8},{8,12},{12,16},{16,20},{20,24},{24,28},{28,32},{32,36}... | collective-permute-start | bytes 49160 | tf_op jit(solution)/shard_map/ppermute | solution.py:280
  47.4 1.9 %collective-permute-start.5 = (bf16[64,128]{1,0:T(8,128)(2,1)S(1)}, bf16[64,128]{1,0:T(8,128)(2,1)S(1)}, u32[]{:S(2)}, u32[]{:S(2)}) collective-permute-start(bf16[64,128]{1,0:T(8,128)(2,1)S(1)} %get-tuple-element.33), channel_id=1, source_target_pairs={{4,0},{8,4},{12,8},{16,12},{20,16},{24,20},{28,24},{32,28},{36,32}... | collective-permute-start | bytes 49160 | tf_op jit(solution)/shard_map/ppermute | solution.py:280
  49.3 10.1 %all-to-all-done = bf16[128,8,128]{2,1,0:T(8,128)(2,1)S(1)} async-done(((bf16[128,8,128]{2,1,0:T(8,128)(2,1)}), bf16[128,8,128]{2,1,0:T(8,128)(2,1)S(1)}, u32[]{:S(2)}, u32[]{:S(2)}) %all-to-all-start) | async-done | bytes 262176 | tf_op jit(solution)/shard_map/all_to_all | solution.py:334
  59.4 1.9 %shard_map.71 = (bf16[1024,128]{1,0:T(8,128)(2,1)}, f32[128,128]{1,0:T(8,128)S(1)}, f32[16,64]{1,0:T(8,128)S(1)}) custom-call(s32[1,1024]{1,0:T(1,128)S(1)} %copy-done.3, f32[512,128]{1,0:T(8,128)S(1)} %get-tuple-element.21.v, f32[512,128]{1,0:T(8,128)S(1)} %get-tuple-element.29.ap.v, bf16[16,1024]{1,0:T(8,128)(2,1)S(1)} %copy-done.2, ...), custom_call_target="tpu_custom_call" | custom-call | flops 1000000 | bytes 1048576 | tf_op jit(solution)/shard_map/pallas_call | solution.py:260
  61.4 7.4 %all-to-all-start.1 = ((bf16[128,8,128]{2,1,0:T(8,128)(2,1)}), bf16[128,8,128]{2,1,0:T(8,128)(2,1)S(1)}, u32[]{:S(2)}, u32[]{:S(2)}) async-start(bf16[128,8,128]{2,1,0:T(8,128)(2,1)} %bitcast.2), calls=%async_computation.1 | async-start | bytes 524288 | tf_op jit(solution)/shard_map/all_to_all | solution.py:334
  68.8 0.0 collective-permute-done.5.after
  68.8 0.0 collective-permute-done.6.left
  68.8 1.2 shard_map.72.packed
  70.0 21.3 %all-to-all-done.1 = bf16[128,8,128]{2,1,0:T(8,128)(2,1)S(1)} async-done(((bf16[128,8,128]{2,1,0:T(8,128)(2,1)}), bf16[128,8,128]{2,1,0:T(8,128)(2,1)S(1)}, u32[]{:S(2)}, u32[]{:S(2)}) %all-to-all-start.1) | async-done | bytes 262176 | tf_op jit(solution)/shard_map/all_to_all | solution.py:334
  91.3 0.2 shard_map.73
  91.5 16.0 %all_to_all.25 = f32[32,4,128]{2,1,0:T(4,128)S(1)} all-to-all(f32[32,4,128]{2,1,0:T(4,128)S(1)} %bitcast.9), channel_id=1, replica_groups={{0,1,2,3,4,5,6,7,128,129,130,131,132,133,134,135,256,257,258,259,260,26..., dimensions={0} | all-to-all | bytes 131072 | tf_op jit(solution)/shard_map/all_to_all | solution.py:308
  107.6 14.1 %all_to_all.26 = f32[16,4,128]{2,1,0:T(4,128)S(1)} all-to-all(f32[16,4,128]{2,1,0:T(4,128)S(1)} %broadcast_in_dim.4), channel_id=1, replica_groups={{0,8,16,24,32,40,48,56,64,72,80,88,96,104,112,120},{1,9,17,25,33,41,49,..., dimensions={0} | all-to-all | bytes 65536 | tf_op jit(solution)/shard_map/all_to_all | solution.py:308
  121.7 11.9 %all_to_all.27 = f32[32,4,128]{2,1,0:T(4,128)S(1)} all-to-all(f32[32,4,128]{2,1,0:T(4,128)S(1)} %broadcast_in_dim.5), channel_id=1, replica_groups={{0,1,2,3,4,5,6,7,128,129,130,131,132,133,134,135,256,257,258,259,260,26..., dimensions={0} | all-to-all | bytes 131072 | tf_op jit(solution)/shard_map/all_to_all | solution.py:308
  133.6 5.9 %shard_map.74 = (f32[16,64]{1,0:T(8,128)}, f32[64,64]{1,0:T(8,128)}) custom-call(f32[128,128]{1,0:T(8,128)S(1)} %bitcast.8, f32[16,64]{1,0:T(8,128)S(1)} %get-tuple-element.38.refs_1_, f32[16,64]{1,0:T(8,128)S(1)} %get-tuple-element.39.refs_2_), custom_call_target="tpu_custom_call" | custom-call | flops 1000000 | bytes 1048576 | tf_op jit(solution)/shard_map/pallas_call | solution.py:260
  (12 shorter events, 0.1 us)
Async XLA Ops:
  0.6 1.0 copy-start
  1.6 0.9 copy-start.1
  3.3 12.7 %copy-start.3 = (s32[1,1024]{1,0:T(1,128)S(1)}, s32[1,1024]{1,0:T(1,128)}, u32[]{:S(2)}) copy-start(s32[1,1024]{1,0:T(1,128)} %order.3) | copy-start | bytes 12292
  3.3 33.6 %collective-permute-start.2 = (bf16[256,128]{1,0:T(8,128)(2,1)S(1)}, bf16[256,128]{1,0:T(8,128)(2,1)S(1)}, u32[]{:S(2)}, u32[]{:S(2)}) collective-permute-start(bf16[256,128]{1,0:T(8,128)(2,1)S(1)} %get-tuple-element.27), channel_id=1, source_target_pairs={{0,1},{1,2},{2,3},{4,5},{5,6},{6,7},{8,9},{9,10},{10,11},{12,13},{... | collective-permute-start | bytes 196616 | tf_op jit(solution)/shard_map/ppermute | solution.py:280
  7.4 29.6 %collective-permute-start.3 = (bf16[256,128]{1,0:T(8,128)(2,1)S(1)}, bf16[256,128]{1,0:T(8,128)(2,1)S(1)}, u32[]{:S(2)}, u32[]{:S(2)}) collective-permute-start(bf16[256,128]{1,0:T(8,128)(2,1)S(1)} %get-tuple-element.28), channel_id=1, source_target_pairs={{1,0},{2,1},{3,2},{5,4},{6,5},{7,6},{9,8},{10,9},{11,10},{13,12},{... | collective-permute-start | bytes 196616 | tf_op jit(solution)/shard_map/ppermute | solution.py:280
  8.7 28.3 %collective-permute-start = (bf16[64,128]{1,0:T(8,128)(2,1)S(1)}, bf16[64,128]{1,0:T(8,128)(2,1)S(1)}, u32[]{:S(2)}, u32[]{:S(2)}) collective-permute-start(bf16[64,128]{1,0:T(8,128)(2,1)S(1)} %get-tuple-element.25), channel_id=1, source_target_pairs={{0,4},{4,8},{8,12},{12,16},{16,20},{20,24},{24,28},{28,32},{32,36}... | collective-permute-start | bytes 49160 | tf_op jit(solution)/shard_map/ppermute | solution.py:280
  13.1 23.9 %collective-permute-start.1 = (bf16[64,128]{1,0:T(8,128)(2,1)S(1)}, bf16[64,128]{1,0:T(8,128)(2,1)S(1)}, u32[]{:S(2)}, u32[]{:S(2)}) collective-permute-start(bf16[64,128]{1,0:T(8,128)(2,1)S(1)} %get-tuple-element.26), channel_id=1, source_target_pairs={{4,0},{8,4},{12,8},{16,12},{20,16},{24,20},{28,24},{32,28},{36,32}... | collective-permute-start | bytes 49160 | tf_op jit(solution)/shard_map/ppermute | solution.py:280
  17.5 19.5 %copy-start.4 = (f32[16,64]{1,0:T(8,128)S(1)}, f32[16,64]{1,0:T(8,128)}, u32[]{:S(2)}) copy-start(f32[16,64]{1,0:T(8,128)} %stor.3) | copy-start | bytes 12292
  17.5 41.9 %all-to-all-start = ((bf16[128,8,128]{2,1,0:T(8,128)(2,1)}), bf16[128,8,128]{2,1,0:T(8,128)(2,1)S(1)}, u32[]{:S(2)}, u32[]{:S(2)}) async-start(bf16[128,8,128]{2,1,0:T(8,128)(2,1)} %bitcast), calls=%async_computation | async-start | bytes 524288 | tf_op jit(solution)/shard_map/all_to_all | solution.py:334
  37.0 22.4 %copy-start.2 = (bf16[16,1024]{1,0:T(8,128)(2,1)S(1)}, bf16[16,1024]{1,0:T(8,128)(2,1)}, u32[]{:S(2)}) copy-start(bf16[16,1024]{1,0:T(8,128)(2,1)} %kriging.3) | copy-start | bytes 98308
  38.0 30.8 %collective-permute-start.6 = (bf16[256,128]{1,0:T(8,128)(2,1)S(1)}, bf16[256,128]{1,0:T(8,128)(2,1)S(1)}, u32[]{:S(2)}, u32[]{:S(2)}) collective-permute-start(bf16[256,128]{1,0:T(8,128)(2,1)S(1)} %get-tuple-element.34), channel_id=1, source_target_pairs={{0,1},{1,2},{2,3},{4,5},{5,6},{6,7},{8,9},{9,10},{10,11},{12,13},{... | collective-permute-start | bytes 196616 | tf_op jit(solution)/shard_map/ppermute | solution.py:280
  42.3 26.5 %collective-permute-start.7 = (bf16[256,128]{1,0:T(8,128)(2,1)S(1)}, bf16[256,128]{1,0:T(8,128)(2,1)S(1)}, u32[]{:S(2)}, u32[]{:S(2)}) collective-permute-start(bf16[256,128]{1,0:T(8,128)(2,1)S(1)} %get-tuple-element.35), channel_id=1, source_target_pairs={{1,0},{2,1},{3,2},{5,4},{6,5},{7,6},{9,8},{10,9},{11,10},{13,12},{... | collective-permute-start | bytes 196616 | tf_op jit(solution)/shard_map/ppermute | solution.py:280
  43.6 25.2 %collective-permute-start.4 = (bf16[64,128]{1,0:T(8,128)(2,1)S(1)}, bf16[64,128]{1,0:T(8,128)(2,1)S(1)}, u32[]{:S(2)}, u32[]{:S(2)}) collective-permute-start(bf16[64,128]{1,0:T(8,128)(2,1)S(1)} %get-tuple-element.32), channel_id=1, source_target_pairs={{0,4},{4,8},{8,12},{12,16},{16,20},{20,24},{24,28},{28,32},{32,36}... | collective-permute-start | bytes 49160 | tf_op jit(solution)/shard_map/ppermute | solution.py:280
  47.4 21.4 %collective-permute-start.5 = (bf16[64,128]{1,0:T(8,128)(2,1)S(1)}, bf16[64,128]{1,0:T(8,128)(2,1)S(1)}, u32[]{:S(2)}, u32[]{:S(2)}) collective-permute-start(bf16[64,128]{1,0:T(8,128)(2,1)S(1)} %get-tuple-element.33), channel_id=1, source_target_pairs={{4,0},{8,4},{12,8},{16,12},{20,16},{24,20},{28,24},{32,28},{36,32}... | collective-permute-start | bytes 49160 | tf_op jit(solution)/shard_map/ppermute | solution.py:280
  61.4 29.9 %all-to-all-start.1 = ((bf16[128,8,128]{2,1,0:T(8,128)(2,1)}), bf16[128,8,128]{2,1,0:T(8,128)(2,1)S(1)}, u32[]{:S(2)}, u32[]{:S(2)}) async-start(bf16[128,8,128]{2,1,0:T(8,128)(2,1)} %bitcast.2), calls=%async_computation.1 | async-start | bytes 524288 | tf_op jit(solution)/shard_map/all_to_all | solution.py:334

commit v4 on v3

--- a/solution.py
+++ b/solution.py
@@ -14,6 +14,8 @@
 BF16 = jnp.bfloat16
 HIGHEST = lax.Precision.HIGHEST
 PARAMS = pltpu.CompilerParams(vmem_limit_bytes=40 * 1024 * 1024)
+PIECES = 4
+WIDTH = RHS * CB // PIECES
 LONG = 10**11
 NN = (((1,), (0,)), ((), ()))
 NT = (((1,), (1,)), ((), ()))
@@ -59,7 +61,18 @@
         tr[part(i), :] = jnp.where(low, swap(even), odd).astype(BF16)
 
 
-def first_kernel(pump, coup, p_out, sh_out, sl_out, u_out, dl, dr, tl, tr, rows_p, rows_s, mats):
+def first_kernel(pump_hbm, coup_hbm, p_out, sh_out, sl_out, u_out, dl, dr, tl, tr, pump, coup, rows_p, rows_s, mats, arrived):
+    copies = []
+    for i in range(PIECES):
+        columns = pl.ds(i * WIDTH, WIDTH)
+        for j, (source, target) in enumerate(((coup_hbm, coup), (pump_hbm, pump))):
+            copies.append(
+                pltpu.make_async_copy(source.at[:, columns], target.at[:, columns], arrived.at[j, i])
+            )
+    for copy in copies:
+        copy.start()
+    for copy in copies:
+        copy.wait()
     for k in range(RHS // 2):
         chunk = slice(k * LANE, (k + 1) * LANE)
         rows_p[pl.ds(k, 16, stride=32), :] = pump[:, chunk]
@@ -120,11 +133,14 @@
     write_edges(spread, dl, dr, tl, tr)
 
 
-def deal(order, v, cells, table):
-    for x in range(FX):
-        high, rest = split(v[part(x), :])
-        table[:RHS, x * LANE : (x + 1) * LANE] = high
-        table[RHS:, x * LANE : (x + 1) * LANE] = rest
+def deal_kernel(order, v, ap, cells, grams, table):
+    total = jnp.zeros((2 * RHS, 2 * RHS), F32)
+    for x in range(FX):
+        high, rest = split(jnp.concatenate([v[part(x), :], ap[part(x), :]], axis=0))
+        table[: 2 * RHS, x * LANE : (x + 1) * LANE] = high
+        table[2 * RHS :, x * LANE : (x + 1) * LANE] = rest
+        total += dot3((high, rest), (high, rest), NT)
+    grams[...] = total
     lane = lax.broadcasted_iota(jnp.int32, (LANE, LANE), 1)
     for g in range(FX):
         row = jnp.broadcast_to(order[:, g * LANE : (g + 1) * LANE], (LANE, LANE))
@@ -135,21 +151,6 @@
         cells[pl.ds(g * LANE, LANE), :] = dot(
             jnp.concatenate(picks, axis=1), table[...], NT
         ).astype(BF16)
-
-
-def weigh(kriging, cells):
-    product = dot(kriging[...], cells[...], NN)
-    return product[:, :RHS] + product[:, RHS:]
-
-
-def deal_images(order, v, ap, kriging, arrived, cells, grams, weighted, table):
-    deal(order, ap, cells, table)
-    total = jnp.zeros((2 * RHS, 2 * RHS), F32)
-    for x in range(FX):
-        both = split(jnp.concatenate([v[part(x), :], ap[part(x), :]], axis=0))
-        total += dot3(both, both, NT)
-    grams[...] = total
-    weighted[...] = weigh(kriging, arrived)
 
 
 def third_kernel(v, u, sh, sl, stor, before, after, left, right, grams, packed):
@@ -168,11 +169,6 @@
     packed[:RHS, :] = jnp.concatenate([jnp.where(upper, m0, m2), jnp.where(upper, m1, m3)], axis=1)
     ends = jnp.where(row == 0, diagonal(m2), jnp.where(row == 1, diagonal(m3), 0.0))
     packed[RHS:, :] = jnp.concatenate([m4, ends], axis=1)
-
-
-def weigh_images(kriging, arrived, packed, weighted, packed_out):
-    weighted[...] = weigh(kriging, arrived)
-    packed_out[...] = packed[...]
 
 
 def square_index():
@@ -241,26 +237,40 @@
     return 0.5 * (matrix + jnp.transpose(matrix))
 
 
-def final_kernel(cell_total, packed, weighted_p, weighted_ap, sens, gram):
+def solve_kernel(packed, cells, heads, weights, later):
     m0, m2 = unpack_pair(packed[:RHS, :RHS], packed[RHS : RHS + 1, RHS:])
     m1, m3 = unpack_pair(packed[:RHS, RHS:], packed[RHS + 1 : RHS + 2, RHS:])
-    m4 = packed[RHS:, :RHS]
     first = eliminate(jnp.concatenate([m1, m0, m2], axis=1))
     alpha, shift = first[:, :RHS], first[:, RHS:]
     curved = symmetric(m3 - exact(m2, shift))
     target = m1 - exact(m2, alpha)
     gamma = eliminate(jnp.concatenate([curved, target], axis=1))
     mixed = alpha - exact(shift, gamma)
-    rest = exact(m4, gamma) + exact(m3, mixed) - m2
+    both = jnp.concatenate([mixed, gamma], axis=0)
+    high, rest = split(jnp.concatenate([both, both], axis=1))
+    value = dot3((cells[:, :LANE], cells[:, LANE:]), (high, rest), NN)
+    high = value.astype(BF16).astype(F32)
+    heads[...] = jnp.where(low_lanes(FX * LANE), high, value - high).astype(BF16)
+    weights[...] = both
+    later[...] = jnp.concatenate([m2, m3], axis=1)
+
+
+def gram_kernel(cell_total, packed, weights, later, gram):
+    mixed, gamma = weights[:RHS, :], weights[RHS:, :]
+    rest = exact(packed[RHS:, :RHS], gamma) + exact(later[:, RHS:], mixed) - later[:, :RHS]
     gram[...] = symmetric(exact(jnp.transpose(gamma), rest)) * (1.0 / cell_total)
-    sens[...] = exact(weighted_p[...], mixed) + exact(weighted_ap[...], gamma)
-
-
-def call(kernel, shapes, *operands, scratch=(), flops=1000000):
+
+
+def product_kernel(kriging, arrived, sens):
+    product = dot(kriging[...], arrived[...], NN)
+    sens[...] = product[:, :RHS] + product[:, RHS:]
+
+
+def call(kernel, shapes, *operands, scratch=(), flops=1000000, place=pltpu.VMEM):
     return pl.pallas_call(
         kernel,
         out_shape=[jax.ShapeDtypeStruct(shape, kind) for shape, kind in shapes],
-        in_specs=[pl.BlockSpec(memory_space=pltpu.VMEM)] * len(operands),
+        in_specs=[pl.BlockSpec(memory_space=place)] * len(operands),
         out_specs=[pl.BlockSpec(memory_space=pltpu.VMEM)] * len(shapes),
         scratch_shapes=list(scratch),
         compiler_params=PARAMS,
@@ -322,42 +332,45 @@
         (FIELD, ((FX * LANE, LANE), BF16), ((FX * LANE, LANE), BF16), FIELD) + EDGES,
         pumping,
         coupling,
-        scratch=(scratch(ROWS), scratch(ROWS), scratch(FX * LANE)),
+        scratch=(
+            pltpu.VMEM((16, RHS * CB), F32),
+            pltpu.VMEM((16, CB * CB), F32),
+            scratch(ROWS),
+            scratch(ROWS),
+            scratch(FX * LANE),
+            pltpu.SemaphoreType.DMA((2, PIECES)),
+        ),
+        place=pltpu.HBM,
     )
     halo = exchange(*edges)
-    table = pltpu.VMEM((2 * RHS, FX * LANE), BF16)
-    cells = ((FX * LANE, 2 * RHS), BF16)
-    product = ((kriging.shape[0], RHS), F32)
-
-    def deliver(rows):
-        rows = rows.reshape(groups, -1, 2 * RHS)
-        return lax.all_to_all(rows, "dom", 0, 0, tiled=True).reshape(-1, 2 * RHS)
-
-    (dealt,) = call(deal, (cells,), tile_order, p, scratch=(table,))
-    arrived = deliver(dealt)
-    ap, u, *edges = call(
-        second_kernel, (FIELD, FIELD) + EDGES, p, u, sh, sl, storage, *halo, flops=LONG
-    )
+    ap, u, *edges = call(second_kernel, (FIELD, FIELD) + EDGES, p, u, sh, sl, storage, *halo)
     halo = exchange(*edges)
-    dealt, grams, weighted_p = call(
-        deal_images,
-        (cells, ((2 * RHS, 2 * RHS), F32), product),
-        *(tile_order, p, ap, kriging, arrived),
-        scratch=(table,),
-    )
-    arrived = deliver(dealt)
-    moments = ((2 * RHS, LANE), F32)
+    cells, grams = call(
+        deal_kernel,
+        (((FX * LANE, 4 * RHS), BF16), ((2 * RHS, LANE), F32)),
+        *(tile_order, p, ap),
+        scratch=(pltpu.VMEM((4 * RHS, FX * LANE), BF16),),
+    )
     (packed,) = call(
-        third_kernel, (moments,), *(ap, u, sh, sl, storage, *halo, grams), flops=LONG
-    )
-    weighted_ap, packed = call(weigh_images, (product, moments), kriging, arrived, packed)
+        third_kernel, (((2 * RHS, LANE), F32),), ap, u, sh, sl, storage, *halo, grams
+    )
     packed = reduce_all(packed)
-    sens, gram = call(
-        lambda *refs: final_kernel(cell_total, *refs),
-        (((kriging.shape[0], RHS), F32), ((RHS, RHS), F32)),
-        packed,
-        weighted_p,
-        weighted_ap,
+    heads, weights, later = call(
+        solve_kernel,
+        (((FX * LANE, LANE), BF16), ((2 * RHS, RHS), F32), ((RHS, LANE), F32)),
+        *(packed, cells),
+    )
+    heads = lax.all_to_all(heads.reshape(groups, -1, LANE), "dom", 0, 0, tiled=True)
+    (gram,) = call(
+        lambda *refs: gram_kernel(cell_total, *refs),
+        (((RHS, RHS), F32),),
+        *(packed, weights, later),
+        flops=LONG,
+    )
+    (sens,) = call(
+        product_kernel,
+        (((kriging.shape[0], RHS), F32),),
+        *(kriging, heads.reshape(-1, LANE)),
     )
     return sens, gram
 

time: 140 us -> 124 us (0.89)
  starting transfers between devices: 50.8 us -> 28.1 us
  blocking collectives: 42 us -> 55.3 us
  waiting for transfers between devices: 31.4 us -> 24.5 us
    all_to_all x2 -> x1, starting transfers between devices: 26.8 us -> 5.54 us  [shards(): lax.all_to_all(heads.reshape(groups, -1, LANE), 'dom', 0, 0, tiled=True)]
    all_to_all x3, blocking collectives: 42 us -> 55.3 us  [trade(): lax.all_to_all(array, axes, 0, 0, axis_index_groups=groups, tiled=True)]
    all_to_all x2 -> x1, waiting for transfers between devices: 31.4 us -> 21.5 us  [shards(): lax.all_to_all(heads.reshape(groups, -1, LANE), 'dom', 0, 0, tiled=True)]
    ppermute x8, waiting for transfers between devices: 0.02 us -> 3.04 us  [along(): return (lax.ppermute(last, axis, up), lax.ppermute(first, axis, down))]
    ppermute x8, starting transfers between devices: 24 us -> 22.5 us  [along(): return (lax.ppermute(last, axis, up), lax.ppermute(first, axis, down))]
  transfers between devices with their start and end apart: 10 -> 9, of which waited for: 2 -> 3; matrix products, arithmetic and copies ran while one was open for 0% -> 0% of each run, Pallas kernels for 4% -> 3%
where the time goes in v4:
time: 124 us
  blocking collectives  55.3 us (45%)
  starting transfers between devices  28.1 us (23%)
  waiting for transfers between devices  24.5 us (20%)
  Pallas kernels  13.1 us (11%)
  local copies, waits for them, and re-layouts  1.93 us (2%)
    all_to_all x3, blocking collectives, trade(): lax.all_to_all(array, axes, 0, 0, axis_index_groups=groups, tiled=True)  55.3 us
    ppermute x8, starting transfers between devices, along(): return (lax.ppermute(last, axis, up), lax.ppermute(first, axis, down))  22.5 us
    all_to_all x1, waiting for transfers between devices, shards(): lax.all_to_all(heads.reshape(groups, -1, LANE), 'dom', 0, 0, tiled=True)  21.5 us
    pallas_call x7, Pallas kernels, call(): pl.pallas_call(kernel, out_shape=[jax.ShapeDtypeStruct(shape, kind) for s...  13.1 us
    all_to_all x1, starting transfers between devices, shards(): lax.all_to_all(heads.reshape(groups, -1, LANE), 'dom', 0, 0, tiled=True)  5.54 us
    ppermute x8, waiting for transfers between devices, along(): return (lax.ppermute(last, axis, up), lax.ppermute(first, axis, down))  3.04 us
  transfers between devices with their start and end apart: 9, of which 3 were waited for; matrix products, arithmetic and copies ran while one was open for 0% of the time, Pallas kernels for 3%

profile of v4, /device:TPU:1, one launch (start us, length us, event | category | flops | bytes accessed | tf_op | source)
XLA Modules:
  0.0 123.8 jit_solution(16949268333588007367)
XLA Ops:
  0.6 0.9 copy-done
  1.6 0.9 copy-done.1
  2.5 1.2 shard_map.68
  3.7 0.0 copy-start.2
  3.7 4.0 %collective-permute-start.2 = (bf16[256,128]{1,0:T(8,128)(2,1)S(1)}, bf16[256,128]{1,0:T(8,128)(2,1)S(1)}, u32[]{:S(2)}, u32[]{:S(2)}) collective-permute-start(bf16[256,128]{1,0:T(8,128)(2,1)S(1)} %get-tuple-element.27), channel_id=1, source_target_pairs={{0,1},{1,2},{2,3},{4,5},{5,6},{6,7},{8,9},{9,10},{10,11},{12,13},{... | collective-permute-start | bytes 196616 | tf_op jit(solution)/shard_map/ppermute | solution.py:290
  7.8 1.3 %collective-permute-start.3 = (bf16[256,128]{1,0:T(8,128)(2,1)S(1)}, bf16[256,128]{1,0:T(8,128)(2,1)S(1)}, u32[]{:S(2)}, u32[]{:S(2)}) collective-permute-start(bf16[256,128]{1,0:T(8,128)(2,1)S(1)} %get-tuple-element.28), channel_id=1, source_target_pairs={{1,0},{2,1},{3,2},{5,4},{6,5},{7,6},{9,8},{10,9},{11,10},{13,12},{... | collective-permute-start | bytes 196616 | tf_op jit(solution)/shard_map/ppermute | solution.py:290
  9.1 4.4 %collective-permute-start = (bf16[64,128]{1,0:T(8,128)(2,1)S(1)}, bf16[64,128]{1,0:T(8,128)(2,1)S(1)}, u32[]{:S(2)}, u32[]{:S(2)}) collective-permute-start(bf16[64,128]{1,0:T(8,128)(2,1)S(1)} %get-tuple-element.25), channel_id=1, source_target_pairs={{0,4},{4,8},{8,12},{12,16},{16,20},{20,24},{24,28},{28,32},{32,36}... | collective-permute-start | bytes 49160 | tf_op jit(solution)/shard_map/ppermute | solution.py:290
  13.5 3.0 %collective-permute-start.1 = (bf16[64,128]{1,0:T(8,128)(2,1)S(1)}, bf16[64,128]{1,0:T(8,128)(2,1)S(1)}, u32[]{:S(2)}, u32[]{:S(2)}) collective-permute-start(bf16[64,128]{1,0:T(8,128)(2,1)S(1)} %get-tuple-element.26), channel_id=1, source_target_pairs={{4,0},{8,4},{12,8},{16,12},{20,16},{24,20},{28,24},{32,28},{36,32}... | collective-permute-start | bytes 49160 | tf_op jit(solution)/shard_map/ppermute | solution.py:290
  16.4 0.0 collective-permute-done.before
  16.4 2.1 %collective-permute-done.1.after = bf16[64,128]{1,0:T(8,128)(2,1)S(1)} collective-permute-done((bf16[64,128]{1,0:T(8,128)(2,1)S(1)}, bf16[64,128]{1,0:T(8,128)(2,1)S(1)}, u32[]{:S(2)}, u32[]{:S(2)}) %collective-permute-start.1) | collective-permute-done | bytes 16416 | tf_op jit(solution)/shard_map/ppermute | solution.py:290
  18.5 0.0 collective-permute-done.2.left
  18.5 0.0 collective-permute-done.3.right
  18.5 1.0 shard_map.69
  19.5 0.0 copy-start.4
  19.6 4.3 %collective-permute-start.6 = (bf16[256,128]{1,0:T(8,128)(2,1)S(1)}, bf16[256,128]{1,0:T(8,128)(2,1)S(1)}, u32[]{:S(2)}, u32[]{:S(2)}) collective-permute-start(bf16[256,128]{1,0:T(8,128)(2,1)S(1)} %get-tuple-element.33), channel_id=1, source_target_pairs={{0,1},{1,2},{2,3},{4,5},{5,6},{6,7},{8,9},{9,10},{10,11},{12,13},{... | collective-permute-start | bytes 196616 | tf_op jit(solution)/shard_map/ppermute | solution.py:290
  23.8 1.3 %collective-permute-start.7 = (bf16[256,128]{1,0:T(8,128)(2,1)S(1)}, bf16[256,128]{1,0:T(8,128)(2,1)S(1)}, u32[]{:S(2)}, u32[]{:S(2)}) collective-permute-start(bf16[256,128]{1,0:T(8,128)(2,1)S(1)} %get-tuple-element.34), channel_id=1, source_target_pairs={{1,0},{2,1},{3,2},{5,4},{6,5},{7,6},{9,8},{10,9},{11,10},{13,12},{... | collective-permute-start | bytes 196616 | tf_op jit(solution)/shard_map/ppermute | solution.py:290
  25.1 2.2 %collective-permute-start.4 = (bf16[64,128]{1,0:T(8,128)(2,1)S(1)}, bf16[64,128]{1,0:T(8,128)(2,1)S(1)}, u32[]{:S(2)}, u32[]{:S(2)}) collective-permute-start(bf16[64,128]{1,0:T(8,128)(2,1)S(1)} %get-tuple-element.31), channel_id=1, source_target_pairs={{0,4},{4,8},{8,12},{12,16},{16,20},{20,24},{24,28},{28,32},{32,36}... | collective-permute-start | bytes 49160 | tf_op jit(solution)/shard_map/ppermute | solution.py:290
  27.4 2.1 %collective-permute-start.5 = (bf16[64,128]{1,0:T(8,128)(2,1)S(1)}, bf16[64,128]{1,0:T(8,128)(2,1)S(1)}, u32[]{:S(2)}, u32[]{:S(2)}) collective-permute-start(bf16[64,128]{1,0:T(8,128)(2,1)S(1)} %get-tuple-element.32), channel_id=1, source_target_pairs={{4,0},{8,4},{12,8},{16,12},{20,16},{24,20},{28,24},{32,28},{36,32}... | collective-permute-start | bytes 49160 | tf_op jit(solution)/shard_map/ppermute | solution.py:290
  29.5 2.0 %shard_map.70 = (bf16[1024,256]{1,0:T(8,128)(2,1)S(1)}, f32[128,128]{1,0:T(8,128)S(1)}) custom-call(s32[1,1024]{1,0:T(1,128)S(1)} %copy-done.4, f32[512,128]{1,0:T(8,128)S(1)} %get-tuple-element.21.v, f32[512,128]{1,0:T(8,128)S(1)} %get-tuple-element.29.ap.v), custom_call_target="tpu_custom_call" | custom-call | flops 1000000 | bytes 1048576 | tf_op jit(solution)/shard_map/pallas_call | solution.py:270
  31.5 0.9 collective-permute-done.5.after
  32.4 0.0 collective-permute-done.6.left
  32.4 0.0 collective-permute-done.7.right
  32.4 1.2 shard_map.71
  33.6 23.1 %all_to_all.20 = f32[32,4,128]{2,1,0:T(4,128)S(1)} all-to-all(f32[32,4,128]{2,1,0:T(4,128)S(1)} %bitcast.7), channel_id=1, replica_groups={{0,1,2,3,4,5,6,7,128,129,130,131,132,133,134,135,256,257,258,259,260,26..., dimensions={0} | all-to-all | bytes 131072 | tf_op jit(solution)/shard_map/all_to_all | solution.py:318
  56.8 19.9 %all_to_all.21 = f32[16,4,128]{2,1,0:T(4,128)S(1)} all-to-all(f32[16,4,128]{2,1,0:T(4,128)S(1)} %broadcast_in_dim.4), channel_id=1, replica_groups={{0,8,16,24,32,40,48,56,64,72,80,88,96,104,112,120},{1,9,17,25,33,41,49,..., dimensions={0} | all-to-all | bytes 65536 | tf_op jit(solution)/shard_map/all_to_all | solution.py:318
  76.7 12.3 %all_to_all.22 = f32[32,4,128]{2,1,0:T(4,128)S(1)} all-to-all(f32[32,4,128]{2,1,0:T(4,128)S(1)} %broadcast_in_dim.5), channel_id=1, replica_groups={{0,1,2,3,4,5,6,7,128,129,130,131,132,133,134,135,256,257,258,259,260,26..., dimensions={0} | all-to-all | bytes 131072 | tf_op jit(solution)/shard_map/all_to_all | solution.py:318
  89.0 5.8 %shard_map.72 = (bf16[1024,128]{1,0:T(8,128)(2,1)}, f32[128,64]{1,0:T(8,128)S(1)}, f32[64,128]{1,0:T(8,128)S(1)}) custom-call(f32[128,128]{1,0:T(8,128)S(1)} %bitcast.5, bf16[1024,256]{1,0:T(8,128)(2,1)S(1)} %get-tuple-element.36.cells), custom_call_target="tpu_custom_call" | custom-call | flops 1000000 | bytes 1048576 | tf_op jit(solution)/shard_map/pallas_call | solution.py:270
  94.8 5.5 %all-to-all-start.3 = ((bf16[128,8,128]{2,1,0:T(8,128)(2,1)}), bf16[128,8,128]{2,1,0:T(8,128)(2,1)S(1)}, u32[]{:S(2)}, u32[]{:S(2)}) async-start(bf16[128,8,128]{2,1,0:T(8,128)(2,1)} %bitcast.2), calls=%async_computation.3 | async-start | bytes 524288 | tf_op jit(solution)/shard_map/all_to_all | solution.py:363
  100.4 0.0 copy-start.3
  100.4 1.1 shard_map.74
  101.5 21.5 %all-to-all-done.3 = bf16[128,8,128]{2,1,0:T(8,128)(2,1)S(1)} async-done(((bf16[128,8,128]{2,1,0:T(8,128)(2,1)}), bf16[128,8,128]{2,1,0:T(8,128)(2,1)S(1)}, u32[]{:S(2)}, u32[]{:S(2)}) %all-to-all-start.3) | async-done | bytes 262176 | tf_op jit(solution)/shard_map/all_to_all | solution.py:363
  123.0 0.8 shard_map.73
  (10 shorter events, 0.1 us)
Async XLA Ops:
  0.6 1.0 copy-start
  1.6 0.9 copy-start.1
  3.7 14.8 %copy-start.2 = (f32[16,64]{1,0:T(8,128)S(1)}, f32[16,64]{1,0:T(8,128)}, u32[]{:S(2)}) copy-start(f32[16,64]{1,0:T(8,128)} %stor.3) | copy-start | bytes 12292
  3.7 14.8 %collective-permute-start.2 = (bf16[256,128]{1,0:T(8,128)(2,1)S(1)}, bf16[256,128]{1,0:T(8,128)(2,1)S(1)}, u32[]{:S(2)}, u32[]{:S(2)}) collective-permute-start(bf16[256,128]{1,0:T(8,128)(2,1)S(1)} %get-tuple-element.27), channel_id=1, source_target_pairs={{0,1},{1,2},{2,3},{4,5},{5,6},{6,7},{8,9},{9,10},{10,11},{12,13},{... | collective-permute-start | bytes 196616 | tf_op jit(solution)/shard_map/ppermute | solution.py:290
  7.8 10.8 %collective-permute-start.3 = (bf16[256,128]{1,0:T(8,128)(2,1)S(1)}, bf16[256,128]{1,0:T(8,128)(2,1)S(1)}, u32[]{:S(2)}, u32[]{:S(2)}) collective-permute-start(bf16[256,128]{1,0:T(8,128)(2,1)S(1)} %get-tuple-element.28), channel_id=1, source_target_pairs={{1,0},{2,1},{3,2},{5,4},{6,5},{7,6},{9,8},{10,9},{11,10},{13,12},{... | collective-permute-start | bytes 196616 | tf_op jit(solution)/shard_map/ppermute | solution.py:290
  9.1 7.4 %collective-permute-start = (bf16[64,128]{1,0:T(8,128)(2,1)S(1)}, bf16[64,128]{1,0:T(8,128)(2,1)S(1)}, u32[]{:S(2)}, u32[]{:S(2)}) collective-permute-start(bf16[64,128]{1,0:T(8,128)(2,1)S(1)} %get-tuple-element.25), channel_id=1, source_target_pairs={{0,4},{4,8},{8,12},{12,16},{16,20},{20,24},{24,28},{28,32},{32,36}... | collective-permute-start | bytes 49160 | tf_op jit(solution)/shard_map/ppermute | solution.py:290
  13.5 5.1 %collective-permute-start.1 = (bf16[64,128]{1,0:T(8,128)(2,1)S(1)}, bf16[64,128]{1,0:T(8,128)(2,1)S(1)}, u32[]{:S(2)}, u32[]{:S(2)}) collective-permute-start(bf16[64,128]{1,0:T(8,128)(2,1)S(1)} %get-tuple-element.26), channel_id=1, source_target_pairs={{4,0},{8,4},{12,8},{16,12},{20,16},{24,20},{28,24},{32,28},{36,32}... | collective-permute-start | bytes 49160 | tf_op jit(solution)/shard_map/ppermute | solution.py:290
  19.5 9.9 %copy-start.4 = (s32[1,1024]{1,0:T(1,128)S(1)}, s32[1,1024]{1,0:T(1,128)}, u32[]{:S(2)}) copy-start(s32[1,1024]{1,0:T(1,128)} %order.1) | copy-start | bytes 12292
  19.6 12.9 %collective-permute-start.6 = (bf16[256,128]{1,0:T(8,128)(2,1)S(1)}, bf16[256,128]{1,0:T(8,128)(2,1)S(1)}, u32[]{:S(2)}, u32[]{:S(2)}) collective-permute-start(bf16[256,128]{1,0:T(8,128)(2,1)S(1)} %get-tuple-element.33), channel_id=1, source_target_pairs={{0,1},{1,2},{2,3},{4,5},{5,6},{6,7},{8,9},{9,10},{10,11},{12,13},{... | collective-permute-start | bytes 196616 | tf_op jit(solution)/shard_map/ppermute | solution.py:290
  23.8 8.6 %collective-permute-start.7 = (bf16[256,128]{1,0:T(8,128)(2,1)S(1)}, bf16[256,128]{1,0:T(8,128)(2,1)S(1)}, u32[]{:S(2)}, u32[]{:S(2)}) collective-permute-start(bf16[256,128]{1,0:T(8,128)(2,1)S(1)} %get-tuple-element.34), channel_id=1, source_target_pairs={{1,0},{2,1},{3,2},{5,4},{6,5},{7,6},{9,8},{10,9},{11,10},{13,12},{... | collective-permute-start | bytes 196616 | tf_op jit(solution)/shard_map/ppermute | solution.py:290
  25.1 6.3 %collective-permute-start.4 = (bf16[64,128]{1,0:T(8,128)(2,1)S(1)}, bf16[64,128]{1,0:T(8,128)(2,1)S(1)}, u32[]{:S(2)}, u32[]{:S(2)}) collective-permute-start(bf16[64,128]{1,0:T(8,128)(2,1)S(1)} %get-tuple-element.31), channel_id=1, source_target_pairs={{0,4},{4,8},{8,12},{12,16},{16,20},{20,24},{24,28},{28,32},{32,36}... | collective-permute-start | bytes 49160 | tf_op jit(solution)/shard_map/ppermute | solution.py:290
  27.4 5.1 %collective-permute-start.5 = (bf16[64,128]{1,0:T(8,128)(2,1)S(1)}, bf16[64,128]{1,0:T(8,128)(2,1)S(1)}, u32[]{:S(2)}, u32[]{:S(2)}) collective-permute-start(bf16[64,128]{1,0:T(8,128)(2,1)S(1)} %get-tuple-element.32), channel_id=1, source_target_pairs={{4,0},{8,4},{12,8},{16,12},{20,16},{24,20},{28,24},{32,28},{36,32}... | collective-permute-start | bytes 49160 | tf_op jit(solution)/shard_map/ppermute | solution.py:290
  94.8 28.2 %all-to-all-start.3 = ((bf16[128,8,128]{2,1,0:T(8,128)(2,1)}), bf16[128,8,128]{2,1,0:T(8,128)(2,1)S(1)}, u32[]{:S(2)}, u32[]{:S(2)}) async-start(bf16[128,8,128]{2,1,0:T(8,128)(2,1)} %bitcast.2), calls=%async_computation.3 | async-start | bytes 524288 | tf_op jit(solution)/shard_map/all_to_all | solution.py:363
  100.4 22.6 %copy-start.3 = (bf16[16,1024]{1,0:T(8,128)(2,1)S(1)}, bf16[16,1024]{1,0:T(8,128)(2,1)}, u32[]{:S(2)}) copy-start(bf16[16,1024]{1,0:T(8,128)(2,1)} %kriging.1) | copy-start | bytes 98308

commit v5 on v4

--- a/solution.py
+++ b/solution.py
@@ -51,17 +51,30 @@
     return pl.ds(x * RHS, RHS)
 
 
-def write_edges(spread, dl, dr, tl, tr):
+def is_even(axis):
+    return lax.rem(lax.axis_index(axis), 2) == 0
+
+
+def by_parity(axis, first, second):
+    even = is_even(axis)
+    return jnp.where(even, first, second), jnp.where(even, second, first)
+
+
+def write_edges(spread, d1, d2, t1, t2):
     low = low_lanes(RHS)
-    dl[...] = spread[0].astype(BF16)
-    dr[...] = spread[FX - 1].astype(BF16)
+    one, two = by_parity("dom", spread[FX - 1], spread[0])
+    d1[...] = one.astype(BF16)
+    d2[...] = two.astype(BF16)
     for i in range(FX // 2):
         even, odd = spread[2 * i], spread[2 * i + 1]
-        tl[part(i), :] = jnp.where(low, even, swap(odd)).astype(BF16)
-        tr[part(i), :] = jnp.where(low, swap(even), odd).astype(BF16)
-
-
-def first_kernel(pump_hbm, coup_hbm, p_out, sh_out, sl_out, u_out, dl, dr, tl, tr, pump, coup, rows_p, rows_s, mats, arrived):
+        left = jnp.where(low, even, swap(odd))
+        right = jnp.where(low, swap(even), odd)
+        one, two = by_parity("tile", right, left)
+        t1[part(i), :] = one.astype(BF16)
+        t2[part(i), :] = two.astype(BF16)
+
+
+def first_kernel(pump_hbm, coup_hbm, p_out, sh_out, sl_out, u_out, d1, d2, t1, t2, pump, coup, rows_p, rows_s, mats, arrived):
     copies = []
     for i in range(PIECES):
         columns = pl.ds(i * WIDTH, WIDTH)
@@ -97,17 +110,22 @@
         u = dot3(split(p_out[part(x), :]), (high, rest), NN)
         u_out[part(x), :] = u
         spread.append(u)
-    write_edges(spread, dl, dr, tl, tr)
-
-
-def operator(v, u, sh, sl, stor, before, after, left, right):
+    write_edges(spread, d1, d2, t1, t2)
+
+
+def operator(v, u, sh, sl, stor, d1, d2, t1, t2):
     low = low_lanes(RHS)
     spread = [u[part(x), :] for x in range(FX)]
-    ends = [before[...].astype(F32)] + spread + [after[...].astype(F32)]
+    after, before = by_parity("dom", d1[...].astype(F32), d2[...].astype(F32))
+    ends = [before] + spread + [after]
+    right, left = [], []
+    for i in range(FX // 2):
+        one, two = by_parity("tile", t1[part(i), :].astype(F32), t2[part(i), :].astype(F32))
+        right.append(one)
+        left.append(two)
     applied = []
     for x in range(FX):
-        from_left = left[part(x // 2), :].astype(F32)
-        from_right = right[part(x // 2), :].astype(F32)
+        from_left, from_right = left[x // 2], right[x // 2]
         if x % 2 == 0:
             outside = jnp.where(low, from_left, swap(from_right))
         else:
@@ -121,8 +139,8 @@
     return applied
 
 
-def second_kernel(v, u, sh, sl, stor, before, after, left, right, ap_out, u_out, dl, dr, tl, tr):
-    applied = operator(v, u, sh, sl, stor, before, after, left, right)
+def second_kernel(v, u, sh, sl, stor, d1, d2, t1, t2, ap_out, u_out, *edges):
+    applied = operator(v, u, sh, sl, stor, d1, d2, t1, t2)
     spread = []
     for x in range(FX):
         ap_out[part(x), :] = applied[x]
@@ -130,17 +148,14 @@
         s = dot3(split(applied[x]), (sh[block, :], sl[block, :]), NN)
         u_out[part(x), :] = s
         spread.append(s)
-    write_edges(spread, dl, dr, tl, tr)
-
-
-def deal_kernel(order, v, ap, cells, grams, table):
-    total = jnp.zeros((2 * RHS, 2 * RHS), F32)
+    write_edges(spread, *edges)
+
+
+def deal_kernel(order, v, ap, cells, table):
     for x in range(FX):
         high, rest = split(jnp.concatenate([v[part(x), :], ap[part(x), :]], axis=0))
         table[: 2 * RHS, x * LANE : (x + 1) * LANE] = high
         table[2 * RHS :, x * LANE : (x + 1) * LANE] = rest
-        total += dot3((high, rest), (high, rest), NT)
-    grams[...] = total
     lane = lax.broadcasted_iota(jnp.int32, (LANE, LANE), 1)
     for g in range(FX):
         row = jnp.broadcast_to(order[:, g * LANE : (g + 1) * LANE], (LANE, LANE))
@@ -153,15 +168,18 @@
         ).astype(BF16)
 
 
-def third_kernel(v, u, sh, sl, stor, before, after, left, right, grams, packed):
-    applied = operator(v, u, sh, sl, stor, before, after, left, right)
+def third_kernel(v, u, sh, sl, stor, d1, d2, t1, t2, p, packed):
+    applied = operator(v, u, sh, sl, stor, d1, d2, t1, t2)
+    base = jnp.zeros((2 * RHS, 2 * RHS), F32)
     total = jnp.zeros((2 * RHS, RHS), F32)
     for x in range(FX):
-        high, rest = split(jnp.concatenate([v[part(x), :], applied[x]], axis=0))
-        total += dot3((high, rest), (high[RHS:], rest[RHS:]), NT)
-    m0 = symmetric(grams[:RHS, :RHS])
-    m1 = 0.5 * (grams[:RHS, RHS:] + grams[RHS:, :RHS])
-    m2 = symmetric(grams[RHS:, RHS:])
+        low, image = split(jnp.concatenate([p[part(x), :], v[part(x), :]], axis=0)), split(applied[x])
+        base += dot3(low, low, NT)
+        both = [jnp.concatenate([a[RHS:], b], axis=0) for a, b in zip(low, image)]
+        total += dot3(both, image, NT)
+    m0 = symmetric(base[:RHS, :RHS])
+    m1 = 0.5 * (base[:RHS, RHS:] + base[RHS:, :RHS])
+    m2 = symmetric(base[RHS:, RHS:])
     m3 = symmetric(total[:RHS])
     m4 = symmetric(total[RHS:])
     row, column = square_index()
@@ -282,14 +300,14 @@
 FIELD = ((ROWS, LANE), F32)
 
 
-def exchange(dl, dr, tl, tr):
-    def along(axis, first, last):
+def exchange(d1, d2, t1, t2):
+    def along(axis, one, two):
         devices = lax.axis_size(axis)
-        up = [(i, i + 1) for i in range(devices - 1)]
-        down = [(i + 1, i) for i in range(devices - 1)]
-        return lax.ppermute(last, axis, up), lax.ppermute(first, axis, down)
-
-    return along("dom", dl, dr) + along("tile", tl, tr)
+        first = [(i, i ^ 1) for i in range(devices)]
+        second = [(i, ((i + 1) ^ 1) - 1) for i in range(1, devices - 1)]
+        return lax.ppermute(one, axis, first), lax.ppermute(two, axis, second)
+
+    return along("dom", d1, d2) + along("tile", t1, t2)
 
 
 def member_groups(sizes, together):
@@ -330,8 +348,8 @@
     p, sh, sl, u, *edges = call(
         first_kernel,
         (FIELD, ((FX * LANE, LANE), BF16), ((FX * LANE, LANE), BF16), FIELD) + EDGES,
-        pumping,
-        coupling,
+        pltpu.with_memory_space_constraint(pumping, pltpu.HBM),
+        pltpu.with_memory_space_constraint(coupling, pltpu.HBM),
         scratch=(
             pltpu.VMEM((16, RHS * CB), F32),
             pltpu.VMEM((16, CB * CB), F32),
@@ -345,14 +363,15 @@
     halo = exchange(*edges)
     ap, u, *edges = call(second_kernel, (FIELD, FIELD) + EDGES, p, u, sh, sl, storage, *halo)
     halo = exchange(*edges)
-    cells, grams = call(
+    (packed,) = call(
+        third_kernel, (((2 * RHS, LANE), F32),), ap, u, sh, sl, storage, *halo, p
+    )
+    (cells,) = call(
         deal_kernel,
-        (((FX * LANE, 4 * RHS), BF16), ((2 * RHS, LANE), F32)),
+        (((FX * LANE, 4 * RHS), BF16),),
         *(tile_order, p, ap),
         scratch=(pltpu.VMEM((4 * RHS, FX * LANE), BF16),),
-    )
-    (packed,) = call(
-        third_kernel, (((2 * RHS, LANE), F32),), ap, u, sh, sl, storage, *halo, grams
+        flops=LONG,
     )
     packed = reduce_all(packed)
     heads, weights, later = call(

time: 124 us -> 123 us (level)
  blocking collectives: 55.3 us -> 40.2 us
  waiting for transfers between devices: 24.5 us -> 33.2 us
  starting transfers between devices: 28.1 us -> 33.9 us
  local copies, waits for them, and re-layouts: 1.93 us -> 0.67 us
    all_to_all x3 -> x2, blocking collectives: 55.3 us -> 40.2 us  [trade(): lax.all_to_all(array, axes, 0, 0, axis_index_groups=groups, tiled=True)]
    all_to_all x0 -> x1, waiting for transfers between devices: none -> 5.77 us  [trade(): lax.all_to_all(array, axes, 0, 0, axis_index_groups=groups, tiled=True)]
    all_to_all x0 -> x1, starting transfers between devices: none -> 5.41 us  [trade(): lax.all_to_all(array, axes, 0, 0, axis_index_groups=groups, tiled=True)]
    ppermute x8, waiting for transfers between devices: 3.04 us -> 5.96 us  [along(): return (lax.ppermute(one, axis, first), lax.ppermute(two, axis, second))]
    unnamed x10 -> x6, local copies, waits for them, and re-layouts: 1.91 us -> 0.02 us
  transfers between devices with their start and end apart: 9 -> 10, of which waited for: 3 -> 4; matrix products, arithmetic and copies ran while one was open for 0% -> 0% of each run, Pallas kernels for 3% -> 2%
where the time goes in v5:
time: 123 us
  blocking collectives  40.2 us (33%)
  starting transfers between devices  33.9 us (28%)
  waiting for transfers between devices  33.2 us (27%)
  Pallas kernels  13.9 us (11%)
    all_to_all x2, blocking collectives, trade(): lax.all_to_all(array, axes, 0, 0, axis_index_groups=groups, tiled=True)  40.2 us
    ppermute x8, starting transfers between devices, along(): return (lax.ppermute(one, axis, first), lax.ppermute(two, axis, second))  23 us
    all_to_all x1, waiting for transfers between devices, shards(): lax.all_to_all(heads.reshape(groups, -1, LANE), 'dom', 0, 0, tiled=True)  21.5 us
    pallas_call x7, Pallas kernels, call(): pl.pallas_call(kernel, out_shape=[jax.ShapeDtypeStruct(shape, kind) for s...  13.9 us
    ppermute x8, waiting for transfers between devices, along(): return (lax.ppermute(one, axis, first), lax.ppermute(two, axis, second))  5.96 us
    all_to_all x1, waiting for transfers between devices, trade(): lax.all_to_all(array, axes, 0, 0, axis_index_groups=groups, tiled=True)  5.77 us
    all_to_all x1, starting transfers between devices, shards(): lax.all_to_all(heads.reshape(groups, -1, LANE), 'dom', 0, 0, tiled=True)  5.53 us
    all_to_all x1, starting transfers between devices, trade(): lax.all_to_all(array, axes, 0, 0, axis_index_groups=groups, tiled=True)  5.41 us
  transfers between devices with their start and end apart: 10, of which 4 were waited for; matrix products, arithmetic and copies ran while one was open for 0% of the time, Pallas kernels for 2%

profile of v5, /device:TPU:1, one launch (start us, length us, event | category | flops | bytes accessed | tf_op | source)
XLA Modules:
  0.0 122.8 jit_solution(4516096561471362770)
XLA Ops:
  0.6 1.9 %shard_map.68 = (f32[512,128]{1,0:T(8,128)S(1)}, bf16[1024,128]{1,0:T(8,128)(2,1)S(1)}, bf16[1024,128]{1,0:T(8,128)(2,1)S(1)}, f32[512,128]{1,0:T(8,128)S(1)}, b...) custom-call(f32[16,4096]{1,0:T(8,128)} %pump_hbm.1, ...), custom_call_target="tpu_custom_call" | custom-call | flops 1000000 | bytes 1048576 | tf_op jit(solution)/shard_map/pallas_call | solution.py:288
  2.6 0.0 copy-start
  2.6 4.0 %collective-permute-start.2 = (bf16[256,128]{1,0:T(8,128)(2,1)S(1)}, bf16[256,128]{1,0:T(8,128)(2,1)S(1)}, u32[]{:S(2)}, u32[]{:S(2)}) collective-permute-start(bf16[256,128]{1,0:T(8,128)(2,1)S(1)} %get-tuple-element.25), channel_id=1, source_target_pairs={{0,1},{1,0},{2,3},{3,2},{4,5},{5,4},{6,7},{7,6},{8,9},{9,8},{10,11... | collective-permute-start | bytes 196616 | tf_op jit(solution)/shard_map/ppermute | solution.py:308
  6.6 0.7 collective-permute-start.3
  7.3 6.7 %collective-permute-start = (bf16[64,128]{1,0:T(8,128)(2,1)S(1)}, bf16[64,128]{1,0:T(8,128)(2,1)S(1)}, u32[]{:S(2)}, u32[]{:S(2)}) collective-permute-start(bf16[64,128]{1,0:T(8,128)(2,1)S(1)} %get-tuple-element.23), channel_id=1, source_target_pairs={{0,4},{4,0},{8,12},{12,8},{16,20},{20,16},{24,28},{28,24},{32,36},... | collective-permute-start | bytes 49160 | tf_op jit(solution)/shard_map/ppermute | solution.py:308
  14.0 1.9 %collective-permute-start.1 = (bf16[64,128]{1,0:T(8,128)(2,1)S(1)}, bf16[64,128]{1,0:T(8,128)(2,1)S(1)}, u32[]{:S(2)}, u32[]{:S(2)}) collective-permute-start(bf16[64,128]{1,0:T(8,128)(2,1)S(1)} %get-tuple-element.24), channel_id=1, source_target_pairs={{4,8},{8,4},{12,16},{16,12},{20,24},{24,20},{28,32},{32,28},{36,40... | collective-permute-start | bytes 49160 | tf_op jit(solution)/shard_map/ppermute | solution.py:308
  15.9 0.0 collective-permute-done.d1
  15.9 3.1 %collective-permute-done.1.d2 = bf16[64,128]{1,0:T(8,128)(2,1)S(1)} collective-permute-done((bf16[64,128]{1,0:T(8,128)(2,1)S(1)}, bf16[64,128]{1,0:T(8,128)(2,1)S(1)}, u32[]{:S(2)}, u32[]{:S(2)}) %collective-permute-start.1) | collective-permute-done | bytes 16416 | tf_op jit(solution)/shard_map/ppermute | solution.py:308
  19.0 0.0 collective-permute-done.2.t1
  19.0 0.0 collective-permute-done.3.t2
  19.0 1.0 shard_map.69
  20.0 4.9 %collective-permute-start.6 = (bf16[256,128]{1,0:T(8,128)(2,1)S(1)}, bf16[256,128]{1,0:T(8,128)(2,1)S(1)}, u32[]{:S(2)}, u32[]{:S(2)}) collective-permute-start(bf16[256,128]{1,0:T(8,128)(2,1)S(1)} %get-tuple-element.31), channel_id=1, source_target_pairs={{0,1},{1,0},{2,3},{3,2},{4,5},{5,4},{6,7},{7,6},{8,9},{9,8},{10,11... | collective-permute-start | bytes 196616 | tf_op jit(solution)/shard_map/ppermute | solution.py:308
  24.9 0.7 collective-permute-start.7
  25.6 1.9 %collective-permute-start.4 = (bf16[64,128]{1,0:T(8,128)(2,1)S(1)}, bf16[64,128]{1,0:T(8,128)(2,1)S(1)}, u32[]{:S(2)}, u32[]{:S(2)}) collective-permute-start(bf16[64,128]{1,0:T(8,128)(2,1)S(1)} %get-tuple-element.29), channel_id=1, source_target_pairs={{0,4},{4,0},{8,12},{12,8},{16,20},{20,16},{24,28},{28,24},{32,36},... | collective-permute-start | bytes 49160 | tf_op jit(solution)/shard_map/ppermute | solution.py:308
  27.5 2.2 %collective-permute-start.5 = (bf16[64,128]{1,0:T(8,128)(2,1)S(1)}, bf16[64,128]{1,0:T(8,128)(2,1)S(1)}, u32[]{:S(2)}, u32[]{:S(2)}) collective-permute-start(bf16[64,128]{1,0:T(8,128)(2,1)S(1)} %get-tuple-element.30), channel_id=1, source_target_pairs={{4,8},{8,4},{12,16},{16,12},{20,24},{24,20},{28,32},{32,28},{36,40... | collective-permute-start | bytes 49160 | tf_op jit(solution)/shard_map/ppermute | solution.py:308
  29.8 0.0 collective-permute-done.4.d1
  29.8 2.8 %collective-permute-done.5.d2 = bf16[64,128]{1,0:T(8,128)(2,1)S(1)} collective-permute-done((bf16[64,128]{1,0:T(8,128)(2,1)S(1)}, bf16[64,128]{1,0:T(8,128)(2,1)S(1)}, u32[]{:S(2)}, u32[]{:S(2)}) %collective-permute-start.5) | collective-permute-done | bytes 16416 | tf_op jit(solution)/shard_map/ppermute | solution.py:308
  32.6 0.0 collective-permute-done.6.t1
  32.6 0.0 collective-permute-done.7.t2
  32.6 1.7 %shard_map.70 = f32[128,128]{1,0:T(8,128)S(1)} custom-call(f32[512,128]{1,0:T(8,128)S(1)} %get-tuple-element.27.v.ap, f32[512,128]{1,0:T(8,128)S(1)} %get-tuple-element.28.u, bf16[1024,128]{1,0:T(8,128)(2,1)S(1)} %get-tuple-element.21.sh, bf16[1024,128]{1,0:T(8,128)(2,1)S(1)} %get-tuple-element.22.sl, f32[16,64]{1,0:T(8,128)S(1)} %copy-done, ...), custom_call_target="tpu_custom_call" | custom-call | flops 1000000 | bytes 1048576 | tf_op jit(solution)/shard_map/pallas_call | solution.py:288
  34.3 21.6 %all_to_all.20 = f32[32,4,128]{2,1,0:T(4,128)S(1)} all-to-all(f32[32,4,128]{2,1,0:T(4,128)S(1)} %bitcast.7), channel_id=1, replica_groups={{0,1,2,3,4,5,6,7,128,129,130,131,132,133,134,135,256,257,258,259,260,26..., dimensions={0} | all-to-all | bytes 131072 | tf_op jit(solution)/shard_map/all_to_all | solution.py:336
  56.0 18.6 %all_to_all.21 = f32[16,4,128]{2,1,0:T(4,128)S(1)} all-to-all(f32[16,4,128]{2,1,0:T(4,128)S(1)} %broadcast_in_dim.4), channel_id=1, replica_groups={{0,8,16,24,32,40,48,56,64,72,80,88,96,104,112,120},{1,9,17,25,33,41,49,..., dimensions={0} | all-to-all | bytes 65536 | tf_op jit(solution)/shard_map/all_to_all | solution.py:336
  74.6 0.6 broadcast_in_dim.5
  75.2 5.4 %all-to-all-start.2 = ((f32[32,4,128]{2,1,0:T(4,128)}), f32[32,4,128]{2,1,0:T(4,128)S(1)}, u32[]{:S(2)}, u32[]{:S(2)}) async-start(f32[32,4,128]{2,1,0:T(4,128)} %broadcast_in_dim.5), calls=%async_computation.2 | async-start | bytes 131072 | tf_op jit(solution)/shard_map/all_to_all | solution.py:336
  80.7 1.5 %shard_map.71.cells = bf16[1024,256]{1,0:T(8,128)(2,1)S(1)} custom-call(s32[1,1024]{1,0:T(1,128)S(1)} %copy-done.2, f32[512,128]{1,0:T(8,128)S(1)} %get-tuple-element.19.v.p, f32[512,128]{1,0:T(8,128)S(1)} %get-tuple-element.27.v.ap), custom_call_target="tpu_custom_call" | custom-call | flops 99999997952 | bytes 1048576 | tf_op jit(solution)/shard_map/pallas_call | solution.py:288
  82.2 5.8 %all-to-all-done.2 = f32[32,4,128]{2,1,0:T(4,128)S(1)} async-done(((f32[32,4,128]{2,1,0:T(4,128)}), f32[32,4,128]{2,1,0:T(4,128)S(1)}, u32[]{:S(2)}, u32[]{:S(2)}) %all-to-all-start.2) | async-done | bytes 65568 | tf_op jit(solution)/shard_map/all_to_all | solution.py:336
  88.0 5.8 %shard_map.72 = (bf16[1024,128]{1,0:T(8,128)(2,1)}, f32[128,64]{1,0:T(8,128)S(1)}, f32[64,128]{1,0:T(8,128)S(1)}) custom-call(f32[128,128]{1,0:T(8,128)S(1)} %bitcast.5, bf16[1024,256]{1,0:T(8,128)(2,1)S(1)} %shard_map.71.cells), custom_call_target="tpu_custom_call" | custom-call | flops 1000000 | bytes 1048576 | tf_op jit(solution)/shard_map/pallas_call | solution.py:288
  93.8 5.5 %all-to-all-start.3 = ((bf16[128,8,128]{2,1,0:T(8,128)(2,1)}), bf16[128,8,128]{2,1,0:T(8,128)(2,1)S(1)}, u32[]{:S(2)}, u32[]{:S(2)}) async-start(bf16[128,8,128]{2,1,0:T(8,128)(2,1)} %bitcast.2), calls=%async_computation.3 | async-start | bytes 524288 | tf_op jit(solution)/shard_map/all_to_all | solution.py:382
  99.4 0.0 copy-start.1
  99.4 1.1 shard_map.74
  100.5 21.5 %all-to-all-done.3 = bf16[128,8,128]{2,1,0:T(8,128)(2,1)S(1)} async-done(((bf16[128,8,128]{2,1,0:T(8,128)(2,1)}), bf16[128,8,128]{2,1,0:T(8,128)(2,1)S(1)}, u32[]{:S(2)}, u32[]{:S(2)}) %all-to-all-start.3) | async-done | bytes 262176 | tf_op jit(solution)/shard_map/all_to_all | solution.py:382
  122.0 0.8 shard_map.73
  (7 shorter events, 0.1 us)
Async XLA Ops:
  2.6 16.5 %copy-start = (f32[16,64]{1,0:T(8,128)S(1)}, f32[16,64]{1,0:T(8,128)}, u32[]{:S(2)}) copy-start(f32[16,64]{1,0:T(8,128)} %stor.3) | copy-start | bytes 12292
  2.6 16.5 %collective-permute-start.2 = (bf16[256,128]{1,0:T(8,128)(2,1)S(1)}, bf16[256,128]{1,0:T(8,128)(2,1)S(1)}, u32[]{:S(2)}, u32[]{:S(2)}) collective-permute-start(bf16[256,128]{1,0:T(8,128)(2,1)S(1)} %get-tuple-element.25), channel_id=1, source_target_pairs={{0,1},{1,0},{2,3},{3,2},{4,5},{5,4},{6,7},{7,6},{8,9},{9,8},{10,11... | collective-permute-start | bytes 196616 | tf_op jit(solution)/shard_map/ppermute | solution.py:308
  6.6 12.4 %collective-permute-start.3 = (bf16[256,128]{1,0:T(8,128)(2,1)S(1)}, bf16[256,128]{1,0:T(8,128)(2,1)S(1)}, u32[]{:S(2)}, u32[]{:S(2)}) collective-permute-start(bf16[256,128]{1,0:T(8,128)(2,1)S(1)} %get-tuple-element.26), channel_id=1, source_target_pairs={{1,2},{2,1},{5,6},{6,5},{9,10},{10,9},{13,14},{14,13},{17,18},{18,... | collective-permute-start | bytes 196616 | tf_op jit(solution)/shard_map/ppermute | solution.py:308
  7.3 8.6 %collective-permute-start = (bf16[64,128]{1,0:T(8,128)(2,1)S(1)}, bf16[64,128]{1,0:T(8,128)(2,1)S(1)}, u32[]{:S(2)}, u32[]{:S(2)}) collective-permute-start(bf16[64,128]{1,0:T(8,128)(2,1)S(1)} %get-tuple-element.23), channel_id=1, source_target_pairs={{0,4},{4,0},{8,12},{12,8},{16,20},{20,16},{24,28},{28,24},{32,36},... | collective-permute-start | bytes 49160 | tf_op jit(solution)/shard_map/ppermute | solution.py:308
  14.0 5.1 %collective-permute-start.1 = (bf16[64,128]{1,0:T(8,128)(2,1)S(1)}, bf16[64,128]{1,0:T(8,128)(2,1)S(1)}, u32[]{:S(2)}, u32[]{:S(2)}) collective-permute-start(bf16[64,128]{1,0:T(8,128)(2,1)S(1)} %get-tuple-element.24), channel_id=1, source_target_pairs={{4,8},{8,4},{12,16},{16,12},{20,24},{24,20},{28,32},{32,28},{36,40... | collective-permute-start | bytes 49160 | tf_op jit(solution)/shard_map/ppermute | solution.py:308
  20.0 12.6 %collective-permute-start.6 = (bf16[256,128]{1,0:T(8,128)(2,1)S(1)}, bf16[256,128]{1,0:T(8,128)(2,1)S(1)}, u32[]{:S(2)}, u32[]{:S(2)}) collective-permute-start(bf16[256,128]{1,0:T(8,128)(2,1)S(1)} %get-tuple-element.31), channel_id=1, source_target_pairs={{0,1},{1,0},{2,3},{3,2},{4,5},{5,4},{6,7},{7,6},{8,9},{9,8},{10,11... | collective-permute-start | bytes 196616 | tf_op jit(solution)/shard_map/ppermute | solution.py:308
  24.9 7.7 %collective-permute-start.7 = (bf16[256,128]{1,0:T(8,128)(2,1)S(1)}, bf16[256,128]{1,0:T(8,128)(2,1)S(1)}, u32[]{:S(2)}, u32[]{:S(2)}) collective-permute-start(bf16[256,128]{1,0:T(8,128)(2,1)S(1)} %get-tuple-element.32), channel_id=1, source_target_pairs={{1,2},{2,1},{5,6},{6,5},{9,10},{10,9},{13,14},{14,13},{17,18},{18,... | collective-permute-start | bytes 196616 | tf_op jit(solution)/shard_map/ppermute | solution.py:308
  25.6 4.2 %collective-permute-start.4 = (bf16[64,128]{1,0:T(8,128)(2,1)S(1)}, bf16[64,128]{1,0:T(8,128)(2,1)S(1)}, u32[]{:S(2)}, u32[]{:S(2)}) collective-permute-start(bf16[64,128]{1,0:T(8,128)(2,1)S(1)} %get-tuple-element.29), channel_id=1, source_target_pairs={{0,4},{4,0},{8,12},{12,8},{16,20},{20,16},{24,28},{28,24},{32,36},... | collective-permute-start | bytes 49160 | tf_op jit(solution)/shard_map/ppermute | solution.py:308
  27.5 5.1 %collective-permute-start.5 = (bf16[64,128]{1,0:T(8,128)(2,1)S(1)}, bf16[64,128]{1,0:T(8,128)(2,1)S(1)}, u32[]{:S(2)}, u32[]{:S(2)}) collective-permute-start(bf16[64,128]{1,0:T(8,128)(2,1)S(1)} %get-tuple-element.30), channel_id=1, source_target_pairs={{4,8},{8,4},{12,16},{16,12},{20,24},{24,20},{28,32},{32,28},{36,40... | collective-permute-start | bytes 49160 | tf_op jit(solution)/shard_map/ppermute | solution.py:308
  75.2 5.4 %copy-start.2 = (s32[1,1024]{1,0:T(1,128)S(1)}, s32[1,1024]{1,0:T(1,128)}, u32[]{:S(2)}) copy-start(s32[1,1024]{1,0:T(1,128)} %order.1) | copy-start | bytes 12292
  75.2 12.8 %all-to-all-start.2 = ((f32[32,4,128]{2,1,0:T(4,128)}), f32[32,4,128]{2,1,0:T(4,128)S(1)}, u32[]{:S(2)}, u32[]{:S(2)}) async-start(f32[32,4,128]{2,1,0:T(4,128)} %broadcast_in_dim.5), calls=%async_computation.2 | async-start | bytes 131072 | tf_op jit(solution)/shard_map/all_to_all | solution.py:336
  93.8 28.2 %all-to-all-start.3 = ((bf16[128,8,128]{2,1,0:T(8,128)(2,1)}), bf16[128,8,128]{2,1,0:T(8,128)(2,1)S(1)}, u32[]{:S(2)}, u32[]{:S(2)}) async-start(bf16[128,8,128]{2,1,0:T(8,128)(2,1)} %bitcast.2), calls=%async_computation.3 | async-start | bytes 524288 | tf_op jit(solution)/shard_map/all_to_all | solution.py:382
  99.4 22.6 %copy-start.1 = (bf16[16,1024]{1,0:T(8,128)(2,1)S(1)}, bf16[16,1024]{1,0:T(8,128)(2,1)}, u32[]{:S(2)}) copy-start(bf16[16,1024]{1,0:T(8,128)(2,1)} %kriging.1) | copy-start | bytes 98308

commit v6 on v5

--- a/solution.py
+++ b/solution.py
@@ -64,7 +64,8 @@
     low = low_lanes(RHS)
     one, two = by_parity("dom", spread[FX - 1], spread[0])
     d1[...] = one.astype(BF16)
-    d2[...] = two.astype(BF16)
+    d2[:RHS, :] = two.astype(BF16)
+    d2[RHS:, :] = jnp.zeros((d2.shape[0] - RHS, LANE), BF16)
     for i in range(FX // 2):
         even, odd = spread[2 * i], spread[2 * i + 1]
         left = jnp.where(low, even, swap(odd))
@@ -116,7 +117,7 @@
 def operator(v, u, sh, sl, stor, d1, d2, t1, t2):
     low = low_lanes(RHS)
     spread = [u[part(x), :] for x in range(FX)]
-    after, before = by_parity("dom", d1[...].astype(F32), d2[...].astype(F32))
+    after, before = by_parity("dom", d1[...].astype(F32), d2[:RHS, :].astype(F32))
     ends = [before] + spread + [after]
     right, left = [], []
     for i in range(FX // 2):
@@ -296,7 +297,7 @@
     )(*operands)
 
 
-EDGES = (((RHS, LANE), BF16), ((RHS, LANE), BF16), ((ROWS // 2, LANE), BF16), ((ROWS // 2, LANE), BF16))
+EDGES = (((RHS, LANE), BF16), ((ROWS // 2 + 16, LANE), BF16), ((ROWS // 2, LANE), BF16), ((ROWS // 2, LANE), BF16))
 FIELD = ((ROWS, LANE), F32)
 
 
@@ -305,9 +306,12 @@
         devices = lax.axis_size(axis)
         first = [(i, i ^ 1) for i in range(devices)]
         second = [(i, ((i + 1) ^ 1) - 1) for i in range(1, devices - 1)]
-        return lax.ppermute(one, axis, first), lax.ppermute(two, axis, second)
-
-    return along("dom", d1, d2) + along("tile", t1, t2)
+        two = lax.ppermute(two, axis, second)
+        return lax.ppermute(one, axis, first), two
+
+    t1, t2 = along("tile", t1, t2)
+    d1, d2 = along("dom", d1, d2)
+    return d1, d2, t1, t2
 
 
 def member_groups(sizes, together):

time: 123 us -> 119 us (0.967)
  waiting for transfers between devices: 33.2 us -> 29.2 us
    ppermute x8, waiting for transfers between devices: 5.96 us -> 1.98 us  [the longest x4 1.97 us: along(): return (lax.ppermute(one, axis, first), two)]
where the time goes in v6:
time: 119 us
  blocking collectives  40.5 us (34%)
  starting transfers between devices  33.6 us (28%)
  waiting for transfers between devices  29.2 us (25%)
  Pallas kernels  13.9 us (12%)
    all_to_all x2, blocking collectives, trade(): lax.all_to_all(array, axes, 0, 0, axis_index_groups=groups, tiled=True)  40.5 us
    all_to_all x1, waiting for transfers between devices, shards(): lax.all_to_all(heads.reshape(groups, -1, LANE), 'dom', 0, 0, tiled=True)  21.5 us
    pallas_call x7, Pallas kernels, call(): pl.pallas_call(kernel, out_shape=[jax.ShapeDtypeStruct(shape, kind) for s...  13.9 us
    ppermute x4, starting transfers between devices, along(): return (lax.ppermute(one, axis, first), two)  13.8 us
    ppermute x4, starting transfers between devices, along(): two = lax.ppermute(two, axis, second)  8.88 us
    all_to_all x1, waiting for transfers between devices, trade(): lax.all_to_all(array, axes, 0, 0, axis_index_groups=groups, tiled=True)  5.78 us
    all_to_all x1, starting transfers between devices, shards(): lax.all_to_all(heads.reshape(groups, -1, LANE), 'dom', 0, 0, tiled=True)  5.53 us
    all_to_all x1, starting transfers between devices, trade(): lax.all_to_all(array, axes, 0, 0, axis_index_groups=groups, tiled=True)  5.41 us
  transfers between devices with their start and end apart: 10, of which 4 were waited for; matrix products, arithmetic and copies ran while one was open for 0% of the time, Pallas kernels for 2%

profile of v6, /device:TPU:1, one launch (start us, length us, event | category | flops | bytes accessed | tf_op | source)
XLA Modules:
  0.0 118.8 jit_solution(7722116192755426559)
XLA Ops:
  0.6 1.9 %shard_map.68 = (f32[512,128]{1,0:T(8,128)S(1)}, bf16[1024,128]{1,0:T(8,128)(2,1)S(1)}, bf16[1024,128]{1,0:T(8,128)(2,1)S(1)}, f32[512,128]{1,0:T(8,128)S(1)}, b...) custom-call(f32[16,4096]{1,0:T(8,128)} %pump_hbm.1, ...), custom_call_target="tpu_custom_call" | custom-call | flops 1000000 | bytes 1048576 | tf_op jit(solution)/shard_map/pallas_call | solution.py:289
  2.6 0.0 copy-start
  2.6 4.9 %collective-permute-start.1 = (bf16[272,128]{1,0:T(8,128)(2,1)S(1)}, bf16[272,128]{1,0:T(8,128)(2,1)S(1)}, u32[]{:S(2)}, u32[]{:S(2)}) collective-permute-start(bf16[272,128]{1,0:T(8,128)(2,1)S(1)} %get-tuple-element.24), channel_id=1, source_target_pairs={{4,8},{8,4},{12,16},{16,12},{20,24},{24,20},{28,32},{32,28},{36,40... | collective-permute-start | bytes 208904 | tf_op jit(solution)/shard_map/ppermute | solution.py:309
  7.5 3.2 %collective-permute-start.2 = (bf16[256,128]{1,0:T(8,128)(2,1)S(1)}, bf16[256,128]{1,0:T(8,128)(2,1)S(1)}, u32[]{:S(2)}, u32[]{:S(2)}) collective-permute-start(bf16[256,128]{1,0:T(8,128)(2,1)S(1)} %get-tuple-element.25), channel_id=1, source_target_pairs={{0,1},{1,0},{2,3},{3,2},{4,5},{5,4},{6,7},{7,6},{8,9},{9,8},{10,11... | collective-permute-start | bytes 196616 | tf_op jit(solution)/shard_map/ppermute | solution.py:310
  10.7 0.7 collective-permute-start.3
  11.4 3.2 %collective-permute-start = (bf16[64,128]{1,0:T(8,128)(2,1)S(1)}, bf16[64,128]{1,0:T(8,128)(2,1)S(1)}, u32[]{:S(2)}, u32[]{:S(2)}) collective-permute-start(bf16[64,128]{1,0:T(8,128)(2,1)S(1)} %get-tuple-element.23), channel_id=1, source_target_pairs={{0,4},{4,0},{8,12},{12,8},{16,20},{20,16},{24,28},{28,24},{32,36},... | collective-permute-start | bytes 49160 | tf_op jit(solution)/shard_map/ppermute | solution.py:310
  14.6 0.8 collective-permute-done.d1
  15.5 0.0 collective-permute-done.2.t1
  15.5 0.0 collective-permute-done.3.t2
  15.5 0.0 collective-permute-done.1.d2
  15.5 1.0 shard_map.69
  16.5 2.6 %collective-permute-start.5 = (bf16[272,128]{1,0:T(8,128)(2,1)S(1)}, bf16[272,128]{1,0:T(8,128)(2,1)S(1)}, u32[]{:S(2)}, u32[]{:S(2)}) collective-permute-start(bf16[272,128]{1,0:T(8,128)(2,1)S(1)} %get-tuple-element.30), channel_id=1, source_target_pairs={{4,8},{8,4},{12,16},{16,12},{20,24},{24,20},{28,32},{32,28},{36,40... | collective-permute-start | bytes 208904 | tf_op jit(solution)/shard_map/ppermute | solution.py:309
  19.1 5.5 %collective-permute-start.6 = (bf16[256,128]{1,0:T(8,128)(2,1)S(1)}, bf16[256,128]{1,0:T(8,128)(2,1)S(1)}, u32[]{:S(2)}, u32[]{:S(2)}) collective-permute-start(bf16[256,128]{1,0:T(8,128)(2,1)S(1)} %get-tuple-element.31), channel_id=1, source_target_pairs={{0,1},{1,0},{2,3},{3,2},{4,5},{5,4},{6,7},{7,6},{8,9},{9,8},{10,11... | collective-permute-start | bytes 196616 | tf_op jit(solution)/shard_map/ppermute | solution.py:310
  24.6 0.7 collective-permute-start.7
  25.2 1.9 %collective-permute-start.4 = (bf16[64,128]{1,0:T(8,128)(2,1)S(1)}, bf16[64,128]{1,0:T(8,128)(2,1)S(1)}, u32[]{:S(2)}, u32[]{:S(2)}) collective-permute-start(bf16[64,128]{1,0:T(8,128)(2,1)S(1)} %get-tuple-element.29), channel_id=1, source_target_pairs={{0,4},{4,0},{8,12},{12,8},{16,20},{20,16},{24,28},{28,24},{32,36},... | collective-permute-start | bytes 49160 | tf_op jit(solution)/shard_map/ppermute | solution.py:310
  27.2 1.1 collective-permute-done.4.d1
  28.3 0.0 collective-permute-done.6.t1
  28.3 0.0 collective-permute-done.7.t2
  28.3 0.0 collective-permute-done.5.d2
  28.3 1.7 %shard_map.70 = f32[128,128]{1,0:T(8,128)S(1)} custom-call(f32[512,128]{1,0:T(8,128)S(1)} %get-tuple-element.27.v.ap, f32[512,128]{1,0:T(8,128)S(1)} %get-tuple-element.28.u, bf16[1024,128]{1,0:T(8,128)(2,1)S(1)} %get-tuple-element.21.sh, bf16[1024,128]{1,0:T(8,128)(2,1)S(1)} %get-tuple-element.22.sl, f32[16,64]{1,0:T(8,128)S(1)} %copy-done, ...), custom_call_target="tpu_custom_call" | custom-call | flops 1000000 | bytes 1048576 | tf_op jit(solution)/shard_map/pallas_call | solution.py:289
  30.0 21.6 %all_to_all.20 = f32[32,4,128]{2,1,0:T(4,128)S(1)} all-to-all(f32[32,4,128]{2,1,0:T(4,128)S(1)} %bitcast.7), channel_id=1, replica_groups={{0,1,2,3,4,5,6,7,128,129,130,131,132,133,134,135,256,257,258,259,260,26..., dimensions={0} | all-to-all | bytes 131072 | tf_op jit(solution)/shard_map/all_to_all | solution.py:340
  51.7 18.9 %all_to_all.21 = f32[16,4,128]{2,1,0:T(4,128)S(1)} all-to-all(f32[16,4,128]{2,1,0:T(4,128)S(1)} %broadcast_in_dim.4), channel_id=1, replica_groups={{0,8,16,24,32,40,48,56,64,72,80,88,96,104,112,120},{1,9,17,25,33,41,49,..., dimensions={0} | all-to-all | bytes 65536 | tf_op jit(solution)/shard_map/all_to_all | solution.py:340
  70.6 0.6 broadcast_in_dim.5
  71.2 5.4 %all-to-all-start.2 = ((f32[32,4,128]{2,1,0:T(4,128)}), f32[32,4,128]{2,1,0:T(4,128)S(1)}, u32[]{:S(2)}, u32[]{:S(2)}) async-start(f32[32,4,128]{2,1,0:T(4,128)} %broadcast_in_dim.5), calls=%async_computation.2 | async-start | bytes 131072 | tf_op jit(solution)/shard_map/all_to_all | solution.py:340
  76.7 1.5 %shard_map.71.cells = bf16[1024,256]{1,0:T(8,128)(2,1)S(1)} custom-call(s32[1,1024]{1,0:T(1,128)S(1)} %copy-done.2, f32[512,128]{1,0:T(8,128)S(1)} %get-tuple-element.19.v.p, f32[512,128]{1,0:T(8,128)S(1)} %get-tuple-element.27.v.ap), custom_call_target="tpu_custom_call" | custom-call | flops 99999997952 | bytes 1048576 | tf_op jit(solution)/shard_map/pallas_call | solution.py:289
  78.2 5.8 %all-to-all-done.2 = f32[32,4,128]{2,1,0:T(4,128)S(1)} async-done(((f32[32,4,128]{2,1,0:T(4,128)}), f32[32,4,128]{2,1,0:T(4,128)S(1)}, u32[]{:S(2)}, u32[]{:S(2)}) %all-to-all-start.2) | async-done | bytes 65568 | tf_op jit(solution)/shard_map/all_to_all | solution.py:340
  84.0 5.8 %shard_map.72 = (bf16[1024,128]{1,0:T(8,128)(2,1)}, f32[128,64]{1,0:T(8,128)S(1)}, f32[64,128]{1,0:T(8,128)S(1)}) custom-call(f32[128,128]{1,0:T(8,128)S(1)} %bitcast.5, bf16[1024,256]{1,0:T(8,128)(2,1)S(1)} %shard_map.71.cells), custom_call_target="tpu_custom_call" | custom-call | flops 1000000 | bytes 1048576 | tf_op jit(solution)/shard_map/pallas_call | solution.py:289
  89.8 5.5 %all-to-all-start.3 = ((bf16[128,8,128]{2,1,0:T(8,128)(2,1)}), bf16[128,8,128]{2,1,0:T(8,128)(2,1)S(1)}, u32[]{:S(2)}, u32[]{:S(2)}) async-start(bf16[128,8,128]{2,1,0:T(8,128)(2,1)} %bitcast.2), calls=%async_computation.3 | async-start | bytes 524288 | tf_op jit(solution)/shard_map/all_to_all | solution.py:386
  95.4 0.0 copy-start.1
  95.4 1.1 shard_map.74
  96.5 21.5 %all-to-all-done.3 = bf16[128,8,128]{2,1,0:T(8,128)(2,1)S(1)} async-done(((bf16[128,8,128]{2,1,0:T(8,128)(2,1)}), bf16[128,8,128]{2,1,0:T(8,128)(2,1)S(1)}, u32[]{:S(2)}, u32[]{:S(2)}) %all-to-all-start.3) | async-done | bytes 262176 | tf_op jit(solution)/shard_map/all_to_all | solution.py:386
  118.0 0.8 shard_map.73
  (7 shorter events, 0.1 us)
Async XLA Ops:
  2.6 12.9 %copy-start = (f32[16,64]{1,0:T(8,128)S(1)}, f32[16,64]{1,0:T(8,128)}, u32[]{:S(2)}) copy-start(f32[16,64]{1,0:T(8,128)} %stor.3) | copy-start | bytes 12292
  2.6 12.9 %collective-permute-start.1 = (bf16[272,128]{1,0:T(8,128)(2,1)S(1)}, bf16[272,128]{1,0:T(8,128)(2,1)S(1)}, u32[]{:S(2)}, u32[]{:S(2)}) collective-permute-start(bf16[272,128]{1,0:T(8,128)(2,1)S(1)} %get-tuple-element.24), channel_id=1, source_target_pairs={{4,8},{8,4},{12,16},{16,12},{20,24},{24,20},{28,32},{32,28},{36,40... | collective-permute-start | bytes 208904 | tf_op jit(solution)/shard_map/ppermute | solution.py:309
  7.5 7.9 %collective-permute-start.2 = (bf16[256,128]{1,0:T(8,128)(2,1)S(1)}, bf16[256,128]{1,0:T(8,128)(2,1)S(1)}, u32[]{:S(2)}, u32[]{:S(2)}) collective-permute-start(bf16[256,128]{1,0:T(8,128)(2,1)S(1)} %get-tuple-element.25), channel_id=1, source_target_pairs={{0,1},{1,0},{2,3},{3,2},{4,5},{5,4},{6,7},{7,6},{8,9},{9,8},{10,11... | collective-permute-start | bytes 196616 | tf_op jit(solution)/shard_map/ppermute | solution.py:310
  10.7 4.7 %collective-permute-start.3 = (bf16[256,128]{1,0:T(8,128)(2,1)S(1)}, bf16[256,128]{1,0:T(8,128)(2,1)S(1)}, u32[]{:S(2)}, u32[]{:S(2)}) collective-permute-start(bf16[256,128]{1,0:T(8,128)(2,1)S(1)} %get-tuple-element.26), channel_id=1, source_target_pairs={{1,2},{2,1},{5,6},{6,5},{9,10},{10,9},{13,14},{14,13},{17,18},{18,... | collective-permute-start | bytes 196616 | tf_op jit(solution)/shard_map/ppermute | solution.py:309
  11.4 4.1 %collective-permute-start = (bf16[64,128]{1,0:T(8,128)(2,1)S(1)}, bf16[64,128]{1,0:T(8,128)(2,1)S(1)}, u32[]{:S(2)}, u32[]{:S(2)}) collective-permute-start(bf16[64,128]{1,0:T(8,128)(2,1)S(1)} %get-tuple-element.23), channel_id=1, source_target_pairs={{0,4},{4,0},{8,12},{12,8},{16,20},{20,16},{24,28},{28,24},{32,36},... | collective-permute-start | bytes 49160 | tf_op jit(solution)/shard_map/ppermute | solution.py:310
  16.5 11.8 %collective-permute-start.5 = (bf16[272,128]{1,0:T(8,128)(2,1)S(1)}, bf16[272,128]{1,0:T(8,128)(2,1)S(1)}, u32[]{:S(2)}, u32[]{:S(2)}) collective-permute-start(bf16[272,128]{1,0:T(8,128)(2,1)S(1)} %get-tuple-element.30), channel_id=1, source_target_pairs={{4,8},{8,4},{12,16},{16,12},{20,24},{24,20},{28,32},{32,28},{36,40... | collective-permute-start | bytes 208904 | tf_op jit(solution)/shard_map/ppermute | solution.py:309
  19.1 9.2 %collective-permute-start.6 = (bf16[256,128]{1,0:T(8,128)(2,1)S(1)}, bf16[256,128]{1,0:T(8,128)(2,1)S(1)}, u32[]{:S(2)}, u32[]{:S(2)}) collective-permute-start(bf16[256,128]{1,0:T(8,128)(2,1)S(1)} %get-tuple-element.31), channel_id=1, source_target_pairs={{0,1},{1,0},{2,3},{3,2},{4,5},{5,4},{6,7},{7,6},{8,9},{9,8},{10,11... | collective-permute-start | bytes 196616 | tf_op jit(solution)/shard_map/ppermute | solution.py:310
  24.6 3.8 %collective-permute-start.7 = (bf16[256,128]{1,0:T(8,128)(2,1)S(1)}, bf16[256,128]{1,0:T(8,128)(2,1)S(1)}, u32[]{:S(2)}, u32[]{:S(2)}) collective-permute-start(bf16[256,128]{1,0:T(8,128)(2,1)S(1)} %get-tuple-element.32), channel_id=1, source_target_pairs={{1,2},{2,1},{5,6},{6,5},{9,10},{10,9},{13,14},{14,13},{17,18},{18,... | collective-permute-start | bytes 196616 | tf_op jit(solution)/shard_map/ppermute | solution.py:309
  25.2 3.1 %collective-permute-start.4 = (bf16[64,128]{1,0:T(8,128)(2,1)S(1)}, bf16[64,128]{1,0:T(8,128)(2,1)S(1)}, u32[]{:S(2)}, u32[]{:S(2)}) collective-permute-start(bf16[64,128]{1,0:T(8,128)(2,1)S(1)} %get-tuple-element.29), channel_id=1, source_target_pairs={{0,4},{4,0},{8,12},{12,8},{16,20},{20,16},{24,28},{28,24},{32,36},... | collective-permute-start | bytes 49160 | tf_op jit(solution)/shard_map/ppermute | solution.py:310
  71.2 5.4 %copy-start.2 = (s32[1,1024]{1,0:T(1,128)S(1)}, s32[1,1024]{1,0:T(1,128)}, u32[]{:S(2)}) copy-start(s32[1,1024]{1,0:T(1,128)} %order.1) | copy-start | bytes 12292
  71.2 12.8 %all-to-all-start.2 = ((f32[32,4,128]{2,1,0:T(4,128)}), f32[32,4,128]{2,1,0:T(4,128)S(1)}, u32[]{:S(2)}, u32[]{:S(2)}) async-start(f32[32,4,128]{2,1,0:T(4,128)} %broadcast_in_dim.5), calls=%async_computation.2 | async-start | bytes 131072 | tf_op jit(solution)/shard_map/all_to_all | solution.py:340
  89.8 28.1 %all-to-all-start.3 = ((bf16[128,8,128]{2,1,0:T(8,128)(2,1)}), bf16[128,8,128]{2,1,0:T(8,128)(2,1)S(1)}, u32[]{:S(2)}, u32[]{:S(2)}) async-start(bf16[128,8,128]{2,1,0:T(8,128)(2,1)} %bitcast.2), calls=%async_computation.3 | async-start | bytes 524288 | tf_op jit(solution)/shard_map/all_to_all | solution.py:386
  95.4 22.6 %copy-start.1 = (bf16[16,1024]{1,0:T(8,128)(2,1)S(1)}, bf16[16,1024]{1,0:T(8,128)(2,1)}, u32[]{:S(2)}) copy-start(bf16[16,1024]{1,0:T(8,128)(2,1)} %kriging.1) | copy-start | bytes 98308

commit v7 on v6

--- a/solution.py
+++ b/solution.py
@@ -197,6 +197,11 @@
 def diagonal(matrix):
     row, column = square_index()
     return jnp.sum(jnp.where(row == column, matrix, 0.0), axis=0, keepdims=True)
+
+
+def column_diagonal(matrix):
+    row, column = square_index()
+    return jnp.sum(jnp.where(row == column, matrix, 0.0), axis=1, keepdims=True)
 
 
 def unpack_pair(matrix, ends):
@@ -256,7 +261,7 @@
     return 0.5 * (matrix + jnp.transpose(matrix))
 
 
-def solve_kernel(packed, cells, heads, weights, later):
+def solve_kernel(cell_total, packed, cells, heads, scale, weights, later, rows):
     m0, m2 = unpack_pair(packed[:RHS, :RHS], packed[RHS : RHS + 1, RHS:])
     m1, m3 = unpack_pair(packed[:RHS, RHS:], packed[RHS + 1 : RHS + 2, RHS:])
     first = eliminate(jnp.concatenate([m1, m0, m2], axis=1))
@@ -266,10 +271,16 @@
     gamma = eliminate(jnp.concatenate([curved, target], axis=1))
     mixed = alpha - exact(shift, gamma)
     both = jnp.concatenate([mixed, gamma], axis=0)
-    high, rest = split(jnp.concatenate([both, both], axis=1))
+    spread = jnp.concatenate([column_diagonal(m0), column_diagonal(m2)], axis=0)
+    bound = jnp.sum(jnp.abs(both) * jnp.sqrt(spread * (1.0 / cell_total)), axis=0, keepdims=True)
+    bound = jnp.where(bound > 0.0, bound, 1.0)
+    scale[...] = bound
+    high, rest = split(jnp.concatenate([both / bound, both / bound], axis=1))
     value = dot3((cells[:, :LANE], cells[:, LANE:]), (high, rest), NN)
-    high = value.astype(BF16).astype(F32)
-    heads[...] = jnp.where(low_lanes(FX * LANE), high, value - high).astype(BF16)
+    rows[...] = value
+    half = FX * LANE // 2
+    even, odd = rows[pl.ds(0, half, stride=2), :], rows[pl.ds(1, half, stride=2), :]
+    heads[...] = jnp.where(low_lanes(half), even, odd)
     weights[...] = both
     later[...] = jnp.concatenate([m2, m3], axis=1)
 
@@ -280,9 +291,13 @@
     gram[...] = symmetric(exact(jnp.transpose(gamma), rest)) * (1.0 / cell_total)
 
 
-def product_kernel(kriging, arrived, sens):
-    product = dot(kriging[...], arrived[...], NN)
-    sens[...] = product[:, :RHS] + product[:, RHS:]
+def product_kernel(kriging, arrived, scale, sens, rows):
+    half = FX * LANE // 2
+    value = arrived[...].astype(F32)
+    rows[pl.ds(0, half, stride=2), :] = value
+    rows[pl.ds(1, half, stride=2), :] = swap(value)
+    high, rest = split(rows[...])
+    sens[...] = (dot(kriging[...], high, NN) + dot(kriging[...], rest, NN))[:, :RHS] * scale[...]
 
 
 def call(kernel, shapes, *operands, scratch=(), flops=1000000, place=pltpu.VMEM):
@@ -378,12 +393,14 @@
         flops=LONG,
     )
     packed = reduce_all(packed)
-    heads, weights, later = call(
-        solve_kernel,
-        (((FX * LANE, LANE), BF16), ((2 * RHS, RHS), F32), ((RHS, LANE), F32)),
+    heads, scale, weights, later = call(
+        lambda *refs: solve_kernel(cell_total, *refs),
+        (((FX * LANE // 2, LANE), F32), ((1, RHS), F32), ((2 * RHS, RHS), F32), ((RHS, LANE), F32)),
         *(packed, cells),
-    )
-    heads = lax.all_to_all(heads.reshape(groups, -1, LANE), "dom", 0, 0, tiled=True)
+        scratch=(scratch(FX * LANE),),
+    )
+    heads = heads.astype(jnp.float16).reshape(groups, -1, LANE)
+    heads = lax.all_to_all(heads, "dom", 0, 0, tiled=True).reshape(-1, LANE).astype(F32)
     (gram,) = call(
         lambda *refs: gram_kernel(cell_total, *refs),
         (((RHS, RHS), F32),),
@@ -393,7 +410,8 @@
     (sens,) = call(
         product_kernel,
         (((kriging.shape[0], RHS), F32),),
-        *(kriging, heads.reshape(-1, LANE)),
+        *(kriging, heads, scale),
+        scratch=(scratch(FX * LANE),),
     )
     return sens, gram
 

time: 119 us -> 115 us (0.966)
  waiting for transfers between devices: 29.2 us -> 24.1 us
    all_to_all x1, waiting for transfers between devices: 21.5 us -> 16.4 us  [shards(): lax.all_to_all(heads, 'dom', 0, 0, tiled=True).reshape(-1, LANE).astype(F32)]
where the time goes in v7:
time: 115 us
  blocking collectives  40.5 us (35%)
  starting transfers between devices  33.6 us (29%)
  waiting for transfers between devices  24.1 us (21%)
  Pallas kernels  13.4 us (12%)
  local copies, waits for them, and re-layouts  1.4 us (1%)
    all_to_all x2, blocking collectives, trade(): lax.all_to_all(array, axes, 0, 0, axis_index_groups=groups, tiled=True)  40.5 us
    all_to_all x1, waiting for transfers between devices, shards(): lax.all_to_all(heads, 'dom', 0, 0, tiled=True).reshape(-1, LANE).astype(F32)  16.4 us
    ppermute x4, starting transfers between devices, along(): return (lax.ppermute(one, axis, first), two)  13.8 us
    pallas_call x7, Pallas kernels, call(): pl.pallas_call(kernel, out_shape=[jax.ShapeDtypeStruct(shape, kind) for s...  13.4 us
    ppermute x4, starting transfers between devices, along(): two = lax.ppermute(two, axis, second)  8.88 us
    all_to_all x1, waiting for transfers between devices, trade(): lax.all_to_all(array, axes, 0, 0, axis_index_groups=groups, tiled=True)  5.78 us
    all_to_all x1, starting transfers between devices, shards(): lax.all_to_all(heads, 'dom', 0, 0, tiled=True).reshape(-1, LANE).astype(F32)  5.5 us
    all_to_all x1, starting transfers between devices, trade(): lax.all_to_all(array, axes, 0, 0, axis_index_groups=groups, tiled=True)  5.41 us
  transfers between devices with their start and end apart: 10, of which 4 were waited for; matrix products, arithmetic and copies ran while one was open for 0% of the time, Pallas kernels for 2%

profile of v7, /device:TPU:1, one launch (start us, length us, event | category | flops | bytes accessed | tf_op | source)
XLA Modules:
  0.0 114.6 jit_solution(16920347711579870576)
XLA Ops:
  0.6 1.9 %shard_map.68 = (f32[512,128]{1,0:T(8,128)S(1)}, bf16[1024,128]{1,0:T(8,128)(2,1)S(1)}, bf16[1024,128]{1,0:T(8,128)(2,1)S(1)}, f32[512,128]{1,0:T(8,128)S(1)}, b...) custom-call(f32[16,4096]{1,0:T(8,128)} %pump_hbm.1, ...), custom_call_target="tpu_custom_call" | custom-call | flops 1000000 | bytes 1048576 | tf_op jit(solution)/shard_map/pallas_call | solution.py:304
  2.6 0.0 copy-start
  2.6 4.9 %collective-permute-start.1 = (bf16[272,128]{1,0:T(8,128)(2,1)S(1)}, bf16[272,128]{1,0:T(8,128)(2,1)S(1)}, u32[]{:S(2)}, u32[]{:S(2)}) collective-permute-start(bf16[272,128]{1,0:T(8,128)(2,1)S(1)} %get-tuple-element.25), channel_id=1, source_target_pairs={{4,8},{8,4},{12,16},{16,12},{20,24},{24,20},{28,32},{32,28},{36,40... | collective-permute-start | bytes 208904 | tf_op jit(solution)/shard_map/ppermute | solution.py:324
  7.5 3.2 %collective-permute-start.2 = (bf16[256,128]{1,0:T(8,128)(2,1)S(1)}, bf16[256,128]{1,0:T(8,128)(2,1)S(1)}, u32[]{:S(2)}, u32[]{:S(2)}) collective-permute-start(bf16[256,128]{1,0:T(8,128)(2,1)S(1)} %get-tuple-element.26), channel_id=1, source_target_pairs={{0,1},{1,0},{2,3},{3,2},{4,5},{5,4},{6,7},{7,6},{8,9},{9,8},{10,11... | collective-permute-start | bytes 196616 | tf_op jit(solution)/shard_map/ppermute | solution.py:325
  10.7 0.7 collective-permute-start.3
  11.4 3.2 %collective-permute-start = (bf16[64,128]{1,0:T(8,128)(2,1)S(1)}, bf16[64,128]{1,0:T(8,128)(2,1)S(1)}, u32[]{:S(2)}, u32[]{:S(2)}) collective-permute-start(bf16[64,128]{1,0:T(8,128)(2,1)S(1)} %get-tuple-element.24), channel_id=1, source_target_pairs={{0,4},{4,0},{8,12},{12,8},{16,20},{20,16},{24,28},{28,24},{32,36},... | collective-permute-start | bytes 49160 | tf_op jit(solution)/shard_map/ppermute | solution.py:325
  14.6 0.8 collective-permute-done.d1
  15.5 0.0 collective-permute-done.2.t1
  15.5 0.0 collective-permute-done.3.t2
  15.5 0.0 collective-permute-done.1.d2
  15.5 1.0 shard_map.69
  16.5 2.6 %collective-permute-start.5 = (bf16[272,128]{1,0:T(8,128)(2,1)S(1)}, bf16[272,128]{1,0:T(8,128)(2,1)S(1)}, u32[]{:S(2)}, u32[]{:S(2)}) collective-permute-start(bf16[272,128]{1,0:T(8,128)(2,1)S(1)} %get-tuple-element.31), channel_id=1, source_target_pairs={{4,8},{8,4},{12,16},{16,12},{20,24},{24,20},{28,32},{32,28},{36,40... | collective-permute-start | bytes 208904 | tf_op jit(solution)/shard_map/ppermute | solution.py:324
  19.1 5.5 %collective-permute-start.6 = (bf16[256,128]{1,0:T(8,128)(2,1)S(1)}, bf16[256,128]{1,0:T(8,128)(2,1)S(1)}, u32[]{:S(2)}, u32[]{:S(2)}) collective-permute-start(bf16[256,128]{1,0:T(8,128)(2,1)S(1)} %get-tuple-element.32), channel_id=1, source_target_pairs={{0,1},{1,0},{2,3},{3,2},{4,5},{5,4},{6,7},{7,6},{8,9},{9,8},{10,11... | collective-permute-start | bytes 196616 | tf_op jit(solution)/shard_map/ppermute | solution.py:325
  24.6 0.7 collective-permute-start.7
  25.2 1.9 %collective-permute-start.4 = (bf16[64,128]{1,0:T(8,128)(2,1)S(1)}, bf16[64,128]{1,0:T(8,128)(2,1)S(1)}, u32[]{:S(2)}, u32[]{:S(2)}) collective-permute-start(bf16[64,128]{1,0:T(8,128)(2,1)S(1)} %get-tuple-element.30), channel_id=1, source_target_pairs={{0,4},{4,0},{8,12},{12,8},{16,20},{20,16},{24,28},{28,24},{32,36},... | collective-permute-start | bytes 49160 | tf_op jit(solution)/shard_map/ppermute | solution.py:325
  27.2 1.1 %collective-permute-done.4.d1 = bf16[64,128]{1,0:T(8,128)(2,1)S(1)} collective-permute-done((bf16[64,128]{1,0:T(8,128)(2,1)S(1)}, bf16[64,128]{1,0:T(8,128)(2,1)S(1)}, u32[]{:S(2)}, u32[]{:S(2)}) %collective-permute-start.4) | collective-permute-done | bytes 16416 | tf_op jit(solution)/shard_map/ppermute | solution.py:325
  28.3 0.0 collective-permute-done.6.t1
  28.3 0.0 collective-permute-done.7.t2
  28.3 1.7 %shard_map.70 = f32[128,128]{1,0:T(8,128)S(1)} custom-call(f32[512,128]{1,0:T(8,128)S(1)} %get-tuple-element.28.v.ap, f32[512,128]{1,0:T(8,128)S(1)} %get-tuple-element.29.u, bf16[1024,128]{1,0:T(8,128)(2,1)S(1)} %get-tuple-element.22.sh, bf16[1024,128]{1,0:T(8,128)(2,1)S(1)} %get-tuple-element.23.sl, f32[16,64]{1,0:T(8,128)S(1)} %copy-done, ...), custom_call_target="tpu_custom_call" | custom-call | flops 1000000 | bytes 1048576 | tf_op jit(solution)/shard_map/pallas_call | solution.py:304
  30.0 21.6 %all_to_all.20 = f32[32,4,128]{2,1,0:T(4,128)S(1)} all-to-all(f32[32,4,128]{2,1,0:T(4,128)S(1)} %bitcast.7), channel_id=1, replica_groups={{0,1,2,3,4,5,6,7,128,129,130,131,132,133,134,135,256,257,258,259,260,26..., dimensions={0} | all-to-all | bytes 131072 | tf_op jit(solution)/shard_map/all_to_all | solution.py:355
  51.7 18.9 %all_to_all.21 = f32[16,4,128]{2,1,0:T(4,128)S(1)} all-to-all(f32[16,4,128]{2,1,0:T(4,128)S(1)} %broadcast_in_dim.4), channel_id=1, replica_groups={{0,8,16,24,32,40,48,56,64,72,80,88,96,104,112,120},{1,9,17,25,33,41,49,..., dimensions={0} | all-to-all | bytes 65536 | tf_op jit(solution)/shard_map/all_to_all | solution.py:355
  70.6 0.6 broadcast_in_dim.5
  71.2 5.4 %all-to-all-start.2 = ((f32[32,4,128]{2,1,0:T(4,128)}), f32[32,4,128]{2,1,0:T(4,128)S(1)}, u32[]{:S(2)}, u32[]{:S(2)}) async-start(f32[32,4,128]{2,1,0:T(4,128)} %broadcast_in_dim.5), calls=%async_computation.2 | async-start | bytes 131072 | tf_op jit(solution)/shard_map/all_to_all | solution.py:355
  76.7 1.5 %shard_map.71.refs_1_ = bf16[1024,256]{1,0:T(8,128)(2,1)S(1)} custom-call(s32[1,1024]{1,0:T(1,128)S(1)} %copy-done.2, f32[512,128]{1,0:T(8,128)S(1)} %get-tuple-element.20.v.p, f32[512,128]{1,0:T(8,128)S(1)} %get-tuple-element.28.v.ap), custom_call_target="tpu_custom_call" | custom-call | flops 99999997952 | bytes 1048576 | tf_op jit(solution)/shard_map/pallas_call | solution.py:304
  78.2 5.8 %all-to-all-done.2 = f32[32,4,128]{2,1,0:T(4,128)S(1)} async-done(((f32[32,4,128]{2,1,0:T(4,128)}), f32[32,4,128]{2,1,0:T(4,128)S(1)}, u32[]{:S(2)}, u32[]{:S(2)}) %all-to-all-start.2) | async-done | bytes 65568 | tf_op jit(solution)/shard_map/all_to_all | solution.py:355
  84.0 5.2 %shard_map.72 = (f32[512,128]{1,0:T(8,128)S(1)}, f32[1,64]{1,0:T(1,128)S(1)}, f32[128,64]{1,0:T(8,128)S(1)}, f32[64,128]{1,0:T(8,128)S(1)}) custom-call(f32[128,128]{1,0:T(8,128)S(1)} %bitcast.5, bf16[1024,256]{1,0:T(8,128)(2,1)S(1)} %shard_map.71.refs_1_), custom_call_target="tpu_custom_call" | custom-call | flops 1000000 | bytes 1048576 | tf_op jit(solution)/shard_map/pallas_call | solution.py:304
  89.2 0.7 convert_element_type.8
  89.9 5.5 %all-to-all-start.3 = ((f16[128,4,128]{2,1,0:T(4,128)(2,1)}), f16[128,4,128]{2,1,0:T(4,128)(2,1)S(1)}, u32[]{:S(2)}, u32[]{:S(2)}) async-start(f16[128,4,128]{2,1,0:T(4,128)(2,1)} %bitcast.2), calls=%async_computation.3 | async-start | bytes 262144 | tf_op jit(solution)/shard_map/all_to_all | solution.py:403
  95.4 1.1 shard_map.74
  96.5 16.4 %all-to-all-done.3 = f16[128,4,128]{2,1,0:T(4,128)(2,1)S(1)} async-done(((f16[128,4,128]{2,1,0:T(4,128)(2,1)}), f16[128,4,128]{2,1,0:T(4,128)(2,1)S(1)}, u32[]{:S(2)}, u32[]{:S(2)}) %all-to-all-start.3) | async-done | bytes 131104 | tf_op jit(solution)/shard_map/all_to_all | solution.py:403
  112.9 0.7 copy-done.1
  113.7 0.9 shard_map.73
  (9 shorter events, 0.1 us)
Async XLA Ops:
  2.6 12.9 %copy-start = (f32[16,64]{1,0:T(8,128)S(1)}, f32[16,64]{1,0:T(8,128)}, u32[]{:S(2)}) copy-start(f32[16,64]{1,0:T(8,128)} %stor.3) | copy-start | bytes 12292
  2.6 12.9 %collective-permute-start.1 = (bf16[272,128]{1,0:T(8,128)(2,1)S(1)}, bf16[272,128]{1,0:T(8,128)(2,1)S(1)}, u32[]{:S(2)}, u32[]{:S(2)}) collective-permute-start(bf16[272,128]{1,0:T(8,128)(2,1)S(1)} %get-tuple-element.25), channel_id=1, source_target_pairs={{4,8},{8,4},{12,16},{16,12},{20,24},{24,20},{28,32},{32,28},{36,40... | collective-permute-start | bytes 208904 | tf_op jit(solution)/shard_map/ppermute | solution.py:324
  7.5 7.9 %collective-permute-start.2 = (bf16[256,128]{1,0:T(8,128)(2,1)S(1)}, bf16[256,128]{1,0:T(8,128)(2,1)S(1)}, u32[]{:S(2)}, u32[]{:S(2)}) collective-permute-start(bf16[256,128]{1,0:T(8,128)(2,1)S(1)} %get-tuple-element.26), channel_id=1, source_target_pairs={{0,1},{1,0},{2,3},{3,2},{4,5},{5,4},{6,7},{7,6},{8,9},{9,8},{10,11... | collective-permute-start | bytes 196616 | tf_op jit(solution)/shard_map/ppermute | solution.py:325
  10.7 4.7 %collective-permute-start.3 = (bf16[256,128]{1,0:T(8,128)(2,1)S(1)}, bf16[256,128]{1,0:T(8,128)(2,1)S(1)}, u32[]{:S(2)}, u32[]{:S(2)}) collective-permute-start(bf16[256,128]{1,0:T(8,128)(2,1)S(1)} %get-tuple-element.27), channel_id=1, source_target_pairs={{1,2},{2,1},{5,6},{6,5},{9,10},{10,9},{13,14},{14,13},{17,18},{18,... | collective-permute-start | bytes 196616 | tf_op jit(solution)/shard_map/ppermute | solution.py:324
  11.4 4.1 %collective-permute-start = (bf16[64,128]{1,0:T(8,128)(2,1)S(1)}, bf16[64,128]{1,0:T(8,128)(2,1)S(1)}, u32[]{:S(2)}, u32[]{:S(2)}) collective-permute-start(bf16[64,128]{1,0:T(8,128)(2,1)S(1)} %get-tuple-element.24), channel_id=1, source_target_pairs={{0,4},{4,0},{8,12},{12,8},{16,20},{20,16},{24,28},{28,24},{32,36},... | collective-permute-start | bytes 49160 | tf_op jit(solution)/shard_map/ppermute | solution.py:325
  16.5 11.8 %collective-permute-start.5 = (bf16[272,128]{1,0:T(8,128)(2,1)S(1)}, bf16[272,128]{1,0:T(8,128)(2,1)S(1)}, u32[]{:S(2)}, u32[]{:S(2)}) collective-permute-start(bf16[272,128]{1,0:T(8,128)(2,1)S(1)} %get-tuple-element.31), channel_id=1, source_target_pairs={{4,8},{8,4},{12,16},{16,12},{20,24},{24,20},{28,32},{32,28},{36,40... | collective-permute-start | bytes 208904 | tf_op jit(solution)/shard_map/ppermute | solution.py:324
  19.1 9.2 %collective-permute-start.6 = (bf16[256,128]{1,0:T(8,128)(2,1)S(1)}, bf16[256,128]{1,0:T(8,128)(2,1)S(1)}, u32[]{:S(2)}, u32[]{:S(2)}) collective-permute-start(bf16[256,128]{1,0:T(8,128)(2,1)S(1)} %get-tuple-element.32), channel_id=1, source_target_pairs={{0,1},{1,0},{2,3},{3,2},{4,5},{5,4},{6,7},{7,6},{8,9},{9,8},{10,11... | collective-permute-start | bytes 196616 | tf_op jit(solution)/shard_map/ppermute | solution.py:325
  24.6 3.8 %collective-permute-start.7 = (bf16[256,128]{1,0:T(8,128)(2,1)S(1)}, bf16[256,128]{1,0:T(8,128)(2,1)S(1)}, u32[]{:S(2)}, u32[]{:S(2)}) collective-permute-start(bf16[256,128]{1,0:T(8,128)(2,1)S(1)} %get-tuple-element.33), channel_id=1, source_target_pairs={{1,2},{2,1},{5,6},{6,5},{9,10},{10,9},{13,14},{14,13},{17,18},{18,... | collective-permute-start | bytes 196616 | tf_op jit(solution)/shard_map/ppermute | solution.py:324
  25.2 3.1 %collective-permute-start.4 = (bf16[64,128]{1,0:T(8,128)(2,1)S(1)}, bf16[64,128]{1,0:T(8,128)(2,1)S(1)}, u32[]{:S(2)}, u32[]{:S(2)}) collective-permute-start(bf16[64,128]{1,0:T(8,128)(2,1)S(1)} %get-tuple-element.30), channel_id=1, source_target_pairs={{0,4},{4,0},{8,12},{12,8},{16,20},{20,16},{24,28},{28,24},{32,36},... | collective-permute-start | bytes 49160 | tf_op jit(solution)/shard_map/ppermute | solution.py:325
  71.2 5.4 %copy-start.2 = (s32[1,1024]{1,0:T(1,128)S(1)}, s32[1,1024]{1,0:T(1,128)}, u32[]{:S(2)}) copy-start(s32[1,1024]{1,0:T(1,128)} %order.1) | copy-start | bytes 12292
  71.2 12.8 %all-to-all-start.2 = ((f32[32,4,128]{2,1,0:T(4,128)}), f32[32,4,128]{2,1,0:T(4,128)S(1)}, u32[]{:S(2)}, u32[]{:S(2)}) async-start(f32[32,4,128]{2,1,0:T(4,128)} %broadcast_in_dim.5), calls=%async_computation.2 | async-start | bytes 131072 | tf_op jit(solution)/shard_map/all_to_all | solution.py:355
  89.9 23.0 %all-to-all-start.3 = ((f16[128,4,128]{2,1,0:T(4,128)(2,1)}), f16[128,4,128]{2,1,0:T(4,128)(2,1)S(1)}, u32[]{:S(2)}, u32[]{:S(2)}) async-start(f16[128,4,128]{2,1,0:T(4,128)(2,1)} %bitcast.2), calls=%async_computation.3 | async-start | bytes 262144 | tf_op jit(solution)/shard_map/all_to_all | solution.py:403
  112.9 0.8 copy-start.1

commit v8 on v7

--- a/solution.py
+++ b/solution.py
@@ -77,20 +77,19 @@
 
 def first_kernel(pump_hbm, coup_hbm, p_out, sh_out, sl_out, u_out, d1, d2, t1, t2, pump, coup, rows_p, rows_s, mats, arrived):
     copies = []
-    for i in range(PIECES):
-        columns = pl.ds(i * WIDTH, WIDTH)
-        for j, (source, target) in enumerate(((coup_hbm, coup), (pump_hbm, pump))):
+    for source, target, order in ((pump_hbm, pump, 0), (coup_hbm, coup, 1)):
+        for i in range(PIECES):
+            columns = pl.ds(i * WIDTH, WIDTH)
             copies.append(
-                pltpu.make_async_copy(source.at[:, columns], target.at[:, columns], arrived.at[j, i])
+                pltpu.make_async_copy(source.at[:, columns], target.at[:, columns], arrived.at[order, i])
             )
-    for copy in copies:
-        copy.start()
-    for copy in copies:
+            copies[-1].start()
+    for i, copy in enumerate(copies):
+        source, target = (pump, rows_p) if i < PIECES else (coup, rows_s)
         copy.wait()
-    for k in range(RHS // 2):
-        chunk = slice(k * LANE, (k + 1) * LANE)
-        rows_p[pl.ds(k, 16, stride=32), :] = pump[:, chunk]
-        rows_s[pl.ds(k, 16, stride=32), :] = coup[:, chunk]
+        chunks = WIDTH // LANE
+        for k in range(i % PIECES * chunks, (i % PIECES + 1) * chunks):
+            target[pl.ds(k, 16, stride=32), :] = source[:, k * LANE : (k + 1) * LANE]
     low = low_lanes(32)
     zero = jnp.zeros((32, LANE), F32)
     for x in range(FX):
@@ -169,20 +168,25 @@
         ).astype(BF16)
 
 
-def third_kernel(v, u, sh, sl, stor, d1, d2, t1, t2, p, packed):
+def base_kernel(p, v, base):
+    total = jnp.zeros((2 * RHS, 2 * RHS), F32)
+    for x in range(FX):
+        both = split(jnp.concatenate([p[part(x), :], v[part(x), :]], axis=0))
+        total += dot3(both, both, NT)
+    base[...] = total
+
+
+def third_kernel(v, u, sh, sl, stor, d1, d2, t1, t2, base, packed):
     applied = operator(v, u, sh, sl, stor, d1, d2, t1, t2)
-    base = jnp.zeros((2 * RHS, 2 * RHS), F32)
     total = jnp.zeros((2 * RHS, RHS), F32)
     for x in range(FX):
-        low, image = split(jnp.concatenate([p[part(x), :], v[part(x), :]], axis=0)), split(applied[x])
-        base += dot3(low, low, NT)
-        both = [jnp.concatenate([a[RHS:], b], axis=0) for a, b in zip(low, image)]
+        image = split(applied[x])
+        both = [jnp.concatenate([a, b], axis=0) for a, b in zip(split(v[part(x), :]), image)]
         total += dot3(both, image, NT)
-    m0 = symmetric(base[:RHS, :RHS])
-    m1 = 0.5 * (base[:RHS, RHS:] + base[RHS:, :RHS])
-    m2 = symmetric(base[RHS:, RHS:])
+    m0, m1, m2 = base[:RHS, :RHS], base[:RHS, RHS:], base[RHS:, RHS:]
+    m1 = symmetric(m1)
     m3 = symmetric(total[:RHS])
-    m4 = symmetric(total[RHS:])
+    m4 = total[RHS:]
     row, column = square_index()
     upper = row <= column
     packed[:RHS, :] = jnp.concatenate([jnp.where(upper, m0, m2), jnp.where(upper, m1, m3)], axis=1)
@@ -285,7 +289,8 @@
     later[...] = jnp.concatenate([m2, m3], axis=1)
 
 
-def gram_kernel(cell_total, packed, weights, later, gram):
+def gram_kernel(cell_total, packed, weights, later, kriging, gram, kept):
+    kept[...] = kriging[...]
     mixed, gamma = weights[:RHS, :], weights[RHS:, :]
     rest = exact(packed[RHS:, :RHS], gamma) + exact(later[:, RHS:], mixed) - later[:, :RHS]
     gram[...] = symmetric(exact(jnp.transpose(gamma), rest)) * (1.0 / cell_total)
@@ -382,8 +387,9 @@
     halo = exchange(*edges)
     ap, u, *edges = call(second_kernel, (FIELD, FIELD) + EDGES, p, u, sh, sl, storage, *halo)
     halo = exchange(*edges)
+    (base,) = call(base_kernel, (((2 * RHS, LANE), F32),), p, ap)
     (packed,) = call(
-        third_kernel, (((2 * RHS, LANE), F32),), ap, u, sh, sl, storage, *halo, p
+        third_kernel, (((2 * RHS, LANE), F32),), ap, u, sh, sl, storage, *halo, base
     )
     (cells,) = call(
         deal_kernel,
@@ -401,10 +407,10 @@
     )
     heads = heads.astype(jnp.float16).reshape(groups, -1, LANE)
     heads = lax.all_to_all(heads, "dom", 0, 0, tiled=True).reshape(-1, LANE).astype(F32)
-    (gram,) = call(
+    gram, kriging = call(
         lambda *refs: gram_kernel(cell_total, *refs),
-        (((RHS, RHS), F32),),
-        *(packed, weights, later),
+        (((RHS, RHS), F32), (kriging.shape, BF16)),
+        *(packed, weights, later, kriging),
         flops=LONG,
     )
     (sens,) = call(

time: 115 us -> 114 us (level)
    pallas_call x7 -> x8, Pallas kernels: 13.4 us -> 13.5 us  [call(): pl.pallas_call(kernel, out_shape=[jax.ShapeDtypeStruct(shape, kind) for s...]
  transfers between devices with their start and end apart: 10 -> 10, of which waited for: 4 -> 4; matrix products, arithmetic and copies ran while one was open for 0% -> 0% of each run, Pallas kernels for 2% -> 3%
where the time goes in v8:
time: 114 us; the launch traced here: 113 us
  blocking collectives  40.5 us (36%)
  starting transfers between devices  33.7 us (30%)
  waiting for transfers between devices  23.4 us (21%)
  Pallas kernels  13.5 us (12%)
    all_to_all x2, blocking collectives, trade(): lax.all_to_all(array, axes, 0, 0, axis_index_groups=groups, tiled=True)  40.5 us
    all_to_all x1, waiting for transfers between devices, shards(): lax.all_to_all(heads, 'dom', 0, 0, tiled=True).reshape(-1, LANE).astype(F32)  16.4 us
    ppermute x4, starting transfers between devices, along(): return (lax.ppermute(one, axis, first), two)  13.8 us
    pallas_call x8, Pallas kernels, call(): pl.pallas_call(kernel, out_shape=[jax.ShapeDtypeStruct(shape, kind) for s...  13.5 us
    ppermute x4, starting transfers between devices, along(): two = lax.ppermute(two, axis, second)  8.88 us
    all_to_all x1, waiting for transfers between devices, trade(): lax.all_to_all(array, axes, 0, 0, axis_index_groups=groups, tiled=True)  5.77 us
    all_to_all x1, starting transfers between devices, shards(): lax.all_to_all(heads, 'dom', 0, 0, tiled=True).reshape(-1, LANE).astype(F32)  5.64 us
    all_to_all x1, starting transfers between devices, trade(): lax.all_to_all(array, axes, 0, 0, axis_index_groups=groups, tiled=True)  5.41 us
  transfers between devices with their start and end apart: 10, of which 4 were waited for; matrix products, arithmetic and copies ran while one was open for 0% of the time, Pallas kernels for 3%

profile of v8, /device:TPU:1, one launch (start us, length us, event | category | flops | bytes accessed | tf_op | source)
XLA Modules:
  0.0 113.4 jit_solution(360913818631229386)
XLA Ops:
  0.6 1.9 %shard_map.68 = (f32[512,128]{1,0:T(8,128)S(1)}, bf16[1024,128]{1,0:T(8,128)(2,1)S(1)}, bf16[1024,128]{1,0:T(8,128)(2,1)S(1)}, f32[512,128]{1,0:T(8,128)S(1)}, b...) custom-call(f32[16,4096]{1,0:T(8,128)} %pump_hbm.1, ...), custom_call_target="tpu_custom_call" | custom-call | flops 1000000 | bytes 1048576 | tf_op jit(solution)/shard_map/pallas_call | solution.py:309
  2.5 0.0 copy-start
  2.5 4.9 %collective-permute-start.1 = (bf16[272,128]{1,0:T(8,128)(2,1)S(1)}, bf16[272,128]{1,0:T(8,128)(2,1)S(1)}, u32[]{:S(2)}, u32[]{:S(2)}) collective-permute-start(bf16[272,128]{1,0:T(8,128)(2,1)S(1)} %get-tuple-element.27), channel_id=1, source_target_pairs={{4,8},{8,4},{12,16},{16,12},{20,24},{24,20},{28,32},{32,28},{36,40... | collective-permute-start | bytes 208904 | tf_op jit(solution)/shard_map/ppermute | solution.py:329
  7.5 3.2 %collective-permute-start.2 = (bf16[256,128]{1,0:T(8,128)(2,1)S(1)}, bf16[256,128]{1,0:T(8,128)(2,1)S(1)}, u32[]{:S(2)}, u32[]{:S(2)}) collective-permute-start(bf16[256,128]{1,0:T(8,128)(2,1)S(1)} %get-tuple-element.28), channel_id=1, source_target_pairs={{0,1},{1,0},{2,3},{3,2},{4,5},{5,4},{6,7},{7,6},{8,9},{9,8},{10,11... | collective-permute-start | bytes 196616 | tf_op jit(solution)/shard_map/ppermute | solution.py:330
  10.7 0.7 collective-permute-start.3
  11.3 3.2 %collective-permute-start = (bf16[64,128]{1,0:T(8,128)(2,1)S(1)}, bf16[64,128]{1,0:T(8,128)(2,1)S(1)}, u32[]{:S(2)}, u32[]{:S(2)}) collective-permute-start(bf16[64,128]{1,0:T(8,128)(2,1)S(1)} %get-tuple-element.26), channel_id=1, source_target_pairs={{0,4},{4,0},{8,12},{12,8},{16,20},{20,16},{24,28},{28,24},{32,36},... | collective-permute-start | bytes 49160 | tf_op jit(solution)/shard_map/ppermute | solution.py:330
  14.6 0.8 collective-permute-done.d1
  15.4 0.0 collective-permute-done.2.t1
  15.4 0.0 collective-permute-done.1.d2
  15.4 1.0 shard_map.69
  16.4 2.6 %collective-permute-start.5 = (bf16[272,128]{1,0:T(8,128)(2,1)S(1)}, bf16[272,128]{1,0:T(8,128)(2,1)S(1)}, u32[]{:S(2)}, u32[]{:S(2)}) collective-permute-start(bf16[272,128]{1,0:T(8,128)(2,1)S(1)} %get-tuple-element.33), channel_id=1, source_target_pairs={{4,8},{8,4},{12,16},{16,12},{20,24},{24,20},{28,32},{32,28},{36,40... | collective-permute-start | bytes 208904 | tf_op jit(solution)/shard_map/ppermute | solution.py:329
  19.1 5.5 %collective-permute-start.6 = (bf16[256,128]{1,0:T(8,128)(2,1)S(1)}, bf16[256,128]{1,0:T(8,128)(2,1)S(1)}, u32[]{:S(2)}, u32[]{:S(2)}) collective-permute-start(bf16[256,128]{1,0:T(8,128)(2,1)S(1)} %get-tuple-element.34), channel_id=1, source_target_pairs={{0,1},{1,0},{2,3},{3,2},{4,5},{5,4},{6,7},{7,6},{8,9},{9,8},{10,11... | collective-permute-start | bytes 196616 | tf_op jit(solution)/shard_map/ppermute | solution.py:330
  24.5 0.7 collective-permute-start.7
  25.2 1.9 %collective-permute-start.4 = (bf16[64,128]{1,0:T(8,128)(2,1)S(1)}, bf16[64,128]{1,0:T(8,128)(2,1)S(1)}, u32[]{:S(2)}, u32[]{:S(2)}) collective-permute-start(bf16[64,128]{1,0:T(8,128)(2,1)S(1)} %get-tuple-element.32), channel_id=1, source_target_pairs={{0,4},{4,0},{8,12},{12,8},{16,20},{20,16},{24,28},{28,24},{32,36},... | collective-permute-start | bytes 49160 | tf_op jit(solution)/shard_map/ppermute | solution.py:330
  27.1 0.7 shard_map.70.base
  27.8 0.5 collective-permute-done.4.d1
  28.3 0.0 collective-permute-done.6.t1
  28.3 0.0 collective-permute-done.7.t2
  28.3 0.0 collective-permute-done.5.d2
  28.3 1.2 %shard_map.71 = f32[128,128]{1,0:T(8,128)S(1)} custom-call(f32[512,128]{1,0:T(8,128)S(1)} %get-tuple-element.30.v.ap, f32[512,128]{1,0:T(8,128)S(1)} %get-tuple-element.31.u, bf16[1024,128]{1,0:T(8,128)(2,1)S(1)} %get-tuple-element.24.sh, bf16[1024,128]{1,0:T(8,128)(2,1)S(1)} %get-tuple-element.25.sl, f32[16,64]{1,0:T(8,128)S(1)} %copy-done, ...), custom_call_target="tpu_custom_call" | custom-call | flops 1000000 | bytes 1048576 | tf_op jit(solution)/shard_map/pallas_call | solution.py:309
  29.5 21.6 %all_to_all.20 = f32[32,4,128]{2,1,0:T(4,128)S(1)} all-to-all(f32[32,4,128]{2,1,0:T(4,128)S(1)} %bitcast.7), channel_id=1, replica_groups={{0,1,2,3,4,5,6,7,128,129,130,131,132,133,134,135,256,257,258,259,260,26..., dimensions={0} | all-to-all | bytes 131072 | tf_op jit(solution)/shard_map/all_to_all | solution.py:360
  51.1 18.9 %all_to_all.21 = f32[16,4,128]{2,1,0:T(4,128)S(1)} all-to-all(f32[16,4,128]{2,1,0:T(4,128)S(1)} %broadcast_in_dim.4), channel_id=1, replica_groups={{0,8,16,24,32,40,48,56,64,72,80,88,96,104,112,120},{1,9,17,25,33,41,49,..., dimensions={0} | all-to-all | bytes 65536 | tf_op jit(solution)/shard_map/all_to_all | solution.py:360
  70.0 0.6 broadcast_in_dim.5
  70.7 5.4 %all-to-all-start.2 = ((f32[32,4,128]{2,1,0:T(4,128)}), f32[32,4,128]{2,1,0:T(4,128)S(1)}, u32[]{:S(2)}, u32[]{:S(2)}) async-start(f32[32,4,128]{2,1,0:T(4,128)} %broadcast_in_dim.5), calls=%async_computation.2 | async-start | bytes 131072 | tf_op jit(solution)/shard_map/all_to_all | solution.py:360
  76.1 1.5 %shard_map.72.refs_1_ = bf16[1024,256]{1,0:T(8,128)(2,1)S(1)} custom-call(s32[1,1024]{1,0:T(1,128)S(1)} %copy-done.2, f32[512,128]{1,0:T(8,128)S(1)} %get-tuple-element.22.v.p, f32[512,128]{1,0:T(8,128)S(1)} %get-tuple-element.30.v.ap), custom_call_target="tpu_custom_call" | custom-call | flops 99999997952 | bytes 1048576 | tf_op jit(solution)/shard_map/pallas_call | solution.py:309
  77.6 5.8 %all-to-all-done.2 = f32[32,4,128]{2,1,0:T(4,128)S(1)} async-done(((f32[32,4,128]{2,1,0:T(4,128)}), f32[32,4,128]{2,1,0:T(4,128)S(1)}, u32[]{:S(2)}, u32[]{:S(2)}) %all-to-all-start.2) | async-done | bytes 65568 | tf_op jit(solution)/shard_map/all_to_all | solution.py:360
  83.4 5.2 %shard_map.73 = (f32[512,128]{1,0:T(8,128)S(1)}, f32[1,64]{1,0:T(1,128)S(1)}, f32[128,64]{1,0:T(8,128)S(1)}, f32[64,128]{1,0:T(8,128)S(1)}) custom-call(f32[128,128]{1,0:T(8,128)S(1)} %bitcast.5, bf16[1024,256]{1,0:T(8,128)(2,1)S(1)} %shard_map.72.refs_1_), custom_call_target="tpu_custom_call" | custom-call | flops 1000000 | bytes 1048576 | tf_op jit(solution)/shard_map/pallas_call | solution.py:309
  88.6 0.7 convert_element_type.8
  89.3 5.6 %all-to-all-start.3 = ((f16[128,4,128]{2,1,0:T(4,128)(2,1)}), f16[128,4,128]{2,1,0:T(4,128)(2,1)S(1)}, u32[]{:S(2)}, u32[]{:S(2)}) async-start(f16[128,4,128]{2,1,0:T(4,128)(2,1)} %bitcast.2), calls=%async_computation.3 | async-start | bytes 262144 | tf_op jit(solution)/shard_map/all_to_all | solution.py:409
  95.0 1.1 %shard_map.74 = (f32[64,64]{1,0:T(8,128)}, bf16[16,1024]{1,0:T(8,128)(2,1)S(1)}) custom-call(f32[128,128]{1,0:T(8,128)S(1)} %bitcast.6, f32[128,64]{1,0:T(8,128)S(1)} %get-tuple-element.36.refs_1_, f32[64,128]{1,0:T(8,128)S(1)} %get-tuple-element.37.refs_2_, bf16[16,1024]{1,0:T(8,128)(2,1)S(1)} %copy-done.1), custom_call_target="tpu_custom_call" | custom-call | flops 99999997952 | bytes 1048576 | tf_op jit(solution)/shard_map/pallas_call | solution.py:309
  96.1 16.4 %all-to-all-done.3 = f16[128,4,128]{2,1,0:T(4,128)(2,1)S(1)} async-done(((f16[128,4,128]{2,1,0:T(4,128)(2,1)}), f16[128,4,128]{2,1,0:T(4,128)(2,1)S(1)}, u32[]{:S(2)}, u32[]{:S(2)}) %all-to-all-start.3) | async-done | bytes 131104 | tf_op jit(solution)/shard_map/all_to_all | solution.py:409
  112.5 0.9 shard_map.75
  (10 shorter events, 0.1 us)
Async XLA Ops:
  2.5 12.9 %copy-start = (f32[16,64]{1,0:T(8,128)S(1)}, f32[16,64]{1,0:T(8,128)}, u32[]{:S(2)}) copy-start(f32[16,64]{1,0:T(8,128)} %stor.3) | copy-start | bytes 12292
  2.5 12.9 %collective-permute-start.1 = (bf16[272,128]{1,0:T(8,128)(2,1)S(1)}, bf16[272,128]{1,0:T(8,128)(2,1)S(1)}, u32[]{:S(2)}, u32[]{:S(2)}) collective-permute-start(bf16[272,128]{1,0:T(8,128)(2,1)S(1)} %get-tuple-element.27), channel_id=1, source_target_pairs={{4,8},{8,4},{12,16},{16,12},{20,24},{24,20},{28,32},{32,28},{36,40... | collective-permute-start | bytes 208904 | tf_op jit(solution)/shard_map/ppermute | solution.py:329
  7.5 7.9 %collective-permute-start.2 = (bf16[256,128]{1,0:T(8,128)(2,1)S(1)}, bf16[256,128]{1,0:T(8,128)(2,1)S(1)}, u32[]{:S(2)}, u32[]{:S(2)}) collective-permute-start(bf16[256,128]{1,0:T(8,128)(2,1)S(1)} %get-tuple-element.28), channel_id=1, source_target_pairs={{0,1},{1,0},{2,3},{3,2},{4,5},{5,4},{6,7},{7,6},{8,9},{9,8},{10,11... | collective-permute-start | bytes 196616 | tf_op jit(solution)/shard_map/ppermute | solution.py:330
  10.7 4.7 %collective-permute-start.3 = (bf16[256,128]{1,0:T(8,128)(2,1)S(1)}, bf16[256,128]{1,0:T(8,128)(2,1)S(1)}, u32[]{:S(2)}, u32[]{:S(2)}) collective-permute-start(bf16[256,128]{1,0:T(8,128)(2,1)S(1)} %get-tuple-element.29), channel_id=1, source_target_pairs={{1,2},{2,1},{5,6},{6,5},{9,10},{10,9},{13,14},{14,13},{17,18},{18,... | collective-permute-start | bytes 196616 | tf_op jit(solution)/shard_map/ppermute | solution.py:329
  11.3 4.1 %collective-permute-start = (bf16[64,128]{1,0:T(8,128)(2,1)S(1)}, bf16[64,128]{1,0:T(8,128)(2,1)S(1)}, u32[]{:S(2)}, u32[]{:S(2)}) collective-permute-start(bf16[64,128]{1,0:T(8,128)(2,1)S(1)} %get-tuple-element.26), channel_id=1, source_target_pairs={{0,4},{4,0},{8,12},{12,8},{16,20},{20,16},{24,28},{28,24},{32,36},... | collective-permute-start | bytes 49160 | tf_op jit(solution)/shard_map/ppermute | solution.py:330
  16.4 11.8 %collective-permute-start.5 = (bf16[272,128]{1,0:T(8,128)(2,1)S(1)}, bf16[272,128]{1,0:T(8,128)(2,1)S(1)}, u32[]{:S(2)}, u32[]{:S(2)}) collective-permute-start(bf16[272,128]{1,0:T(8,128)(2,1)S(1)} %get-tuple-element.33), channel_id=1, source_target_pairs={{4,8},{8,4},{12,16},{16,12},{20,24},{24,20},{28,32},{32,28},{36,40... | collective-permute-start | bytes 208904 | tf_op jit(solution)/shard_map/ppermute | solution.py:329
  19.1 9.2 %collective-permute-start.6 = (bf16[256,128]{1,0:T(8,128)(2,1)S(1)}, bf16[256,128]{1,0:T(8,128)(2,1)S(1)}, u32[]{:S(2)}, u32[]{:S(2)}) collective-permute-start(bf16[256,128]{1,0:T(8,128)(2,1)S(1)} %get-tuple-element.34), channel_id=1, source_target_pairs={{0,1},{1,0},{2,3},{3,2},{4,5},{5,4},{6,7},{7,6},{8,9},{9,8},{10,11... | collective-permute-start | bytes 196616 | tf_op jit(solution)/shard_map/ppermute | solution.py:330
  24.5 3.8 %collective-permute-start.7 = (bf16[256,128]{1,0:T(8,128)(2,1)S(1)}, bf16[256,128]{1,0:T(8,128)(2,1)S(1)}, u32[]{:S(2)}, u32[]{:S(2)}) collective-permute-start(bf16[256,128]{1,0:T(8,128)(2,1)S(1)} %get-tuple-element.35), channel_id=1, source_target_pairs={{1,2},{2,1},{5,6},{6,5},{9,10},{10,9},{13,14},{14,13},{17,18},{18,... | collective-permute-start | bytes 196616 | tf_op jit(solution)/shard_map/ppermute | solution.py:329
  25.2 3.1 %collective-permute-start.4 = (bf16[64,128]{1,0:T(8,128)(2,1)S(1)}, bf16[64,128]{1,0:T(8,128)(2,1)S(1)}, u32[]{:S(2)}, u32[]{:S(2)}) collective-permute-start(bf16[64,128]{1,0:T(8,128)(2,1)S(1)} %get-tuple-element.32), channel_id=1, source_target_pairs={{0,4},{4,0},{8,12},{12,8},{16,20},{20,16},{24,28},{28,24},{32,36},... | collective-permute-start | bytes 49160 | tf_op jit(solution)/shard_map/ppermute | solution.py:330
  70.7 5.4 %copy-start.2 = (s32[1,1024]{1,0:T(1,128)S(1)}, s32[1,1024]{1,0:T(1,128)}, u32[]{:S(2)}) copy-start(s32[1,1024]{1,0:T(1,128)} %order.1) | copy-start | bytes 12292
  70.7 12.8 %all-to-all-start.2 = ((f32[32,4,128]{2,1,0:T(4,128)}), f32[32,4,128]{2,1,0:T(4,128)S(1)}, u32[]{:S(2)}, u32[]{:S(2)}) async-start(f32[32,4,128]{2,1,0:T(4,128)} %broadcast_in_dim.5), calls=%async_computation.2 | async-start | bytes 131072 | tf_op jit(solution)/shard_map/all_to_all | solution.py:360
  89.3 5.7 %copy-start.1 = (bf16[16,1024]{1,0:T(8,128)(2,1)S(1)}, bf16[16,1024]{1,0:T(8,128)(2,1)}, u32[]{:S(2)}) copy-start(bf16[16,1024]{1,0:T(8,128)(2,1)} %refs_3_.1) | copy-start | bytes 98308
  89.3 23.2 %all-to-all-start.3 = ((f16[128,4,128]{2,1,0:T(4,128)(2,1)}), f16[128,4,128]{2,1,0:T(4,128)(2,1)S(1)}, u32[]{:S(2)}, u32[]{:S(2)}) async-start(f16[128,4,128]{2,1,0:T(4,128)(2,1)} %bitcast.2), calls=%async_computation.3 | async-start | bytes 262144 | tf_op jit(solution)/shard_map/all_to_all | solution.py:409

commit v9 on v8

--- a/solution.py
+++ b/solution.py
@@ -8,6 +8,7 @@
 RHS = 64
 CB = 64
 FX = 8
+N_TILE = 4
 LANE = 128
 ROWS = FX * RHS
 F32 = jnp.float32
@@ -60,22 +61,26 @@
     return jnp.where(even, first, second), jnp.where(even, second, first)
 
 
-def write_edges(spread, d1, d2, t1, t2):
+def slot(step):
+    index = lax.rem(lax.axis_index("tile") + step, N_TILE)
+    return pl.multiple_of(index * (ROWS // 2), ROWS // 2)
+
+
+def write_edges(spread, d1, d2, t):
     low = low_lanes(RHS)
     one, two = by_parity("dom", spread[FX - 1], spread[0])
     d1[...] = one.astype(BF16)
     d2[:RHS, :] = two.astype(BF16)
     d2[RHS:, :] = jnp.zeros((d2.shape[0] - RHS, LANE), BF16)
+    for step in (0, 2):
+        t[pl.ds(slot(step), ROWS // 2), :] = jnp.zeros((ROWS // 2, LANE), BF16)
     for i in range(FX // 2):
         even, odd = spread[2 * i], spread[2 * i + 1]
-        left = jnp.where(low, even, swap(odd))
-        right = jnp.where(low, swap(even), odd)
-        one, two = by_parity("tile", right, left)
-        t1[part(i), :] = one.astype(BF16)
-        t2[part(i), :] = two.astype(BF16)
-
-
-def first_kernel(pump_hbm, coup_hbm, p_out, sh_out, sl_out, u_out, d1, d2, t1, t2, pump, coup, rows_p, rows_s, mats, arrived):
+        t[pl.ds(slot(1) + i * RHS, RHS), :] = jnp.where(low, swap(even), odd).astype(BF16)
+        t[pl.ds(slot(3) + i * RHS, RHS), :] = jnp.where(low, even, swap(odd)).astype(BF16)
+
+
+def first_kernel(pump_hbm, coup_hbm, p_out, sh_out, sl_out, u_out, d1, d2, t, pump, coup, rows_p, rows_s, mats, arrived):
     copies = []
     for source, target, order in ((pump_hbm, pump, 0), (coup_hbm, coup, 1)):
         for i in range(PIECES):
@@ -110,19 +115,21 @@
         u = dot3(split(p_out[part(x), :]), (high, rest), NN)
         u_out[part(x), :] = u
         spread.append(u)
-    write_edges(spread, d1, d2, t1, t2)
-
-
-def operator(v, u, sh, sl, stor, d1, d2, t1, t2):
+    write_edges(spread, d1, d2, t)
+
+
+def operator(v, u, sh, sl, stor, d1, d2, t):
     low = low_lanes(RHS)
     spread = [u[part(x), :] for x in range(FX)]
     after, before = by_parity("dom", d1[...].astype(F32), d2[:RHS, :].astype(F32))
     ends = [before] + spread + [after]
     right, left = [], []
     for i in range(FX // 2):
-        one, two = by_parity("tile", t1[part(i), :].astype(F32), t2[part(i), :].astype(F32))
-        right.append(one)
-        left.append(two)
+        there = t[pl.ds(slot(1) + i * RHS, RHS), :].astype(F32)
+        here = t[pl.ds(slot(3) + i * RHS, RHS), :].astype(F32)
+        place = lax.axis_index("tile")
+        right.append(jnp.where(place < N_TILE - 1, there, jnp.zeros_like(there)))
+        left.append(jnp.where(place > 0, here, jnp.zeros_like(here)))
     applied = []
     for x in range(FX):
         from_left, from_right = left[x // 2], right[x // 2]
@@ -139,8 +146,8 @@
     return applied
 
 
-def second_kernel(v, u, sh, sl, stor, d1, d2, t1, t2, ap_out, u_out, *edges):
-    applied = operator(v, u, sh, sl, stor, d1, d2, t1, t2)
+def second_kernel(v, u, sh, sl, stor, d1, d2, t, ap_out, u_out, *edges):
+    applied = operator(v, u, sh, sl, stor, d1, d2, t)
     spread = []
     for x in range(FX):
         ap_out[part(x), :] = applied[x]
@@ -176,8 +183,8 @@
     base[...] = total
 
 
-def third_kernel(v, u, sh, sl, stor, d1, d2, t1, t2, base, packed):
-    applied = operator(v, u, sh, sl, stor, d1, d2, t1, t2)
+def third_kernel(v, u, sh, sl, stor, d1, d2, t, base, packed):
+    applied = operator(v, u, sh, sl, stor, d1, d2, t)
     total = jnp.zeros((2 * RHS, RHS), F32)
     for x in range(FX):
         image = split(applied[x])
@@ -317,21 +324,17 @@
     )(*operands)
 
 
-EDGES = (((RHS, LANE), BF16), ((ROWS // 2 + 16, LANE), BF16), ((ROWS // 2, LANE), BF16), ((ROWS // 2, LANE), BF16))
+EDGES = (((RHS, LANE), BF16), ((RHS + 16, LANE), BF16), ((N_TILE * ROWS // 2, LANE), BF16))
 FIELD = ((ROWS, LANE), F32)
 
 
-def exchange(d1, d2, t1, t2):
-    def along(axis, one, two):
-        devices = lax.axis_size(axis)
-        first = [(i, i ^ 1) for i in range(devices)]
-        second = [(i, ((i + 1) ^ 1) - 1) for i in range(1, devices - 1)]
-        two = lax.ppermute(two, axis, second)
-        return lax.ppermute(one, axis, first), two
-
-    t1, t2 = along("tile", t1, t2)
-    d1, d2 = along("dom", d1, d2)
-    return d1, d2, t1, t2
+def exchange(d1, d2, t):
+    devices = lax.axis_size("dom")
+    first = [(i, i ^ 1) for i in range(devices)]
+    second = [(i, ((i + 1) ^ 1) - 1) for i in range(1, devices - 1)]
+    t = lax.all_to_all(t.reshape(N_TILE, -1, LANE), "tile", 0, 0, tiled=True)
+    d2 = lax.ppermute(d2, "dom", second)
+    return lax.ppermute(d1, "dom", first), d2, t.reshape(-1, LANE)
 
 
 def member_groups(sizes, together):

time: 114 us -> 114 us (level)
  Pallas kernels: 13.5 us -> 14.8 us
    ppermute x8 -> x4, starting transfers between devices: 22.7 us -> 12.5 us  [the longest x2 7.2 us: exchange(): d2 = lax.ppermute(d2, 'dom', second)]
    all_to_all x0 -> x2, starting transfers between devices: none -> 9.62 us  [exchange(): t = lax.all_to_all(t.reshape(N_TILE, -1, LANE), 'tile', 0, 0, tiled=True)]
    pallas_call x8, Pallas kernels: 13.5 us -> 14.8 us  [call(): pl.pallas_call(kernel, out_shape=[jax.ShapeDtypeStruct(shape, kind) for s...]
  transfers between devices with their start and end apart: 10 -> 8, of which waited for: 4 -> 4; matrix products, arithmetic and copies ran while one was open for 0% -> 0% of each run, Pallas kernels for 3% -> 3%
where the time goes in v9:
time: 114 us
  blocking collectives  40.1 us (35%)
  starting transfers between devices  33.1 us (29%)
  waiting for transfers between devices  23.4 us (21%)
  Pallas kernels  14.8 us (13%)
    all_to_all x2, blocking collectives, trade(): lax.all_to_all(array, axes, 0, 0, axis_index_groups=groups, tiled=True)  40.1 us
    all_to_all x1, waiting for transfers between devices, shards(): lax.all_to_all(heads, 'dom', 0, 0, tiled=True).reshape(-1, LANE).astype(F32)  16.4 us
    pallas_call x8, Pallas kernels, call(): pl.pallas_call(kernel, out_shape=[jax.ShapeDtypeStruct(shape, kind) for s...  14.8 us
    all_to_all x2, starting transfers between devices, exchange(): t = lax.all_to_all(t.reshape(N_TILE, -1, LANE), 'tile', 0, 0, tiled=True)  9.62 us
    ppermute x2, starting transfers between devices, exchange(): d2 = lax.ppermute(d2, 'dom', second)  7.2 us
    all_to_all x1, waiting for transfers between devices, trade(): lax.all_to_all(array, axes, 0, 0, axis_index_groups=groups, tiled=True)  5.77 us
    all_to_all x1, starting transfers between devices, shards(): lax.all_to_all(heads, 'dom', 0, 0, tiled=True).reshape(-1, LANE).astype(F32)  5.64 us
    all_to_all x1, starting transfers between devices, trade(): lax.all_to_all(array, axes, 0, 0, axis_index_groups=groups, tiled=True)  5.41 us
  transfers between devices with their start and end apart: 8, of which 4 were waited for; matrix products, arithmetic and copies ran while one was open for 0% of the time, Pallas kernels for 3%

profile of v9, /device:TPU:1, one launch (start us, length us, event | category | flops | bytes accessed | tf_op | source)
XLA Modules:
  0.0 113.6 jit_solution(7625256862008910810)
XLA Ops:
  0.6 2.5 %shard_map.68 = (f32[512,128]{1,0:T(8,128)S(1)}, bf16[1024,128]{1,0:T(8,128)(2,1)S(1)}, bf16[1024,128]{1,0:T(8,128)(2,1)S(1)}, f32[512,128]{1,0:T(8,128)S(1)}, b...) custom-call(f32[16,4096]{1,0:T(8,128)} %pump_hbm.1, f32[16,4096]{1,0:T(8,128)} %coup_hbm.1), custom_call_target="tpu_custom_call" | custom-call | flops 1000000 | bytes 1048576 | tf_op jit(solution)/shard_map/pallas_call | solution.py:316
  3.2 5.0 %all-to-all-start = ((bf16[4,256,128]{2,1,0:T(8,128)(2,1)}), bf16[4,256,128]{2,1,0:T(8,128)(2,1)S(1)}, u32[]{:S(2)}, u32[]{:S(2)}) async-start(bf16[4,256,128]{2,1,0:T(8,128)(2,1)} %bitcast), calls=%async_computation | async-start | bytes 524288 | tf_op jit(solution)/shard_map/all_to_all | solution.py:335
  8.2 0.0 copy-start
  8.2 4.5 %collective-permute-start.1 = (bf16[80,128]{1,0:T(8,128)(2,1)S(1)}, bf16[80,128]{1,0:T(8,128)(2,1)S(1)}, u32[]{:S(2)}, u32[]{:S(2)}) collective-permute-start(bf16[80,128]{1,0:T(8,128)(2,1)S(1)} %get-tuple-element.25), channel_id=1, source_target_pairs={{4,8},{8,4},{12,16},{16,12},{20,24},{24,20},{28,32},{32,28},{36,40... | collective-permute-start | bytes 61448 | tf_op jit(solution)/shard_map/ppermute | solution.py:336
  12.7 3.4 %collective-permute-start = (bf16[64,128]{1,0:T(8,128)(2,1)S(1)}, bf16[64,128]{1,0:T(8,128)(2,1)S(1)}, u32[]{:S(2)}, u32[]{:S(2)}) collective-permute-start(bf16[64,128]{1,0:T(8,128)(2,1)S(1)} %get-tuple-element.24), channel_id=1, source_target_pairs={{0,4},{4,0},{8,12},{12,8},{16,20},{20,16},{24,28},{28,24},{32,36},... | collective-permute-start | bytes 49160 | tf_op jit(solution)/shard_map/ppermute | solution.py:337
  16.1 0.8 collective-permute-done.d1
  16.9 0.0 collective-permute-done.1.d2
  16.9 0.0 all-to-all-done
  16.9 0.0 copy-done
  16.9 1.6 %shard_map.69 = (f32[512,128]{1,0:T(8,128)S(1)}, f32[512,128]{1,0:T(8,128)S(1)}, bf16[64,128]{1,0:T(8,128)(2,1)S(1)}, bf16[80,128]{1,0:T(8,128)(2,1)S(1)}, bf16[1024,128]{1,0:T(8,128)(2,1)}) custom-call(f32[512,128]{1,0:T(8,128)S(1)} %get-tuple-element.20.v.p, f32[512,128]{1,0:T(8,128)S(1)} %get-tuple-element.21.u, ...), custom_call_target="tpu_custom_call" | custom-call | flops 1000000 | bytes 1048576 | tf_op jit(solution)/shard_map/pallas_call | solution.py:316
  18.5 4.6 %all-to-all-start.1 = ((bf16[4,256,128]{2,1,0:T(8,128)(2,1)}), bf16[4,256,128]{2,1,0:T(8,128)(2,1)S(1)}, u32[]{:S(2)}, u32[]{:S(2)}) async-start(bf16[4,256,128]{2,1,0:T(8,128)(2,1)} %bitcast.2), calls=%async_computation.1 | async-start | bytes 524288 | tf_op jit(solution)/shard_map/all_to_all | solution.py:335
  23.1 2.7 %collective-permute-start.3 = (bf16[80,128]{1,0:T(8,128)(2,1)S(1)}, bf16[80,128]{1,0:T(8,128)(2,1)S(1)}, u32[]{:S(2)}, u32[]{:S(2)}) collective-permute-start(bf16[80,128]{1,0:T(8,128)(2,1)S(1)} %get-tuple-element.30), channel_id=1, source_target_pairs={{4,8},{8,4},{12,16},{16,12},{20,24},{24,20},{28,32},{32,28},{36,40... | collective-permute-start | bytes 61448 | tf_op jit(solution)/shard_map/ppermute | solution.py:336
  25.8 1.9 %collective-permute-start.2 = (bf16[64,128]{1,0:T(8,128)(2,1)S(1)}, bf16[64,128]{1,0:T(8,128)(2,1)S(1)}, u32[]{:S(2)}, u32[]{:S(2)}) collective-permute-start(bf16[64,128]{1,0:T(8,128)(2,1)S(1)} %get-tuple-element.29), channel_id=1, source_target_pairs={{0,4},{4,0},{8,12},{12,8},{16,20},{20,16},{24,28},{28,24},{32,36},... | collective-permute-start | bytes 49160 | tf_op jit(solution)/shard_map/ppermute | solution.py:337
  27.7 0.7 shard_map.70.base
  28.4 0.5 collective-permute-done.2.d1
  28.9 0.0 collective-permute-done.3.d2
  28.9 0.0 all-to-all-done.1
  28.9 1.2 %shard_map.71 = f32[128,128]{1,0:T(8,128)S(1)} custom-call(f32[512,128]{1,0:T(8,128)S(1)} %get-tuple-element.27.v.ap, f32[512,128]{1,0:T(8,128)S(1)} %get-tuple-element.28.u, bf16[1024,128]{1,0:T(8,128)(2,1)S(1)} %get-tuple-element.22.sh, bf16[1024,128]{1,0:T(8,128)(2,1)S(1)} %get-tuple-element.23.sl, f32[16,64]{1,0:T(8,128)S(1)} %copy-done, ...), custom_call_target="tpu_custom_call" | custom-call | flops 1000000 | bytes 1048576 | tf_op jit(solution)/shard_map/pallas_call | solution.py:316
  30.0 21.9 %all_to_all.30 = f32[32,4,128]{2,1,0:T(4,128)S(1)} all-to-all(f32[32,4,128]{2,1,0:T(4,128)S(1)} %bitcast.13), channel_id=1, replica_groups={{0,1,2,3,4,5,6,7,128,129,130,131,132,133,134,135,256,257,258,259,260,26..., dimensions={0} | all-to-all | bytes 131072 | tf_op jit(solution)/shard_map/all_to_all | solution.py:363
  52.0 18.2 %all_to_all.31 = f32[16,4,128]{2,1,0:T(4,128)S(1)} all-to-all(f32[16,4,128]{2,1,0:T(4,128)S(1)} %broadcast_in_dim.4), channel_id=1, replica_groups={{0,8,16,24,32,40,48,56,64,72,80,88,96,104,112,120},{1,9,17,25,33,41,49,..., dimensions={0} | all-to-all | bytes 65536 | tf_op jit(solution)/shard_map/all_to_all | solution.py:363
  70.2 0.6 broadcast_in_dim.5
  70.8 5.4 %all-to-all-start.4 = ((f32[32,4,128]{2,1,0:T(4,128)}), f32[32,4,128]{2,1,0:T(4,128)S(1)}, u32[]{:S(2)}, u32[]{:S(2)}) async-start(f32[32,4,128]{2,1,0:T(4,128)} %broadcast_in_dim.5), calls=%async_computation.4 | async-start | bytes 131072 | tf_op jit(solution)/shard_map/all_to_all | solution.py:363
  76.3 0.0 copy-done.2
  76.3 1.5 %shard_map.72.refs_1_ = bf16[1024,256]{1,0:T(8,128)(2,1)S(1)} custom-call(s32[1,1024]{1,0:T(1,128)S(1)} %copy-done.2, f32[512,128]{1,0:T(8,128)S(1)} %get-tuple-element.20.v.p, f32[512,128]{1,0:T(8,128)S(1)} %get-tuple-element.27.v.ap), custom_call_target="tpu_custom_call" | custom-call | flops 99999997952 | bytes 1048576 | tf_op jit(solution)/shard_map/pallas_call | solution.py:316
  77.8 5.8 %all-to-all-done.4 = f32[32,4,128]{2,1,0:T(4,128)S(1)} async-done(((f32[32,4,128]{2,1,0:T(4,128)}), f32[32,4,128]{2,1,0:T(4,128)S(1)}, u32[]{:S(2)}, u32[]{:S(2)}) %all-to-all-start.4) | async-done | bytes 65568 | tf_op jit(solution)/shard_map/all_to_all | solution.py:363
  83.6 5.2 %shard_map.73 = (f32[512,128]{1,0:T(8,128)S(1)}, f32[1,64]{1,0:T(1,128)S(1)}, f32[128,64]{1,0:T(8,128)S(1)}, f32[64,128]{1,0:T(8,128)S(1)}) custom-call(f32[128,128]{1,0:T(8,128)S(1)} %bitcast.11, bf16[1024,256]{1,0:T(8,128)(2,1)S(1)} %shard_map.72.refs_1_), custom_call_target="tpu_custom_call" | custom-call | flops 1000000 | bytes 1048576 | tf_op jit(solution)/shard_map/pallas_call | solution.py:316
  88.8 0.7 convert_element_type.8
  89.5 5.6 %all-to-all-start.5 = ((f16[128,4,128]{2,1,0:T(4,128)(2,1)}), f16[128,4,128]{2,1,0:T(4,128)(2,1)S(1)}, u32[]{:S(2)}, u32[]{:S(2)}) async-start(f16[128,4,128]{2,1,0:T(4,128)(2,1)} %bitcast.6), calls=%async_computation.5 | async-start | bytes 262144 | tf_op jit(solution)/shard_map/all_to_all | solution.py:412
  95.1 0.0 copy-done.1
  95.1 1.1 %shard_map.74 = (f32[64,64]{1,0:T(8,128)}, bf16[16,1024]{1,0:T(8,128)(2,1)S(1)}) custom-call(f32[128,128]{1,0:T(8,128)S(1)} %bitcast.12, f32[128,64]{1,0:T(8,128)S(1)} %get-tuple-element.32.refs_1_, f32[64,128]{1,0:T(8,128)S(1)} %get-tuple-element.33.refs_2_, bf16[16,1024]{1,0:T(8,128)(2,1)S(1)} %copy-done.1), custom_call_target="tpu_custom_call" | custom-call | flops 99999997952 | bytes 1048576 | tf_op jit(solution)/shard_map/pallas_call | solution.py:316
  96.3 16.4 %all-to-all-done.5 = f16[128,4,128]{2,1,0:T(4,128)(2,1)S(1)} async-done(((f16[128,4,128]{2,1,0:T(4,128)(2,1)}), f16[128,4,128]{2,1,0:T(4,128)(2,1)S(1)}, u32[]{:S(2)}, u32[]{:S(2)}) %all-to-all-start.5) | async-done | bytes 131104 | tf_op jit(solution)/shard_map/all_to_all | solution.py:412
  112.6 0.9 shard_map.75
  (6 shorter events, 0.1 us)
Async XLA Ops:
  3.2 13.7 %all-to-all-start = ((bf16[4,256,128]{2,1,0:T(8,128)(2,1)}), bf16[4,256,128]{2,1,0:T(8,128)(2,1)S(1)}, u32[]{:S(2)}, u32[]{:S(2)}) async-start(bf16[4,256,128]{2,1,0:T(8,128)(2,1)} %bitcast), calls=%async_computation | async-start | bytes 524288 | tf_op jit(solution)/shard_map/all_to_all | solution.py:335
  8.2 8.7 %copy-start = (f32[16,64]{1,0:T(8,128)S(1)}, f32[16,64]{1,0:T(8,128)}, u32[]{:S(2)}) copy-start(f32[16,64]{1,0:T(8,128)} %stor.3) | copy-start | bytes 12292
  8.2 8.7 %collective-permute-start.1 = (bf16[80,128]{1,0:T(8,128)(2,1)S(1)}, bf16[80,128]{1,0:T(8,128)(2,1)S(1)}, u32[]{:S(2)}, u32[]{:S(2)}) collective-permute-start(bf16[80,128]{1,0:T(8,128)(2,1)S(1)} %get-tuple-element.25), channel_id=1, source_target_pairs={{4,8},{8,4},{12,16},{16,12},{20,24},{24,20},{28,32},{32,28},{36,40... | collective-permute-start | bytes 61448 | tf_op jit(solution)/shard_map/ppermute | solution.py:336
  12.7 4.2 %collective-permute-start = (bf16[64,128]{1,0:T(8,128)(2,1)S(1)}, bf16[64,128]{1,0:T(8,128)(2,1)S(1)}, u32[]{:S(2)}, u32[]{:S(2)}) collective-permute-start(bf16[64,128]{1,0:T(8,128)(2,1)S(1)} %get-tuple-element.24), channel_id=1, source_target_pairs={{0,4},{4,0},{8,12},{12,8},{16,20},{20,16},{24,28},{28,24},{32,36},... | collective-permute-start | bytes 49160 | tf_op jit(solution)/shard_map/ppermute | solution.py:337
  18.5 10.4 %all-to-all-start.1 = ((bf16[4,256,128]{2,1,0:T(8,128)(2,1)}), bf16[4,256,128]{2,1,0:T(8,128)(2,1)S(1)}, u32[]{:S(2)}, u32[]{:S(2)}) async-start(bf16[4,256,128]{2,1,0:T(8,128)(2,1)} %bitcast.2), calls=%async_computation.1 | async-start | bytes 524288 | tf_op jit(solution)/shard_map/all_to_all | solution.py:335
  23.1 5.8 %collective-permute-start.3 = (bf16[80,128]{1,0:T(8,128)(2,1)S(1)}, bf16[80,128]{1,0:T(8,128)(2,1)S(1)}, u32[]{:S(2)}, u32[]{:S(2)}) collective-permute-start(bf16[80,128]{1,0:T(8,128)(2,1)S(1)} %get-tuple-element.30), channel_id=1, source_target_pairs={{4,8},{8,4},{12,16},{16,12},{20,24},{24,20},{28,32},{32,28},{36,40... | collective-permute-start | bytes 61448 | tf_op jit(solution)/shard_map/ppermute | solution.py:336
  25.8 3.1 %collective-permute-start.2 = (bf16[64,128]{1,0:T(8,128)(2,1)S(1)}, bf16[64,128]{1,0:T(8,128)(2,1)S(1)}, u32[]{:S(2)}, u32[]{:S(2)}) collective-permute-start(bf16[64,128]{1,0:T(8,128)(2,1)S(1)} %get-tuple-element.29), channel_id=1, source_target_pairs={{0,4},{4,0},{8,12},{12,8},{16,20},{20,16},{24,28},{28,24},{32,36},... | collective-permute-start | bytes 49160 | tf_op jit(solution)/shard_map/ppermute | solution.py:337
  70.8 5.4 %copy-start.2 = (s32[1,1024]{1,0:T(1,128)S(1)}, s32[1,1024]{1,0:T(1,128)}, u32[]{:S(2)}) copy-start(s32[1,1024]{1,0:T(1,128)} %order.1) | copy-start | bytes 12292
  70.8 12.8 %all-to-all-start.4 = ((f32[32,4,128]{2,1,0:T(4,128)}), f32[32,4,128]{2,1,0:T(4,128)S(1)}, u32[]{:S(2)}, u32[]{:S(2)}) async-start(f32[32,4,128]{2,1,0:T(4,128)} %broadcast_in_dim.5), calls=%async_computation.4 | async-start | bytes 131072 | tf_op jit(solution)/shard_map/all_to_all | solution.py:363
  89.5 5.7 %copy-start.1 = (bf16[16,1024]{1,0:T(8,128)(2,1)S(1)}, bf16[16,1024]{1,0:T(8,128)(2,1)}, u32[]{:S(2)}) copy-start(bf16[16,1024]{1,0:T(8,128)(2,1)} %refs_3_.1) | copy-start | bytes 98308
  89.5 23.2 %all-to-all-start.5 = ((f16[128,4,128]{2,1,0:T(4,128)(2,1)}), f16[128,4,128]{2,1,0:T(4,128)(2,1)S(1)}, u32[]{:S(2)}, u32[]{:S(2)}) async-start(f16[128,4,128]{2,1,0:T(4,128)(2,1)} %bitcast.6), calls=%async_computation.5 | async-start | bytes 262144 | tf_op jit(solution)/shard_map/all_to_all | solution.py:412

commit v10 on v9

--- a/solution.py
+++ b/solution.py
@@ -8,6 +8,7 @@
 RHS = 64
 CB = 64
 FX = 8
+PILOT = 16
 N_TILE = 4
 LANE = 128
 ROWS = FX * RHS
@@ -62,8 +63,7 @@
 
 
 def slot(step):
-    index = lax.rem(lax.axis_index("tile") + step, N_TILE)
-    return pl.multiple_of(index * (ROWS // 2), ROWS // 2)
+    return lax.rem(lax.axis_index("tile") + step, N_TILE)
 
 
 def write_edges(spread, d1, d2, t):
@@ -73,11 +73,11 @@
     d2[:RHS, :] = two.astype(BF16)
     d2[RHS:, :] = jnp.zeros((d2.shape[0] - RHS, LANE), BF16)
     for step in (0, 2):
-        t[pl.ds(slot(step), ROWS // 2), :] = jnp.zeros((ROWS // 2, LANE), BF16)
+        t[slot(step)] = jnp.zeros((ROWS // 2, LANE), BF16)
     for i in range(FX // 2):
         even, odd = spread[2 * i], spread[2 * i + 1]
-        t[pl.ds(slot(1) + i * RHS, RHS), :] = jnp.where(low, swap(even), odd).astype(BF16)
-        t[pl.ds(slot(3) + i * RHS, RHS), :] = jnp.where(low, even, swap(odd)).astype(BF16)
+        t[slot(1), part(i), :] = jnp.where(low, swap(even), odd).astype(BF16)
+        t[slot(3), part(i), :] = jnp.where(low, even, swap(odd)).astype(BF16)
 
 
 def first_kernel(pump_hbm, coup_hbm, p_out, sh_out, sl_out, u_out, d1, d2, t, pump, coup, rows_p, rows_s, mats, arrived):
@@ -125,8 +125,8 @@
     ends = [before] + spread + [after]
     right, left = [], []
     for i in range(FX // 2):
-        there = t[pl.ds(slot(1) + i * RHS, RHS), :].astype(F32)
-        here = t[pl.ds(slot(3) + i * RHS, RHS), :].astype(F32)
+        there = t[slot(1), part(i), :].astype(F32)
+        here = t[slot(3), part(i), :].astype(F32)
         place = lax.axis_index("tile")
         right.append(jnp.where(place < N_TILE - 1, there, jnp.zeros_like(there)))
         left.append(jnp.where(place > 0, here, jnp.zeros_like(here)))
@@ -277,8 +277,9 @@
     m1, m3 = unpack_pair(packed[:RHS, RHS:], packed[RHS + 1 : RHS + 2, RHS:])
     first = eliminate(jnp.concatenate([m1, m0, m2], axis=1))
     alpha, shift = first[:, :RHS], first[:, RHS:]
-    curved = symmetric(m3 - exact(m2, shift))
-    target = m1 - exact(m2, alpha)
+    bent = exact(m2, first)
+    curved = symmetric(m3 - bent[:, RHS:])
+    target = m1 - bent[:, :RHS]
     gamma = eliminate(jnp.concatenate([curved, target], axis=1))
     mixed = alpha - exact(shift, gamma)
     both = jnp.concatenate([mixed, gamma], axis=0)
@@ -297,19 +298,21 @@
 
 
 def gram_kernel(cell_total, packed, weights, later, kriging, gram, kept):
-    kept[...] = kriging[...]
+    cells = kriging.shape[1]
+    source = lax.broadcasted_iota(jnp.int32, (cells, cells // 2), 0)
+    target = lax.broadcasted_iota(jnp.int32, (cells, cells // 2), 1)
+    for parity in range(2):
+        pick = jnp.where(source == 2 * target + parity, 1.0, 0.0).astype(BF16)
+        kept[pl.ds(parity * PILOT, PILOT), :] = dot(kriging[...], pick, NN).astype(BF16)
     mixed, gamma = weights[:RHS, :], weights[RHS:, :]
     rest = exact(packed[RHS:, :RHS], gamma) + exact(later[:, RHS:], mixed) - later[:, :RHS]
     gram[...] = symmetric(exact(jnp.transpose(gamma), rest)) * (1.0 / cell_total)
 
 
-def product_kernel(kriging, arrived, scale, sens, rows):
-    half = FX * LANE // 2
-    value = arrived[...].astype(F32)
-    rows[pl.ds(0, half, stride=2), :] = value
-    rows[pl.ds(1, half, stride=2), :] = swap(value)
-    high, rest = split(rows[...])
-    sens[...] = (dot(kriging[...], high, NN) + dot(kriging[...], rest, NN))[:, :RHS] * scale[...]
+def product_kernel(kriging, arrived, scale, sens):
+    high, rest = split(arrived[...])
+    product = dot(kriging[...], high, NN) + dot(kriging[...], rest, NN)
+    sens[...] = (product[:PILOT, :RHS] + product[PILOT:, RHS:]) * scale[...]
 
 
 def call(kernel, shapes, *operands, scratch=(), flops=1000000, place=pltpu.VMEM):
@@ -324,7 +327,7 @@
     )(*operands)
 
 
-EDGES = (((RHS, LANE), BF16), ((RHS + 16, LANE), BF16), ((N_TILE * ROWS // 2, LANE), BF16))
+EDGES = (((RHS, LANE), BF16), ((RHS + 16, LANE), BF16), ((N_TILE, ROWS // 2, LANE), BF16))
 FIELD = ((ROWS, LANE), F32)
 
 
@@ -332,9 +335,9 @@
     devices = lax.axis_size("dom")
     first = [(i, i ^ 1) for i in range(devices)]
     second = [(i, ((i + 1) ^ 1) - 1) for i in range(1, devices - 1)]
-    t = lax.all_to_all(t.reshape(N_TILE, -1, LANE), "tile", 0, 0, tiled=True)
+    t = lax.all_to_all(t, "tile", 0, 0, tiled=True)
     d2 = lax.ppermute(d2, "dom", second)
-    return lax.ppermute(d1, "dom", first), d2, t.reshape(-1, LANE)
+    return lax.ppermute(d1, "dom", first), d2, t
 
 
 def member_groups(sizes, together):
@@ -412,15 +415,14 @@
     heads = lax.all_to_all(heads, "dom", 0, 0, tiled=True).reshape(-1, LANE).astype(F32)
     gram, kriging = call(
         lambda *refs: gram_kernel(cell_total, *refs),
-        (((RHS, RHS), F32), (kriging.shape, BF16)),
+        (((RHS, RHS), F32), ((2 * PILOT, FX * LANE // 2), BF16)),
         *(packed, weights, later, kriging),
         flops=LONG,
     )
     (sens,) = call(
         product_kernel,
-        (((kriging.shape[0], RHS), F32),),
+        (((PILOT, RHS), F32),),
         *(kriging, heads, scale),
-        scratch=(scratch(FX * LANE),),
     )
     return sens, gram
 

time: 114 us -> 114 us (level)
  no operation moved by 1% of the time
where the time goes in v10:
time: 114 us
  blocking collectives  40.1 us (35%)
  starting transfers between devices  33.1 us (29%)
  waiting for transfers between devices  23.2 us (20%)
  Pallas kernels  15.1 us (13%)
    all_to_all x2, blocking collectives, trade(): lax.all_to_all(array, axes, 0, 0, axis_index_groups=groups, tiled=True)  40.1 us
    all_to_all x1, waiting for transfers between devices, shards(): lax.all_to_all(heads, 'dom', 0, 0, tiled=True).reshape(-1, LANE).astype(F32)  16.1 us
    pallas_call x8, Pallas kernels, call(): pl.pallas_call(kernel, out_shape=[jax.ShapeDtypeStruct(shape, kind) for s...  15.1 us
    all_to_all x2, starting transfers between devices, exchange(): t = lax.all_to_all(t, 'tile', 0, 0, tiled=True)  9.62 us
    ppermute x2, starting transfers between devices, exchange(): d2 = lax.ppermute(d2, 'dom', second)  7.19 us
    all_to_all x1, waiting for transfers between devices, trade(): lax.all_to_all(array, axes, 0, 0, axis_index_groups=groups, tiled=True)  5.77 us
    all_to_all x1, starting transfers between devices, shards(): lax.all_to_all(heads, 'dom', 0, 0, tiled=True).reshape(-1, LANE).astype(F32)  5.64 us
    all_to_all x1, starting transfers between devices, trade(): lax.all_to_all(array, axes, 0, 0, axis_index_groups=groups, tiled=True)  5.41 us
  transfers between devices with their start and end apart: 8, of which 4 were waited for; matrix products, arithmetic and copies ran while one was open for 0% of the time, Pallas kernels for 3%

profile of v10, /device:TPU:1, one launch (start us, length us, event | category | flops | bytes accessed | tf_op | source)
XLA Modules:
  0.0 113.6 jit_solution(1454531520513493001)
XLA Ops:
  0.6 2.5 %shard_map.68 = (f32[512,128]{1,0:T(8,128)S(1)}, bf16[1024,128]{1,0:T(8,128)(2,1)S(1)}, bf16[1024,128]{1,0:T(8,128)(2,1)S(1)}, f32[512,128]{1,0:T(8,128)S(1)}, b...) custom-call(f32[16,4096]{1,0:T(8,128)} %pump_hbm.1, f32[16,4096]{1,0:T(8,128)} %coup_hbm.1), custom_call_target="tpu_custom_call" | custom-call | flops 1000000 | bytes 1048576 | tf_op jit(solution)/shard_map/pallas_call | solution.py:319
  3.2 5.0 %all-to-all-start = ((bf16[4,256,128]{2,1,0:T(8,128)(2,1)}), bf16[4,256,128]{2,1,0:T(8,128)(2,1)S(1)}, u32[]{:S(2)}, u32[]{:S(2)}) async-start(bf16[4,256,128]{2,1,0:T(8,128)(2,1)} %get-tuple-element.26), calls=%async_computation | async-start | bytes 524288 | tf_op jit(solution)/shard_map/all_to_all | solution.py:338
  8.2 0.0 copy-start
  8.2 4.5 %collective-permute-start.1 = (bf16[80,128]{1,0:T(8,128)(2,1)S(1)}, bf16[80,128]{1,0:T(8,128)(2,1)S(1)}, u32[]{:S(2)}, u32[]{:S(2)}) collective-permute-start(bf16[80,128]{1,0:T(8,128)(2,1)S(1)} %get-tuple-element.25), channel_id=1, source_target_pairs={{4,8},{8,4},{12,16},{16,12},{20,24},{24,20},{28,32},{32,28},{36,40... | collective-permute-start | bytes 61448 | tf_op jit(solution)/shard_map/ppermute | solution.py:339
  12.7 3.4 %collective-permute-start = (bf16[64,128]{1,0:T(8,128)(2,1)S(1)}, bf16[64,128]{1,0:T(8,128)(2,1)S(1)}, u32[]{:S(2)}, u32[]{:S(2)}) collective-permute-start(bf16[64,128]{1,0:T(8,128)(2,1)S(1)} %get-tuple-element.24), channel_id=1, source_target_pairs={{0,4},{4,0},{8,12},{12,8},{16,20},{20,16},{24,28},{28,24},{32,36},... | collective-permute-start | bytes 49160 | tf_op jit(solution)/shard_map/ppermute | solution.py:340
  16.1 0.8 collective-permute-done.d1
  16.9 0.0 collective-permute-done.1.d2
  16.9 0.0 all-to-all-done.t
  16.9 0.0 copy-done
  16.9 1.6 %shard_map.69 = (f32[512,128]{1,0:T(8,128)S(1)}, f32[512,128]{1,0:T(8,128)S(1)}, bf16[64,128]{1,0:T(8,128)(2,1)S(1)}, bf16[80,128]{1,0:T(8,128)(2,1)S(1)}, bf16[4,256,128]{2,1,0:T(8,128)(2,1)}) custom-call(f32[512,128]{1,0:T(8,128)S(1)} %get-tuple-element.20.v.p, f32[512,128]{1,0:T(8,128)S(1)} %get-tuple-element.21.u, ...), custom_call_target="tpu_custom_call" | custom-call | flops 1000000 | bytes 1048576 | tf_op jit(solution)/shard_map/pallas_call | solution.py:319
  18.5 4.6 %all-to-all-start.1 = ((bf16[4,256,128]{2,1,0:T(8,128)(2,1)}), bf16[4,256,128]{2,1,0:T(8,128)(2,1)S(1)}, u32[]{:S(2)}, u32[]{:S(2)}) async-start(bf16[4,256,128]{2,1,0:T(8,128)(2,1)} %get-tuple-element.31), calls=%async_computation.1 | async-start | bytes 524288 | tf_op jit(solution)/shard_map/all_to_all | solution.py:338
  23.1 2.7 %collective-permute-start.3 = (bf16[80,128]{1,0:T(8,128)(2,1)S(1)}, bf16[80,128]{1,0:T(8,128)(2,1)S(1)}, u32[]{:S(2)}, u32[]{:S(2)}) collective-permute-start(bf16[80,128]{1,0:T(8,128)(2,1)S(1)} %get-tuple-element.30), channel_id=1, source_target_pairs={{4,8},{8,4},{12,16},{16,12},{20,24},{24,20},{28,32},{32,28},{36,40... | collective-permute-start | bytes 61448 | tf_op jit(solution)/shard_map/ppermute | solution.py:339
  25.8 1.9 %collective-permute-start.2 = (bf16[64,128]{1,0:T(8,128)(2,1)S(1)}, bf16[64,128]{1,0:T(8,128)(2,1)S(1)}, u32[]{:S(2)}, u32[]{:S(2)}) collective-permute-start(bf16[64,128]{1,0:T(8,128)(2,1)S(1)} %get-tuple-element.29), channel_id=1, source_target_pairs={{0,4},{4,0},{8,12},{12,8},{16,20},{20,16},{24,28},{28,24},{32,36},... | collective-permute-start | bytes 49160 | tf_op jit(solution)/shard_map/ppermute | solution.py:340
  27.7 0.7 shard_map.70.base
  28.4 0.5 collective-permute-done.2.d1
  28.9 0.0 collective-permute-done.3.d2
  28.9 0.0 all-to-all-done.1.t
  28.9 1.2 %shard_map.71 = f32[128,128]{1,0:T(8,128)S(1)} custom-call(f32[512,128]{1,0:T(8,128)S(1)} %get-tuple-element.27.v.ap, f32[512,128]{1,0:T(8,128)S(1)} %get-tuple-element.28.u, bf16[1024,128]{1,0:T(8,128)(2,1)S(1)} %get-tuple-element.22.sh, bf16[1024,128]{1,0:T(8,128)(2,1)S(1)} %get-tuple-element.23.sl, f32[16,64]{1,0:T(8,128)S(1)} %copy-done, ...), custom_call_target="tpu_custom_call" | custom-call | flops 1000000 | bytes 1048576 | tf_op jit(solution)/shard_map/pallas_call | solution.py:319
  30.0 21.9 %all_to_all.30 = f32[32,4,128]{2,1,0:T(4,128)S(1)} all-to-all(f32[32,4,128]{2,1,0:T(4,128)S(1)} %bitcast.7), channel_id=1, replica_groups={{0,1,2,3,4,5,6,7,128,129,130,131,132,133,134,135,256,257,258,259,260,26..., dimensions={0} | all-to-all | bytes 131072 | tf_op jit(solution)/shard_map/all_to_all | solution.py:366
  52.0 18.2 %all_to_all.31 = f32[16,4,128]{2,1,0:T(4,128)S(1)} all-to-all(f32[16,4,128]{2,1,0:T(4,128)S(1)} %broadcast_in_dim.4), channel_id=1, replica_groups={{0,8,16,24,32,40,48,56,64,72,80,88,96,104,112,120},{1,9,17,25,33,41,49,..., dimensions={0} | all-to-all | bytes 65536 | tf_op jit(solution)/shard_map/all_to_all | solution.py:366
  70.2 0.6 broadcast_in_dim.5
  70.8 5.4 %all-to-all-start.4 = ((f32[32,4,128]{2,1,0:T(4,128)}), f32[32,4,128]{2,1,0:T(4,128)S(1)}, u32[]{:S(2)}, u32[]{:S(2)}) async-start(f32[32,4,128]{2,1,0:T(4,128)} %broadcast_in_dim.5), calls=%async_computation.4 | async-start | bytes 131072 | tf_op jit(solution)/shard_map/all_to_all | solution.py:366
  76.3 0.0 copy-done.2
  76.3 1.5 %shard_map.72.refs_1_ = bf16[1024,256]{1,0:T(8,128)(2,1)S(1)} custom-call(s32[1,1024]{1,0:T(1,128)S(1)} %copy-done.2, f32[512,128]{1,0:T(8,128)S(1)} %get-tuple-element.20.v.p, f32[512,128]{1,0:T(8,128)S(1)} %get-tuple-element.27.v.ap), custom_call_target="tpu_custom_call" | custom-call | flops 99999997952 | bytes 1048576 | tf_op jit(solution)/shard_map/pallas_call | solution.py:319
  77.8 5.8 %all-to-all-done.4 = f32[32,4,128]{2,1,0:T(4,128)S(1)} async-done(((f32[32,4,128]{2,1,0:T(4,128)}), f32[32,4,128]{2,1,0:T(4,128)S(1)}, u32[]{:S(2)}, u32[]{:S(2)}) %all-to-all-start.4) | async-done | bytes 65568 | tf_op jit(solution)/shard_map/all_to_all | solution.py:366
  83.6 5.3 %shard_map.73 = (f32[512,128]{1,0:T(8,128)S(1)}, f32[1,64]{1,0:T(1,128)S(1)}, f32[128,64]{1,0:T(8,128)S(1)}, f32[64,128]{1,0:T(8,128)S(1)}) custom-call(f32[128,128]{1,0:T(8,128)S(1)} %bitcast.5, bf16[1024,256]{1,0:T(8,128)(2,1)S(1)} %shard_map.72.refs_1_), custom_call_target="tpu_custom_call" | custom-call | flops 1000000 | bytes 1048576 | tf_op jit(solution)/shard_map/pallas_call | solution.py:319
  88.9 0.7 convert_element_type.8
  89.6 5.6 %all-to-all-start.5 = ((f16[128,4,128]{2,1,0:T(4,128)(2,1)}), f16[128,4,128]{2,1,0:T(4,128)(2,1)S(1)}, u32[]{:S(2)}, u32[]{:S(2)}) async-start(f16[128,4,128]{2,1,0:T(4,128)(2,1)} %bitcast.2), calls=%async_computation.5 | async-start | bytes 262144 | tf_op jit(solution)/shard_map/all_to_all | solution.py:415
  95.2 0.0 copy-done.1
  95.2 1.4 %shard_map.74 = (f32[64,64]{1,0:T(8,128)}, bf16[32,512]{1,0:T(8,128)(2,1)S(1)}) custom-call(f32[128,128]{1,0:T(8,128)S(1)} %bitcast.6, f32[128,64]{1,0:T(8,128)S(1)} %get-tuple-element.32.refs_1_, f32[64,128]{1,0:T(8,128)S(1)} %get-tuple-element.33.refs_2_, bf16[16,1024]{1,0:T(8,128)(2,1)S(1)} %copy-done.1), custom_call_target="tpu_custom_call" | custom-call | flops 99999997952 | bytes 1048576 | tf_op jit(solution)/shard_map/pallas_call | solution.py:319
  96.6 16.1 %all-to-all-done.5 = f16[128,4,128]{2,1,0:T(4,128)(2,1)S(1)} async-done(((f16[128,4,128]{2,1,0:T(4,128)(2,1)}), f16[128,4,128]{2,1,0:T(4,128)(2,1)S(1)}, u32[]{:S(2)}, u32[]{:S(2)}) %all-to-all-start.5) | async-done | bytes 131104 | tf_op jit(solution)/shard_map/all_to_all | solution.py:415
  112.8 0.8 shard_map.75
  (6 shorter events, 0.1 us)
Async XLA Ops:
  3.2 13.7 %all-to-all-start = ((bf16[4,256,128]{2,1,0:T(8,128)(2,1)}), bf16[4,256,128]{2,1,0:T(8,128)(2,1)S(1)}, u32[]{:S(2)}, u32[]{:S(2)}) async-start(bf16[4,256,128]{2,1,0:T(8,128)(2,1)} %get-tuple-element.26), calls=%async_computation | async-start | bytes 524288 | tf_op jit(solution)/shard_map/all_to_all | solution.py:338
  8.2 8.7 %copy-start = (f32[16,64]{1,0:T(8,128)S(1)}, f32[16,64]{1,0:T(8,128)}, u32[]{:S(2)}) copy-start(f32[16,64]{1,0:T(8,128)} %stor.3) | copy-start | bytes 12292
  8.2 8.7 %collective-permute-start.1 = (bf16[80,128]{1,0:T(8,128)(2,1)S(1)}, bf16[80,128]{1,0:T(8,128)(2,1)S(1)}, u32[]{:S(2)}, u32[]{:S(2)}) collective-permute-start(bf16[80,128]{1,0:T(8,128)(2,1)S(1)} %get-tuple-element.25), channel_id=1, source_target_pairs={{4,8},{8,4},{12,16},{16,12},{20,24},{24,20},{28,32},{32,28},{36,40... | collective-permute-start | bytes 61448 | tf_op jit(solution)/shard_map/ppermute | solution.py:339
  12.7 4.2 %collective-permute-start = (bf16[64,128]{1,0:T(8,128)(2,1)S(1)}, bf16[64,128]{1,0:T(8,128)(2,1)S(1)}, u32[]{:S(2)}, u32[]{:S(2)}) collective-permute-start(bf16[64,128]{1,0:T(8,128)(2,1)S(1)} %get-tuple-element.24), channel_id=1, source_target_pairs={{0,4},{4,0},{8,12},{12,8},{16,20},{20,16},{24,28},{28,24},{32,36},... | collective-permute-start | bytes 49160 | tf_op jit(solution)/shard_map/ppermute | solution.py:340
  18.5 10.4 %all-to-all-start.1 = ((bf16[4,256,128]{2,1,0:T(8,128)(2,1)}), bf16[4,256,128]{2,1,0:T(8,128)(2,1)S(1)}, u32[]{:S(2)}, u32[]{:S(2)}) async-start(bf16[4,256,128]{2,1,0:T(8,128)(2,1)} %get-tuple-element.31), calls=%async_computation.1 | async-start | bytes 524288 | tf_op jit(solution)/shard_map/all_to_all | solution.py:338
  23.1 5.8 %collective-permute-start.3 = (bf16[80,128]{1,0:T(8,128)(2,1)S(1)}, bf16[80,128]{1,0:T(8,128)(2,1)S(1)}, u32[]{:S(2)}, u32[]{:S(2)}) collective-permute-start(bf16[80,128]{1,0:T(8,128)(2,1)S(1)} %get-tuple-element.30), channel_id=1, source_target_pairs={{4,8},{8,4},{12,16},{16,12},{20,24},{24,20},{28,32},{32,28},{36,40... | collective-permute-start | bytes 61448 | tf_op jit(solution)/shard_map/ppermute | solution.py:339
  25.8 3.1 %collective-permute-start.2 = (bf16[64,128]{1,0:T(8,128)(2,1)S(1)}, bf16[64,128]{1,0:T(8,128)(2,1)S(1)}, u32[]{:S(2)}, u32[]{:S(2)}) collective-permute-start(bf16[64,128]{1,0:T(8,128)(2,1)S(1)} %get-tuple-element.29), channel_id=1, source_target_pairs={{0,4},{4,0},{8,12},{12,8},{16,20},{20,16},{24,28},{28,24},{32,36},... | collective-permute-start | bytes 49160 | tf_op jit(solution)/shard_map/ppermute | solution.py:340
  70.8 5.4 %copy-start.2 = (s32[1,1024]{1,0:T(1,128)S(1)}, s32[1,1024]{1,0:T(1,128)}, u32[]{:S(2)}) copy-start(s32[1,1024]{1,0:T(1,128)} %order.1) | copy-start | bytes 12292
  70.8 12.7 %all-to-all-start.4 = ((f32[32,4,128]{2,1,0:T(4,128)}), f32[32,4,128]{2,1,0:T(4,128)S(1)}, u32[]{:S(2)}, u32[]{:S(2)}) async-start(f32[32,4,128]{2,1,0:T(4,128)} %broadcast_in_dim.5), calls=%async_computation.4 | async-start | bytes 131072 | tf_op jit(solution)/shard_map/all_to_all | solution.py:366
  89.6 5.7 %copy-start.1 = (bf16[16,1024]{1,0:T(8,128)(2,1)S(1)}, bf16[16,1024]{1,0:T(8,128)(2,1)}, u32[]{:S(2)}) copy-start(bf16[16,1024]{1,0:T(8,128)(2,1)} %refs_3_.1) | copy-start | bytes 98308
  89.6 23.2 %all-to-all-start.5 = ((f16[128,4,128]{2,1,0:T(4,128)(2,1)}), f16[128,4,128]{2,1,0:T(4,128)(2,1)S(1)}, u32[]{:S(2)}, u32[]{:S(2)}) async-start(f16[128,4,128]{2,1,0:T(4,128)(2,1)} %bitcast.2), calls=%async_computation.5 | async-start | bytes 262144 | tf_op jit(solution)/shard_map/all_to_all | solution.py:415

commit v11 on v8

--- a/solution.py
+++ b/solution.py
@@ -8,6 +8,7 @@
 RHS = 64
 CB = 64
 FX = 8
+PILOT = 16
 LANE = 128
 ROWS = FX * RHS
 F32 = jnp.float32
@@ -252,12 +253,13 @@
         parts[g] = rows
         for h in range(len(parts)):
             if h != g:
-                taken = None
-                for q in range(panel):
-                    column = jnp.broadcast_to(parts[h][:, first + q : first + q + 1], (panel, width))
-                    term = column * rows[q : q + 1, :]
-                    taken = term if taken is None else taken + term
-                parts[h] = parts[h] - taken
+                terms = [
+                    jnp.broadcast_to(parts[h][:, first + q : first + q + 1], (panel, width)) * rows[q : q + 1, :]
+                    for q in range(panel)
+                ]
+                while len(terms) > 1:
+                    terms = [a + b for a, b in zip(terms[::2], terms[1::2])]
+                parts[h] = parts[h] - terms[0]
     return jnp.concatenate(parts, axis=0)[:, order:]
 
 
@@ -270,8 +272,9 @@
     m1, m3 = unpack_pair(packed[:RHS, RHS:], packed[RHS + 1 : RHS + 2, RHS:])
     first = eliminate(jnp.concatenate([m1, m0, m2], axis=1))
     alpha, shift = first[:, :RHS], first[:, RHS:]
-    curved = symmetric(m3 - exact(m2, shift))
-    target = m1 - exact(m2, alpha)
+    bent = exact(m2, first)
+    curved = symmetric(m3 - bent[:, RHS:])
+    target = m1 - bent[:, :RHS]
     gamma = eliminate(jnp.concatenate([curved, target], axis=1))
     mixed = alpha - exact(shift, gamma)
     both = jnp.concatenate([mixed, gamma], axis=0)
@@ -290,19 +293,21 @@
 
 
 def gram_kernel(cell_total, packed, weights, later, kriging, gram, kept):
-    kept[...] = kriging[...]
+    cells = kriging.shape[1]
+    source = lax.broadcasted_iota(jnp.int32, (cells, cells // 2), 0)
+    target = lax.broadcasted_iota(jnp.int32, (cells, cells // 2), 1)
+    for parity in range(2):
+        pick = jnp.where(source == 2 * target + parity, 1.0, 0.0).astype(BF16)
+        kept[pl.ds(parity * PILOT, PILOT), :] = dot(kriging[...], pick, NN).astype(BF16)
     mixed, gamma = weights[:RHS, :], weights[RHS:, :]
     rest = exact(packed[RHS:, :RHS], gamma) + exact(later[:, RHS:], mixed) - later[:, :RHS]
     gram[...] = symmetric(exact(jnp.transpose(gamma), rest)) * (1.0 / cell_total)
 
 
-def product_kernel(kriging, arrived, scale, sens, rows):
-    half = FX * LANE // 2
-    value = arrived[...].astype(F32)
-    rows[pl.ds(0, half, stride=2), :] = value
-    rows[pl.ds(1, half, stride=2), :] = swap(value)
-    high, rest = split(rows[...])
-    sens[...] = (dot(kriging[...], high, NN) + dot(kriging[...], rest, NN))[:, :RHS] * scale[...]
+def product_kernel(kriging, arrived, scale, sens):
+    high, rest = split(arrived[...])
+    product = dot(kriging[...], high, NN) + dot(kriging[...], rest, NN)
+    sens[...] = (product[:PILOT, :RHS] + product[PILOT:, RHS:]) * scale[...]
 
 
 def call(kernel, shapes, *operands, scratch=(), flops=1000000, place=pltpu.VMEM):
@@ -317,7 +322,7 @@
     )(*operands)
 
 
-EDGES = (((RHS, LANE), BF16), ((ROWS // 2 + 16, LANE), BF16), ((ROWS // 2, LANE), BF16), ((ROWS // 2, LANE), BF16))
+EDGES = (((RHS, LANE), BF16), ((RHS + 16, LANE), BF16), ((ROWS // 2, LANE), BF16), ((ROWS // 2, LANE), BF16))
 FIELD = ((ROWS, LANE), F32)
 
 
@@ -409,15 +414,14 @@
     heads = lax.all_to_all(heads, "dom", 0, 0, tiled=True).reshape(-1, LANE).astype(F32)
     gram, kriging = call(
         lambda *refs: gram_kernel(cell_total, *refs),
-        (((RHS, RHS), F32), (kriging.shape, BF16)),
+        (((RHS, RHS), F32), ((2 * PILOT, FX * LANE // 2), BF16)),
         *(packed, weights, later, kriging),
         flops=LONG,
     )
     (sens,) = call(
         product_kernel,
-        (((kriging.shape[0], RHS), F32),),
+        (((PILOT, RHS), F32),),
         *(kriging, heads, scale),
-        scratch=(scratch(FX * LANE),),
     )
     return sens, gram
 

time: 114 us -> 115 us (level)
  no operation moved by 1% of the time
where the time goes in v11:
time: 115 us; the launch traced here: 114 us
  blocking collectives  39.9 us (35%)
  starting transfers between devices  34.6 us (30%)
  waiting for transfers between devices  23.2 us (20%)
  Pallas kernels  13.9 us (12%)
    all_to_all x2, blocking collectives, trade(): lax.all_to_all(array, axes, 0, 0, axis_index_groups=groups, tiled=True)  39.9 us
    all_to_all x1, waiting for transfers between devices, shards(): lax.all_to_all(heads, 'dom', 0, 0, tiled=True).reshape(-1, LANE).astype(F32)  16.1 us
    pallas_call x8, Pallas kernels, call(): pl.pallas_call(kernel, out_shape=[jax.ShapeDtypeStruct(shape, kind) for s...  13.9 us
    ppermute x4, starting transfers between devices, along(): return (lax.ppermute(one, axis, first), two)  13.9 us
    ppermute x4, starting transfers between devices, along(): two = lax.ppermute(two, axis, second)  9.59 us
    all_to_all x1, waiting for transfers between devices, trade(): lax.all_to_all(array, axes, 0, 0, axis_index_groups=groups, tiled=True)  5.78 us
    all_to_all x1, starting transfers between devices, shards(): lax.all_to_all(heads, 'dom', 0, 0, tiled=True).reshape(-1, LANE).astype(F32)  5.64 us
    all_to_all x1, starting transfers between devices, trade(): lax.all_to_all(array, axes, 0, 0, axis_index_groups=groups, tiled=True)  5.41 us
  transfers between devices with their start and end apart: 10, of which 4 were waited for; matrix products, arithmetic and copies ran while one was open for 0% of the time, Pallas kernels for 3%

profile of v11, /device:TPU:1, one launch (start us, length us, event | category | flops | bytes accessed | tf_op | source)
XLA Modules:
  0.0 113.9 jit_solution(16531123578893765032)
XLA Ops:
  0.6 1.9 %shard_map.68 = (f32[512,128]{1,0:T(8,128)S(1)}, bf16[1024,128]{1,0:T(8,128)(2,1)S(1)}, bf16[1024,128]{1,0:T(8,128)(2,1)S(1)}, f32[512,128]{1,0:T(8,128)S(1)}, b...) custom-call(f32[16,4096]{1,0:T(8,128)} %pump_hbm.1, ...), custom_call_target="tpu_custom_call" | custom-call | flops 1000000 | bytes 1048576 | tf_op jit(solution)/shard_map/pallas_call | solution.py:314
  2.5 0.0 copy-start
  2.5 4.0 %collective-permute-start.2 = (bf16[256,128]{1,0:T(8,128)(2,1)S(1)}, bf16[256,128]{1,0:T(8,128)(2,1)S(1)}, u32[]{:S(2)}, u32[]{:S(2)}) collective-permute-start(bf16[256,128]{1,0:T(8,128)(2,1)S(1)} %get-tuple-element.28), channel_id=1, source_target_pairs={{0,1},{1,0},{2,3},{3,2},{4,5},{5,4},{6,7},{7,6},{8,9},{9,8},{10,11... | collective-permute-start | bytes 196616 | tf_op jit(solution)/shard_map/ppermute | solution.py:335
  6.6 0.7 collective-permute-start.3
  7.2 4.4 %collective-permute-start.1 = (bf16[80,128]{1,0:T(8,128)(2,1)S(1)}, bf16[80,128]{1,0:T(8,128)(2,1)S(1)}, u32[]{:S(2)}, u32[]{:S(2)}) collective-permute-start(bf16[80,128]{1,0:T(8,128)(2,1)S(1)} %get-tuple-element.27), channel_id=1, source_target_pairs={{4,8},{8,4},{12,16},{16,12},{20,24},{24,20},{28,32},{32,28},{36,40... | collective-permute-start | bytes 61448 | tf_op jit(solution)/shard_map/ppermute | solution.py:334
  11.6 2.9 %collective-permute-start = (bf16[64,128]{1,0:T(8,128)(2,1)S(1)}, bf16[64,128]{1,0:T(8,128)(2,1)S(1)}, u32[]{:S(2)}, u32[]{:S(2)}) collective-permute-start(bf16[64,128]{1,0:T(8,128)(2,1)S(1)} %get-tuple-element.26), channel_id=1, source_target_pairs={{0,4},{4,0},{8,12},{12,8},{16,20},{20,16},{24,28},{28,24},{32,36},... | collective-permute-start | bytes 49160 | tf_op jit(solution)/shard_map/ppermute | solution.py:335
  14.6 0.8 collective-permute-done.d1
  15.4 0.0 collective-permute-done.1.d2
  15.4 0.0 collective-permute-done.2.t1
  15.4 1.0 shard_map.69
  16.4 5.0 %collective-permute-start.6 = (bf16[256,128]{1,0:T(8,128)(2,1)S(1)}, bf16[256,128]{1,0:T(8,128)(2,1)S(1)}, u32[]{:S(2)}, u32[]{:S(2)}) collective-permute-start(bf16[256,128]{1,0:T(8,128)(2,1)S(1)} %get-tuple-element.34), channel_id=1, source_target_pairs={{0,1},{1,0},{2,3},{3,2},{4,5},{5,4},{6,7},{7,6},{8,9},{9,8},{10,11... | collective-permute-start | bytes 196616 | tf_op jit(solution)/shard_map/ppermute | solution.py:335
  21.5 0.7 collective-permute-start.7
  22.1 3.9 %collective-permute-start.5 = (bf16[80,128]{1,0:T(8,128)(2,1)S(1)}, bf16[80,128]{1,0:T(8,128)(2,1)S(1)}, u32[]{:S(2)}, u32[]{:S(2)}) collective-permute-start(bf16[80,128]{1,0:T(8,128)(2,1)S(1)} %get-tuple-element.33), channel_id=1, source_target_pairs={{4,8},{8,4},{12,16},{16,12},{20,24},{24,20},{28,32},{32,28},{36,40... | collective-permute-start | bytes 61448 | tf_op jit(solution)/shard_map/ppermute | solution.py:334
  26.0 1.9 %collective-permute-start.4 = (bf16[64,128]{1,0:T(8,128)(2,1)S(1)}, bf16[64,128]{1,0:T(8,128)(2,1)S(1)}, u32[]{:S(2)}, u32[]{:S(2)}) collective-permute-start(bf16[64,128]{1,0:T(8,128)(2,1)S(1)} %get-tuple-element.32), channel_id=1, source_target_pairs={{0,4},{4,0},{8,12},{12,8},{16,20},{20,16},{24,28},{28,24},{32,36},... | collective-permute-start | bytes 49160 | tf_op jit(solution)/shard_map/ppermute | solution.py:335
  27.9 0.7 shard_map.70.base
  28.6 0.5 collective-permute-done.4.d1
  29.1 0.0 collective-permute-done.5.d2
  29.1 0.0 collective-permute-done.6.t1
  29.1 0.0 collective-permute-done.7.t2
  29.1 1.2 %shard_map.71 = f32[128,128]{1,0:T(8,128)S(1)} custom-call(f32[512,128]{1,0:T(8,128)S(1)} %get-tuple-element.30.v.ap, f32[512,128]{1,0:T(8,128)S(1)} %get-tuple-element.31.u, bf16[1024,128]{1,0:T(8,128)(2,1)S(1)} %get-tuple-element.24.sh, bf16[1024,128]{1,0:T(8,128)(2,1)S(1)} %get-tuple-element.25.sl, f32[16,64]{1,0:T(8,128)S(1)} %copy-done, ...), custom_call_target="tpu_custom_call" | custom-call | flops 1000000 | bytes 1048576 | tf_op jit(solution)/shard_map/pallas_call | solution.py:314
  30.3 21.7 %all_to_all.20 = f32[32,4,128]{2,1,0:T(4,128)S(1)} all-to-all(f32[32,4,128]{2,1,0:T(4,128)S(1)} %bitcast.7), channel_id=1, replica_groups={{0,1,2,3,4,5,6,7,128,129,130,131,132,133,134,135,256,257,258,259,260,26..., dimensions={0} | all-to-all | bytes 131072 | tf_op jit(solution)/shard_map/all_to_all | solution.py:365
  52.0 18.3 %all_to_all.21 = f32[16,4,128]{2,1,0:T(4,128)S(1)} all-to-all(f32[16,4,128]{2,1,0:T(4,128)S(1)} %broadcast_in_dim.4), channel_id=1, replica_groups={{0,8,16,24,32,40,48,56,64,72,80,88,96,104,112,120},{1,9,17,25,33,41,49,..., dimensions={0} | all-to-all | bytes 65536 | tf_op jit(solution)/shard_map/all_to_all | solution.py:365
  70.3 0.6 broadcast_in_dim.5
  70.9 5.4 %all-to-all-start.2 = ((f32[32,4,128]{2,1,0:T(4,128)}), f32[32,4,128]{2,1,0:T(4,128)S(1)}, u32[]{:S(2)}, u32[]{:S(2)}) async-start(f32[32,4,128]{2,1,0:T(4,128)} %broadcast_in_dim.5), calls=%async_computation.2 | async-start | bytes 131072 | tf_op jit(solution)/shard_map/all_to_all | solution.py:365
  76.4 1.5 %shard_map.72.refs_1_ = bf16[1024,256]{1,0:T(8,128)(2,1)S(1)} custom-call(s32[1,1024]{1,0:T(1,128)S(1)} %copy-done.2, f32[512,128]{1,0:T(8,128)S(1)} %get-tuple-element.22.v.p, f32[512,128]{1,0:T(8,128)S(1)} %get-tuple-element.30.v.ap), custom_call_target="tpu_custom_call" | custom-call | flops 99999997952 | bytes 1048576 | tf_op jit(solution)/shard_map/pallas_call | solution.py:314
  77.9 5.8 %all-to-all-done.2 = f32[32,4,128]{2,1,0:T(4,128)S(1)} async-done(((f32[32,4,128]{2,1,0:T(4,128)}), f32[32,4,128]{2,1,0:T(4,128)S(1)}, u32[]{:S(2)}, u32[]{:S(2)}) %all-to-all-start.2) | async-done | bytes 65568 | tf_op jit(solution)/shard_map/all_to_all | solution.py:365
  83.7 5.5 %shard_map.73 = (f32[512,128]{1,0:T(8,128)S(1)}, f32[1,64]{1,0:T(1,128)S(1)}, f32[128,64]{1,0:T(8,128)S(1)}, f32[64,128]{1,0:T(8,128)S(1)}) custom-call(f32[128,128]{1,0:T(8,128)S(1)} %bitcast.5, bf16[1024,256]{1,0:T(8,128)(2,1)S(1)} %shard_map.72.refs_1_), custom_call_target="tpu_custom_call" | custom-call | flops 1000000 | bytes 1048576 | tf_op jit(solution)/shard_map/pallas_call | solution.py:314
  89.2 0.7 convert_element_type.8
  89.8 5.6 %all-to-all-start.3 = ((f16[128,4,128]{2,1,0:T(4,128)(2,1)}), f16[128,4,128]{2,1,0:T(4,128)(2,1)S(1)}, u32[]{:S(2)}, u32[]{:S(2)}) async-start(f16[128,4,128]{2,1,0:T(4,128)(2,1)} %bitcast.2), calls=%async_computation.3 | async-start | bytes 262144 | tf_op jit(solution)/shard_map/all_to_all | solution.py:414
  95.5 1.4 %shard_map.74 = (f32[64,64]{1,0:T(8,128)}, bf16[32,512]{1,0:T(8,128)(2,1)S(1)}) custom-call(f32[128,128]{1,0:T(8,128)S(1)} %bitcast.6, f32[128,64]{1,0:T(8,128)S(1)} %get-tuple-element.36.refs_1_, f32[64,128]{1,0:T(8,128)S(1)} %get-tuple-element.37.refs_2_, bf16[16,1024]{1,0:T(8,128)(2,1)S(1)} %copy-done.1), custom_call_target="tpu_custom_call" | custom-call | flops 99999997952 | bytes 1048576 | tf_op jit(solution)/shard_map/pallas_call | solution.py:314
  96.9 16.1 %all-to-all-done.3 = f16[128,4,128]{2,1,0:T(4,128)(2,1)S(1)} async-done(((f16[128,4,128]{2,1,0:T(4,128)(2,1)}), f16[128,4,128]{2,1,0:T(4,128)(2,1)S(1)}, u32[]{:S(2)}, u32[]{:S(2)}) %all-to-all-start.3) | async-done | bytes 131104 | tf_op jit(solution)/shard_map/all_to_all | solution.py:414
  113.0 0.9 shard_map.75
  (10 shorter events, 0.1 us)
Async XLA Ops:
  2.5 12.9 %copy-start = (f32[16,64]{1,0:T(8,128)S(1)}, f32[16,64]{1,0:T(8,128)}, u32[]{:S(2)}) copy-start(f32[16,64]{1,0:T(8,128)} %stor.3) | copy-start | bytes 12292
  2.5 12.9 %collective-permute-start.2 = (bf16[256,128]{1,0:T(8,128)(2,1)S(1)}, bf16[256,128]{1,0:T(8,128)(2,1)S(1)}, u32[]{:S(2)}, u32[]{:S(2)}) collective-permute-start(bf16[256,128]{1,0:T(8,128)(2,1)S(1)} %get-tuple-element.28), channel_id=1, source_target_pairs={{0,1},{1,0},{2,3},{3,2},{4,5},{5,4},{6,7},{7,6},{8,9},{9,8},{10,11... | collective-permute-start | bytes 196616 | tf_op jit(solution)/shard_map/ppermute | solution.py:335
  6.6 8.8 %collective-permute-start.3 = (bf16[256,128]{1,0:T(8,128)(2,1)S(1)}, bf16[256,128]{1,0:T(8,128)(2,1)S(1)}, u32[]{:S(2)}, u32[]{:S(2)}) collective-permute-start(bf16[256,128]{1,0:T(8,128)(2,1)S(1)} %get-tuple-element.29), channel_id=1, source_target_pairs={{1,2},{2,1},{5,6},{6,5},{9,10},{10,9},{13,14},{14,13},{17,18},{18,... | collective-permute-start | bytes 196616 | tf_op jit(solution)/shard_map/ppermute | solution.py:334
  7.2 8.2 %collective-permute-start.1 = (bf16[80,128]{1,0:T(8,128)(2,1)S(1)}, bf16[80,128]{1,0:T(8,128)(2,1)S(1)}, u32[]{:S(2)}, u32[]{:S(2)}) collective-permute-start(bf16[80,128]{1,0:T(8,128)(2,1)S(1)} %get-tuple-element.27), channel_id=1, source_target_pairs={{4,8},{8,4},{12,16},{16,12},{20,24},{24,20},{28,32},{32,28},{36,40... | collective-permute-start | bytes 61448 | tf_op jit(solution)/shard_map/ppermute | solution.py:334
  11.6 3.8 %collective-permute-start = (bf16[64,128]{1,0:T(8,128)(2,1)S(1)}, bf16[64,128]{1,0:T(8,128)(2,1)S(1)}, u32[]{:S(2)}, u32[]{:S(2)}) collective-permute-start(bf16[64,128]{1,0:T(8,128)(2,1)S(1)} %get-tuple-element.26), channel_id=1, source_target_pairs={{0,4},{4,0},{8,12},{12,8},{16,20},{20,16},{24,28},{28,24},{32,36},... | collective-permute-start | bytes 49160 | tf_op jit(solution)/shard_map/ppermute | solution.py:335
  16.4 12.7 %collective-permute-start.6 = (bf16[256,128]{1,0:T(8,128)(2,1)S(1)}, bf16[256,128]{1,0:T(8,128)(2,1)S(1)}, u32[]{:S(2)}, u32[]{:S(2)}) collective-permute-start(bf16[256,128]{1,0:T(8,128)(2,1)S(1)} %get-tuple-element.34), channel_id=1, source_target_pairs={{0,1},{1,0},{2,3},{3,2},{4,5},{5,4},{6,7},{7,6},{8,9},{9,8},{10,11... | collective-permute-start | bytes 196616 | tf_op jit(solution)/shard_map/ppermute | solution.py:335
  21.5 7.6 %collective-permute-start.7 = (bf16[256,128]{1,0:T(8,128)(2,1)S(1)}, bf16[256,128]{1,0:T(8,128)(2,1)S(1)}, u32[]{:S(2)}, u32[]{:S(2)}) collective-permute-start(bf16[256,128]{1,0:T(8,128)(2,1)S(1)} %get-tuple-element.35), channel_id=1, source_target_pairs={{1,2},{2,1},{5,6},{6,5},{9,10},{10,9},{13,14},{14,13},{17,18},{18,... | collective-permute-start | bytes 196616 | tf_op jit(solution)/shard_map/ppermute | solution.py:334
  22.1 7.0 %collective-permute-start.5 = (bf16[80,128]{1,0:T(8,128)(2,1)S(1)}, bf16[80,128]{1,0:T(8,128)(2,1)S(1)}, u32[]{:S(2)}, u32[]{:S(2)}) collective-permute-start(bf16[80,128]{1,0:T(8,128)(2,1)S(1)} %get-tuple-element.33), channel_id=1, source_target_pairs={{4,8},{8,4},{12,16},{16,12},{20,24},{24,20},{28,32},{32,28},{36,40... | collective-permute-start | bytes 61448 | tf_op jit(solution)/shard_map/ppermute | solution.py:334
  26.0 3.1 %collective-permute-start.4 = (bf16[64,128]{1,0:T(8,128)(2,1)S(1)}, bf16[64,128]{1,0:T(8,128)(2,1)S(1)}, u32[]{:S(2)}, u32[]{:S(2)}) collective-permute-start(bf16[64,128]{1,0:T(8,128)(2,1)S(1)} %get-tuple-element.32), channel_id=1, source_target_pairs={{0,4},{4,0},{8,12},{12,8},{16,20},{20,16},{24,28},{28,24},{32,36},... | collective-permute-start | bytes 49160 | tf_op jit(solution)/shard_map/ppermute | solution.py:335
  70.9 5.4 %copy-start.2 = (s32[1,1024]{1,0:T(1,128)S(1)}, s32[1,1024]{1,0:T(1,128)}, u32[]{:S(2)}) copy-start(s32[1,1024]{1,0:T(1,128)} %order.1) | copy-start | bytes 12292
  70.9 12.8 %all-to-all-start.2 = ((f32[32,4,128]{2,1,0:T(4,128)}), f32[32,4,128]{2,1,0:T(4,128)S(1)}, u32[]{:S(2)}, u32[]{:S(2)}) async-start(f32[32,4,128]{2,1,0:T(4,128)} %broadcast_in_dim.5), calls=%async_computation.2 | async-start | bytes 131072 | tf_op jit(solution)/shard_map/all_to_all | solution.py:365
  89.8 5.7 %copy-start.1 = (bf16[16,1024]{1,0:T(8,128)(2,1)S(1)}, bf16[16,1024]{1,0:T(8,128)(2,1)}, u32[]{:S(2)}) copy-start(bf16[16,1024]{1,0:T(8,128)(2,1)} %refs_3_.1) | copy-start | bytes 98308
  89.8 23.2 %all-to-all-start.3 = ((f16[128,4,128]{2,1,0:T(4,128)(2,1)}), f16[128,4,128]{2,1,0:T(4,128)(2,1)S(1)}, u32[]{:S(2)}, u32[]{:S(2)}) async-start(f16[128,4,128]{2,1,0:T(4,128)(2,1)} %bitcast.2), calls=%async_computation.3 | async-start | bytes 262144 | tf_op jit(solution)/shard_map/all_to_all | solution.py:414

commit v12 on v10

--- a/solution.py
+++ b/solution.py
@@ -158,7 +158,13 @@
     write_edges(spread, *edges)
 
 
-def deal_kernel(order, v, ap, cells, table):
+def deal_kernel(order, v, ap, kriging, cells, kept, table):
+    count = kriging.shape[1]
+    source = lax.broadcasted_iota(jnp.int32, (count, count // 2), 0)
+    target = lax.broadcasted_iota(jnp.int32, (count, count // 2), 1)
+    for parity in range(2):
+        pick = jnp.where(source == 2 * target + parity, 1.0, 0.0).astype(BF16)
+        kept[pl.ds(parity * PILOT, PILOT), :] = dot(kriging[...], pick, NN).astype(BF16)
     for x in range(FX):
         high, rest = split(jnp.concatenate([v[part(x), :], ap[part(x), :]], axis=0))
         table[: 2 * RHS, x * LANE : (x + 1) * LANE] = high
@@ -297,22 +303,13 @@
     later[...] = jnp.concatenate([m2, m3], axis=1)
 
 
-def gram_kernel(cell_total, packed, weights, later, kriging, gram, kept):
-    cells = kriging.shape[1]
-    source = lax.broadcasted_iota(jnp.int32, (cells, cells // 2), 0)
-    target = lax.broadcasted_iota(jnp.int32, (cells, cells // 2), 1)
-    for parity in range(2):
-        pick = jnp.where(source == 2 * target + parity, 1.0, 0.0).astype(BF16)
-        kept[pl.ds(parity * PILOT, PILOT), :] = dot(kriging[...], pick, NN).astype(BF16)
+def product_kernel(cell_total, kriging, arrived, scale, packed, weights, later, sens, gram):
+    high, rest = split(arrived[...])
+    product = dot(kriging[...], high, NN) + dot(kriging[...], rest, NN)
+    sens[...] = (product[:PILOT, :RHS] + product[PILOT:, RHS:]) * scale[...]
     mixed, gamma = weights[:RHS, :], weights[RHS:, :]
     rest = exact(packed[RHS:, :RHS], gamma) + exact(later[:, RHS:], mixed) - later[:, :RHS]
     gram[...] = symmetric(exact(jnp.transpose(gamma), rest)) * (1.0 / cell_total)
-
-
-def product_kernel(kriging, arrived, scale, sens):
-    high, rest = split(arrived[...])
-    product = dot(kriging[...], high, NN) + dot(kriging[...], rest, NN)
-    sens[...] = (product[:PILOT, :RHS] + product[PILOT:, RHS:]) * scale[...]
 
 
 def call(kernel, shapes, *operands, scratch=(), flops=1000000, place=pltpu.VMEM):
@@ -397,10 +394,10 @@
     (packed,) = call(
         third_kernel, (((2 * RHS, LANE), F32),), ap, u, sh, sl, storage, *halo, base
     )
-    (cells,) = call(
+    cells, kriging = call(
         deal_kernel,
-        (((FX * LANE, 4 * RHS), BF16),),
-        *(tile_order, p, ap),
+        (((FX * LANE, 4 * RHS), BF16), ((2 * PILOT, FX * LANE // 2), BF16)),
+        *(tile_order, p, ap, kriging),
         scratch=(pltpu.VMEM((4 * RHS, FX * LANE), BF16),),
         flops=LONG,
     )
@@ -413,16 +410,10 @@
     )
     heads = heads.astype(jnp.float16).reshape(groups, -1, LANE)
     heads = lax.all_to_all(heads, "dom", 0, 0, tiled=True).reshape(-1, LANE).astype(F32)
-    gram, kriging = call(
-        lambda *refs: gram_kernel(cell_total, *refs),
-        (((RHS, RHS), F32), ((2 * PILOT, FX * LANE // 2), BF16)),
-        *(packed, weights, later, kriging),
-        flops=LONG,
-    )
-    (sens,) = call(
-        product_kernel,
-        (((PILOT, RHS), F32),),
-        *(kriging, heads, scale),
+    sens, gram = call(
+        lambda *refs: product_kernel(cell_total, *refs),
+        (((PILOT, RHS), F32), ((RHS, RHS), F32)),
+        *(kriging, heads, scale, packed, weights, later),
     )
     return sens, gram
 

time: 114 us -> 113 us (level)
  blocking collectives: 40.1 us -> 62.4 us
  waiting for transfers between devices: 23.2 us -> 6.73 us
  starting transfers between devices: 33.1 us -> 27.5 us
    all_to_all x0 -> x1, blocking collectives: none -> 22.3 us  [shards(): lax.all_to_all(heads, 'dom', 0, 0, tiled=True).reshape(-1, LANE).astype(F32)]
    all_to_all x1 -> x0, waiting for transfers between devices: 16.1 us -> none  [shards(): lax.all_to_all(heads, 'dom', 0, 0, tiled=True).reshape(-1, LANE).astype(F32)]
    all_to_all x1 -> x0, starting transfers between devices: 5.64 us -> none  [shards(): lax.all_to_all(heads, 'dom', 0, 0, tiled=True).reshape(-1, LANE).astype(F32)]
    pallas_call x8 -> x7, Pallas kernels: 15.1 us -> 14.3 us  [call(): pl.pallas_call(kernel, out_shape=[jax.ShapeDtypeStruct(shape, kind) for s...]
  transfers between devices with their start and end apart: 8 -> 7, of which waited for: 4 -> 3; matrix products, arithmetic and copies ran while one was open for 0% -> 0% of each run, Pallas kernels for 3% -> 2%
where the time goes in v12:
time: 113 us; the launch traced here: 112 us
  blocking collectives  62.4 us (55%)
  starting transfers between devices  27.5 us (24%)
  Pallas kernels  14.3 us (13%)
  waiting for transfers between devices  6.73 us (6%)
    all_to_all x2, blocking collectives, trade(): lax.all_to_all(array, axes, 0, 0, axis_index_groups=groups, tiled=True)  40.1 us
    all_to_all x1, blocking collectives, shards(): lax.all_to_all(heads, 'dom', 0, 0, tiled=True).reshape(-1, LANE).astype(F32)  22.3 us
    pallas_call x7, Pallas kernels, call(): pl.pallas_call(kernel, out_shape=[jax.ShapeDtypeStruct(shape, kind) for s...  14.3 us
    all_to_all x2, starting transfers between devices, exchange(): t = lax.all_to_all(t, 'tile', 0, 0, tiled=True)  9.62 us
    ppermute x2, starting transfers between devices, exchange(): d2 = lax.ppermute(d2, 'dom', second)  7.2 us
    all_to_all x1, waiting for transfers between devices, trade(): lax.all_to_all(array, axes, 0, 0, axis_index_groups=groups, tiled=True)  5.42 us
    all_to_all x1, starting transfers between devices, trade(): lax.all_to_all(array, axes, 0, 0, axis_index_groups=groups, tiled=True)  5.41 us
    ppermute x2, starting transfers between devices, exchange(): return (lax.ppermute(d1, 'dom', first), d2, t)  5.27 us
  transfers between devices with their start and end apart: 7, of which 3 were waited for; matrix products, arithmetic and copies ran while one was open for 0% of the time, Pallas kernels for 2%

profile of v12, /device:TPU:1, one launch (start us, length us, event | category | flops | bytes accessed | tf_op | source)
XLA Modules:
  0.0 112.5 jit_solution(5705870710820071581)
XLA Ops:
  0.6 2.6 %shard_map.68 = (f32[512,128]{1,0:T(8,128)S(1)}, bf16[1024,128]{1,0:T(8,128)(2,1)S(1)}, bf16[1024,128]{1,0:T(8,128)(2,1)S(1)}, f32[512,128]{1,0:T(8,128)S(1)}, b...) custom-call(f32[16,4096]{1,0:T(8,128)} %pump_hbm.1, f32[16,4096]{1,0:T(8,128)} %coup_hbm.1), custom_call_target="tpu_custom_call" | custom-call | flops 1000000 | bytes 1048576 | tf_op jit(solution)/shard_map/pallas_call | solution.py:316
  3.2 5.0 %all-to-all-start = ((bf16[4,256,128]{2,1,0:T(8,128)(2,1)}), bf16[4,256,128]{2,1,0:T(8,128)(2,1)S(1)}, u32[]{:S(2)}, u32[]{:S(2)}) async-start(bf16[4,256,128]{2,1,0:T(8,128)(2,1)} %get-tuple-element.26), calls=%async_computation | async-start | bytes 524288 | tf_op jit(solution)/shard_map/all_to_all | solution.py:335
  8.2 0.0 copy-start
  8.2 4.5 %collective-permute-start.1 = (bf16[80,128]{1,0:T(8,128)(2,1)S(1)}, bf16[80,128]{1,0:T(8,128)(2,1)S(1)}, u32[]{:S(2)}, u32[]{:S(2)}) collective-permute-start(bf16[80,128]{1,0:T(8,128)(2,1)S(1)} %get-tuple-element.25), channel_id=1, source_target_pairs={{4,8},{8,4},{12,16},{16,12},{20,24},{24,20},{28,32},{32,28},{36,40... | collective-permute-start | bytes 61448 | tf_op jit(solution)/shard_map/ppermute | solution.py:336
  12.7 3.4 %collective-permute-start = (bf16[64,128]{1,0:T(8,128)(2,1)S(1)}, bf16[64,128]{1,0:T(8,128)(2,1)S(1)}, u32[]{:S(2)}, u32[]{:S(2)}) collective-permute-start(bf16[64,128]{1,0:T(8,128)(2,1)S(1)} %get-tuple-element.24), channel_id=1, source_target_pairs={{0,4},{4,0},{8,12},{12,8},{16,20},{20,16},{24,28},{28,24},{32,36},... | collective-permute-start | bytes 49160 | tf_op jit(solution)/shard_map/ppermute | solution.py:337
  16.1 0.8 collective-permute-done.d1
  16.9 0.0 collective-permute-done.1.d2
  16.9 0.0 all-to-all-done.t
  16.9 0.0 copy-done
  16.9 1.6 %shard_map.69 = (f32[512,128]{1,0:T(8,128)S(1)}, f32[512,128]{1,0:T(8,128)S(1)}, bf16[64,128]{1,0:T(8,128)(2,1)S(1)}, bf16[80,128]{1,0:T(8,128)(2,1)S(1)}, bf16[4,256,128]{2,1,0:T(8,128)(2,1)}) custom-call(f32[512,128]{1,0:T(8,128)S(1)} %get-tuple-element.20.v.p, f32[512,128]{1,0:T(8,128)S(1)} %get-tuple-element.21.u, ...), custom_call_target="tpu_custom_call" | custom-call | flops 1000000 | bytes 1048576 | tf_op jit(solution)/shard_map/pallas_call | solution.py:316
  18.5 4.6 %all-to-all-start.1 = ((bf16[4,256,128]{2,1,0:T(8,128)(2,1)}), bf16[4,256,128]{2,1,0:T(8,128)(2,1)S(1)}, u32[]{:S(2)}, u32[]{:S(2)}) async-start(bf16[4,256,128]{2,1,0:T(8,128)(2,1)} %get-tuple-element.32), calls=%async_computation.1 | async-start | bytes 524288 | tf_op jit(solution)/shard_map/all_to_all | solution.py:335
  23.1 2.7 %collective-permute-start.3 = (bf16[80,128]{1,0:T(8,128)(2,1)S(1)}, bf16[80,128]{1,0:T(8,128)(2,1)S(1)}, u32[]{:S(2)}, u32[]{:S(2)}) collective-permute-start(bf16[80,128]{1,0:T(8,128)(2,1)S(1)} %get-tuple-element.31), channel_id=1, source_target_pairs={{4,8},{8,4},{12,16},{16,12},{20,24},{24,20},{28,32},{32,28},{36,40... | collective-permute-start | bytes 61448 | tf_op jit(solution)/shard_map/ppermute | solution.py:336
  25.8 1.9 %collective-permute-start.2 = (bf16[64,128]{1,0:T(8,128)(2,1)S(1)}, bf16[64,128]{1,0:T(8,128)(2,1)S(1)}, u32[]{:S(2)}, u32[]{:S(2)}) collective-permute-start(bf16[64,128]{1,0:T(8,128)(2,1)S(1)} %get-tuple-element.30), channel_id=1, source_target_pairs={{0,4},{4,0},{8,12},{12,8},{16,20},{20,16},{24,28},{28,24},{32,36},... | collective-permute-start | bytes 49160 | tf_op jit(solution)/shard_map/ppermute | solution.py:337
  27.7 0.7 shard_map.71.base
  28.4 0.5 collective-permute-done.2.d1
  28.9 0.0 collective-permute-done.3.d2
  28.9 0.0 all-to-all-done.1.t
  28.9 1.2 %shard_map.72 = f32[128,128]{1,0:T(8,128)S(1)} custom-call(f32[512,128]{1,0:T(8,128)S(1)} %get-tuple-element.27.ap.v, f32[512,128]{1,0:T(8,128)S(1)} %get-tuple-element.29.u, bf16[1024,128]{1,0:T(8,128)(2,1)S(1)} %get-tuple-element.22.sh, bf16[1024,128]{1,0:T(8,128)(2,1)S(1)} %get-tuple-element.23.sl, f32[16,64]{1,0:T(8,128)S(1)} %copy-done, ...), custom_call_target="tpu_custom_call" | custom-call | flops 1000000 | bytes 1048576 | tf_op jit(solution)/shard_map/pallas_call | solution.py:316
  30.1 21.9 %all_to_all.30 = f32[32,4,128]{2,1,0:T(4,128)S(1)} all-to-all(f32[32,4,128]{2,1,0:T(4,128)S(1)} %bitcast.7), channel_id=1, replica_groups={{0,1,2,3,4,5,6,7,128,129,130,131,132,133,134,135,256,257,258,259,260,26..., dimensions={0} | all-to-all | bytes 131072 | tf_op jit(solution)/shard_map/all_to_all | solution.py:363
  52.0 18.2 %all_to_all.31 = f32[16,4,128]{2,1,0:T(4,128)S(1)} all-to-all(f32[16,4,128]{2,1,0:T(4,128)S(1)} %broadcast_in_dim.4), channel_id=1, replica_groups={{0,8,16,24,32,40,48,56,64,72,80,88,96,104,112,120},{1,9,17,25,33,41,49,..., dimensions={0} | all-to-all | bytes 65536 | tf_op jit(solution)/shard_map/all_to_all | solution.py:363
  70.2 0.6 broadcast_in_dim.5
  70.9 0.0 copy-start.1
  70.9 0.0 copy-start.2
  70.9 5.4 %all-to-all-start.4 = ((f32[32,4,128]{2,1,0:T(4,128)}), f32[32,4,128]{2,1,0:T(4,128)S(1)}, u32[]{:S(2)}, u32[]{:S(2)}) async-start(f32[32,4,128]{2,1,0:T(4,128)} %broadcast_in_dim.5), calls=%async_computation.4 | async-start | bytes 131072 | tf_op jit(solution)/shard_map/all_to_all | solution.py:363
  76.3 0.0 copy-done.1
  76.3 0.0 copy-done.2
  76.3 1.9 %shard_map.70 = (bf16[1024,256]{1,0:T(8,128)(2,1)S(1)}, bf16[32,512]{1,0:T(8,128)(2,1)S(1)}) custom-call(s32[1,1024]{1,0:T(1,128)S(1)} %copy-done.2, f32[512,128]{1,0:T(8,128)S(1)} %get-tuple-element.20.v.p, f32[512,128]{1,0:T(8,128)S(1)} %get-tuple-element.27.ap.v, bf16[16,1024]{1,0:T(8,128)(2,1)S(1)} %copy-done.1), custom_call_target="tpu_custom_call" | custom-call | flops 99999997952 | bytes 1048576 | tf_op jit(solution)/shard_map/pallas_call | solution.py:316
  78.2 5.4 %all-to-all-done.4 = f32[32,4,128]{2,1,0:T(4,128)S(1)} async-done(((f32[32,4,128]{2,1,0:T(4,128)}), f32[32,4,128]{2,1,0:T(4,128)S(1)}, u32[]{:S(2)}, u32[]{:S(2)}) %all-to-all-start.4) | async-done | bytes 65568 | tf_op jit(solution)/shard_map/all_to_all | solution.py:363
  83.6 5.3 %shard_map.73 = (f32[512,128]{1,0:T(8,128)S(1)}, f32[1,64]{1,0:T(1,128)S(1)}, f32[128,64]{1,0:T(8,128)S(1)}, f32[64,128]{1,0:T(8,128)S(1)}) custom-call(f32[128,128]{1,0:T(8,128)S(1)} %bitcast.5, bf16[1024,256]{1,0:T(8,128)(2,1)S(1)} %get-tuple-element.33.refs_1_), custom_call_target="tpu_custom_call" | custom-call | flops 1000000 | bytes 1048576 | tf_op jit(solution)/shard_map/pallas_call | solution.py:316
  89.0 22.3 %all_to_all.32 = f16[128,4,128]{2,1,0:T(4,128)(2,1)S(1)} all-to-all(f16[128,4,128]{2,1,0:T(4,128)(2,1)S(1)} %bitcast.8), channel_id=1, replica_groups=mesh['dom'=128,'tile'=4] {'dom'}, dimensions={0} | all-to-all | bytes 262144 | tf_op jit(solution)/shard_map/all_to_all | solution.py:412
  111.3 1.2 %shard_map.74 = (f32[16,64]{1,0:T(8,128)}, f32[64,64]{1,0:T(8,128)}) custom-call(bf16[32,512]{1,0:T(8,128)(2,1)S(1)} %get-tuple-element.28.refs_0_, f32[512,128]{1,0:T(8,128)S(1)} %convert.1.refs_1_, f32[1,64]{1,0:T(1,128)S(1)} %get-tuple-element.35.refs_2_, f32[128,128]{1,0:T(8,128)S(1)} %bitcast.6, f32[128,64]{1,0:T(8,128)S(1)} %get-tuple-element.36.refs_4_, ...), custom_call_target="tpu_custom_call" | custom-call | flops 1000000 | bytes 1048576 | tf_op jit(solution)/shard_map/pallas_call | solution.py:316
  (5 shorter events, 0.1 us)
Async XLA Ops:
  3.2 13.7 %all-to-all-start = ((bf16[4,256,128]{2,1,0:T(8,128)(2,1)}), bf16[4,256,128]{2,1,0:T(8,128)(2,1)S(1)}, u32[]{:S(2)}, u32[]{:S(2)}) async-start(bf16[4,256,128]{2,1,0:T(8,128)(2,1)} %get-tuple-element.26), calls=%async_computation | async-start | bytes 524288 | tf_op jit(solution)/shard_map/all_to_all | solution.py:335
  8.2 8.7 %copy-start = (f32[16,64]{1,0:T(8,128)S(1)}, f32[16,64]{1,0:T(8,128)}, u32[]{:S(2)}) copy-start(f32[16,64]{1,0:T(8,128)} %stor.3) | copy-start | bytes 12292
  8.2 8.7 %collective-permute-start.1 = (bf16[80,128]{1,0:T(8,128)(2,1)S(1)}, bf16[80,128]{1,0:T(8,128)(2,1)S(1)}, u32[]{:S(2)}, u32[]{:S(2)}) collective-permute-start(bf16[80,128]{1,0:T(8,128)(2,1)S(1)} %get-tuple-element.25), channel_id=1, source_target_pairs={{4,8},{8,4},{12,16},{16,12},{20,24},{24,20},{28,32},{32,28},{36,40... | collective-permute-start | bytes 61448 | tf_op jit(solution)/shard_map/ppermute | solution.py:336
  12.7 4.2 %collective-permute-start = (bf16[64,128]{1,0:T(8,128)(2,1)S(1)}, bf16[64,128]{1,0:T(8,128)(2,1)S(1)}, u32[]{:S(2)}, u32[]{:S(2)}) collective-permute-start(bf16[64,128]{1,0:T(8,128)(2,1)S(1)} %get-tuple-element.24), channel_id=1, source_target_pairs={{0,4},{4,0},{8,12},{12,8},{16,20},{20,16},{24,28},{28,24},{32,36},... | collective-permute-start | bytes 49160 | tf_op jit(solution)/shard_map/ppermute | solution.py:337
  18.5 10.4 %all-to-all-start.1 = ((bf16[4,256,128]{2,1,0:T(8,128)(2,1)}), bf16[4,256,128]{2,1,0:T(8,128)(2,1)S(1)}, u32[]{:S(2)}, u32[]{:S(2)}) async-start(bf16[4,256,128]{2,1,0:T(8,128)(2,1)} %get-tuple-element.32), calls=%async_computation.1 | async-start | bytes 524288 | tf_op jit(solution)/shard_map/all_to_all | solution.py:335
  23.1 5.8 %collective-permute-start.3 = (bf16[80,128]{1,0:T(8,128)(2,1)S(1)}, bf16[80,128]{1,0:T(8,128)(2,1)S(1)}, u32[]{:S(2)}, u32[]{:S(2)}) collective-permute-start(bf16[80,128]{1,0:T(8,128)(2,1)S(1)} %get-tuple-element.31), channel_id=1, source_target_pairs={{4,8},{8,4},{12,16},{16,12},{20,24},{24,20},{28,32},{32,28},{36,40... | collective-permute-start | bytes 61448 | tf_op jit(solution)/shard_map/ppermute | solution.py:336
  25.8 3.1 %collective-permute-start.2 = (bf16[64,128]{1,0:T(8,128)(2,1)S(1)}, bf16[64,128]{1,0:T(8,128)(2,1)S(1)}, u32[]{:S(2)}, u32[]{:S(2)}) collective-permute-start(bf16[64,128]{1,0:T(8,128)(2,1)S(1)} %get-tuple-element.30), channel_id=1, source_target_pairs={{0,4},{4,0},{8,12},{12,8},{16,20},{20,16},{24,28},{28,24},{32,36},... | collective-permute-start | bytes 49160 | tf_op jit(solution)/shard_map/ppermute | solution.py:337
  70.9 5.4 %copy-start.1 = (bf16[16,1024]{1,0:T(8,128)(2,1)S(1)}, bf16[16,1024]{1,0:T(8,128)(2,1)}, u32[]{:S(2)}) copy-start(bf16[16,1024]{1,0:T(8,128)(2,1)} %kriging.1) | copy-start | bytes 98308
  70.9 5.4 %copy-start.2 = (s32[1,1024]{1,0:T(1,128)S(1)}, s32[1,1024]{1,0:T(1,128)}, u32[]{:S(2)}) copy-start(s32[1,1024]{1,0:T(1,128)} %order.1) | copy-start | bytes 12292
  70.9 12.8 %all-to-all-start.4 = ((f32[32,4,128]{2,1,0:T(4,128)}), f32[32,4,128]{2,1,0:T(4,128)S(1)}, u32[]{:S(2)}, u32[]{:S(2)}) async-start(f32[32,4,128]{2,1,0:T(4,128)} %broadcast_in_dim.5), calls=%async_computation.4 | async-start | bytes 131072 | tf_op jit(solution)/shard_map/all_to_all | solution.py:363

commit v13 on v8

--- a/solution.py
+++ b/solution.py
@@ -8,6 +8,7 @@
 RHS = 64
 CB = 64
 FX = 8
+PILOT = 16
 LANE = 128
 ROWS = FX * RHS
 F32 = jnp.float32
@@ -151,7 +152,13 @@
     write_edges(spread, *edges)
 
 
-def deal_kernel(order, v, ap, cells, table):
+def deal_kernel(order, v, ap, kriging, cells, kept, table):
+    count = kriging.shape[1]
+    source = lax.broadcasted_iota(jnp.int32, (count, count // 2), 0)
+    target = lax.broadcasted_iota(jnp.int32, (count, count // 2), 1)
+    for parity in range(2):
+        pick = jnp.where(source == 2 * target + parity, 1.0, 0.0).astype(BF16)
+        kept[pl.ds(parity * PILOT, PILOT), :] = dot(kriging[...], pick, NN).astype(BF16)
     for x in range(FX):
         high, rest = split(jnp.concatenate([v[part(x), :], ap[part(x), :]], axis=0))
         table[: 2 * RHS, x * LANE : (x + 1) * LANE] = high
@@ -270,8 +277,9 @@
     m1, m3 = unpack_pair(packed[:RHS, RHS:], packed[RHS + 1 : RHS + 2, RHS:])
     first = eliminate(jnp.concatenate([m1, m0, m2], axis=1))
     alpha, shift = first[:, :RHS], first[:, RHS:]
-    curved = symmetric(m3 - exact(m2, shift))
-    target = m1 - exact(m2, alpha)
+    bent = exact(m2, first)
+    curved = symmetric(m3 - bent[:, RHS:])
+    target = m1 - bent[:, :RHS]
     gamma = eliminate(jnp.concatenate([curved, target], axis=1))
     mixed = alpha - exact(shift, gamma)
     both = jnp.concatenate([mixed, gamma], axis=0)
@@ -289,20 +297,13 @@
     later[...] = jnp.concatenate([m2, m3], axis=1)
 
 
-def gram_kernel(cell_total, packed, weights, later, kriging, gram, kept):
-    kept[...] = kriging[...]
+def product_kernel(cell_total, kriging, arrived, scale, packed, weights, later, sens, gram):
+    high, rest = split(arrived[...])
+    product = dot(kriging[...], high, NN) + dot(kriging[...], rest, NN)
+    sens[...] = (product[:PILOT, :RHS] + product[PILOT:, RHS:]) * scale[...]
     mixed, gamma = weights[:RHS, :], weights[RHS:, :]
     rest = exact(packed[RHS:, :RHS], gamma) + exact(later[:, RHS:], mixed) - later[:, :RHS]
     gram[...] = symmetric(exact(jnp.transpose(gamma), rest)) * (1.0 / cell_total)
-
-
-def product_kernel(kriging, arrived, scale, sens, rows):
-    half = FX * LANE // 2
-    value = arrived[...].astype(F32)
-    rows[pl.ds(0, half, stride=2), :] = value
-    rows[pl.ds(1, half, stride=2), :] = swap(value)
-    high, rest = split(rows[...])
-    sens[...] = (dot(kriging[...], high, NN) + dot(kriging[...], rest, NN))[:, :RHS] * scale[...]
 
 
 def call(kernel, shapes, *operands, scratch=(), flops=1000000, place=pltpu.VMEM):
@@ -391,10 +392,10 @@
     (packed,) = call(
         third_kernel, (((2 * RHS, LANE), F32),), ap, u, sh, sl, storage, *halo, base
     )
-    (cells,) = call(
+    cells, kriging = call(
         deal_kernel,
-        (((FX * LANE, 4 * RHS), BF16),),
-        *(tile_order, p, ap),
+        (((FX * LANE, 4 * RHS), BF16), ((2 * PILOT, FX * LANE // 2), BF16)),
+        *(tile_order, p, ap, kriging),
         scratch=(pltpu.VMEM((4 * RHS, FX * LANE), BF16),),
         flops=LONG,
     )
@@ -407,17 +408,10 @@
     )
     heads = heads.astype(jnp.float16).reshape(groups, -1, LANE)
     heads = lax.all_to_all(heads, "dom", 0, 0, tiled=True).reshape(-1, LANE).astype(F32)
-    gram, kriging = call(
-        lambda *refs: gram_kernel(cell_total, *refs),
-        (((RHS, RHS), F32), (kriging.shape, BF16)),
-        *(packed, weights, later, kriging),
-        flops=LONG,
-    )
-    (sens,) = call(
-        product_kernel,
-        (((kriging.shape[0], RHS), F32),),
-        *(kriging, heads, scale),
-        scratch=(scratch(FX * LANE),),
+    sens, gram = call(
+        lambda *refs: product_kernel(cell_total, *refs),
+        (((PILOT, RHS), F32), ((RHS, RHS), F32)),
+        *(kriging, heads, scale, packed, weights, later),
     )
     return sens, gram
 

time: 114 us -> 113 us (level)
  blocking collectives: 40.5 us -> 62.8 us
  waiting for transfers between devices: 23.4 us -> 6.72 us
  starting transfers between devices: 33.7 us -> 28.1 us
    all_to_all x0 -> x1, blocking collectives: none -> 22.3 us  [shards(): lax.all_to_all(heads, 'dom', 0, 0, tiled=True).reshape(-1, LANE).astype(F32)]
    all_to_all x1 -> x0, waiting for transfers between devices: 16.4 us -> none  [shards(): lax.all_to_all(heads, 'dom', 0, 0, tiled=True).reshape(-1, LANE).astype(F32)]
    all_to_all x1 -> x0, starting transfers between devices: 5.64 us -> none  [shards(): lax.all_to_all(heads, 'dom', 0, 0, tiled=True).reshape(-1, LANE).astype(F32)]
    pallas_call x8 -> x7, Pallas kernels: 13.5 us -> 13.1 us  [call(): pl.pallas_call(kernel, out_shape=[jax.ShapeDtypeStruct(shape, kind) for s...]
  transfers between devices with their start and end apart: 10 -> 9, of which waited for: 4 -> 3; matrix products, arithmetic and copies ran while one was open for 0% -> 0% of each run, Pallas kernels for 3% -> 2%
where the time goes in v13:
time: 113 us; the launch traced here: 112 us
  blocking collectives  62.8 us (56%)
  starting transfers between devices  28.1 us (25%)
  Pallas kernels  13.1 us (12%)
  waiting for transfers between devices  6.72 us (6%)
    all_to_all x2, blocking collectives, trade(): lax.all_to_all(array, axes, 0, 0, axis_index_groups=groups, tiled=True)  40.5 us
    all_to_all x1, blocking collectives, shards(): lax.all_to_all(heads, 'dom', 0, 0, tiled=True).reshape(-1, LANE).astype(F32)  22.3 us
    ppermute x4, starting transfers between devices, along(): return (lax.ppermute(one, axis, first), two)  13.8 us
    pallas_call x7, Pallas kernels, call(): pl.pallas_call(kernel, out_shape=[jax.ShapeDtypeStruct(shape, kind) for s...  13.1 us
    ppermute x4, starting transfers between devices, along(): two = lax.ppermute(two, axis, second)  8.88 us
    all_to_all x1, starting transfers between devices, trade(): lax.all_to_all(array, axes, 0, 0, axis_index_groups=groups, tiled=True)  5.41 us
    all_to_all x1, waiting for transfers between devices, trade(): lax.all_to_all(array, axes, 0, 0, axis_index_groups=groups, tiled=True)  5.41 us
  transfers between devices with their start and end apart: 9, of which 3 were waited for; matrix products, arithmetic and copies ran while one was open for 0% of the time, Pallas kernels for 2%

profile of v13, /device:TPU:1, one launch (start us, length us, event | category | flops | bytes accessed | tf_op | source)
XLA Modules:
  0.0 112.3 jit_solution(6585472804774148266)
XLA Ops:
  0.6 1.9 %shard_map.68 = (f32[512,128]{1,0:T(8,128)S(1)}, bf16[1024,128]{1,0:T(8,128)(2,1)S(1)}, bf16[1024,128]{1,0:T(8,128)(2,1)S(1)}, f32[512,128]{1,0:T(8,128)S(1)}, b...) custom-call(f32[16,4096]{1,0:T(8,128)} %pump_hbm.1, ...), custom_call_target="tpu_custom_call" | custom-call | flops 1000000 | bytes 1048576 | tf_op jit(solution)/shard_map/pallas_call | solution.py:310
  2.5 0.0 copy-start
  2.5 4.9 %collective-permute-start.1 = (bf16[272,128]{1,0:T(8,128)(2,1)S(1)}, bf16[272,128]{1,0:T(8,128)(2,1)S(1)}, u32[]{:S(2)}, u32[]{:S(2)}) collective-permute-start(bf16[272,128]{1,0:T(8,128)(2,1)S(1)} %get-tuple-element.27), channel_id=1, source_target_pairs={{4,8},{8,4},{12,16},{16,12},{20,24},{24,20},{28,32},{32,28},{36,40... | collective-permute-start | bytes 208904 | tf_op jit(solution)/shard_map/ppermute | solution.py:330
  7.5 3.2 %collective-permute-start.2 = (bf16[256,128]{1,0:T(8,128)(2,1)S(1)}, bf16[256,128]{1,0:T(8,128)(2,1)S(1)}, u32[]{:S(2)}, u32[]{:S(2)}) collective-permute-start(bf16[256,128]{1,0:T(8,128)(2,1)S(1)} %get-tuple-element.28), channel_id=1, source_target_pairs={{0,1},{1,0},{2,3},{3,2},{4,5},{5,4},{6,7},{7,6},{8,9},{9,8},{10,11... | collective-permute-start | bytes 196616 | tf_op jit(solution)/shard_map/ppermute | solution.py:331
  10.7 0.7 collective-permute-start.3
  11.3 3.2 %collective-permute-start = (bf16[64,128]{1,0:T(8,128)(2,1)S(1)}, bf16[64,128]{1,0:T(8,128)(2,1)S(1)}, u32[]{:S(2)}, u32[]{:S(2)}) collective-permute-start(bf16[64,128]{1,0:T(8,128)(2,1)S(1)} %get-tuple-element.26), channel_id=1, source_target_pairs={{0,4},{4,0},{8,12},{12,8},{16,20},{20,16},{24,28},{28,24},{32,36},... | collective-permute-start | bytes 49160 | tf_op jit(solution)/shard_map/ppermute | solution.py:331
  14.6 0.8 collective-permute-done.d1
  15.4 0.0 collective-permute-done.2.t1
  15.4 0.0 collective-permute-done.3.t2
  15.4 0.0 collective-permute-done.1.d2
  15.4 0.0 copy-done
  15.4 1.0 shard_map.69
  16.4 2.6 %collective-permute-start.5 = (bf16[272,128]{1,0:T(8,128)(2,1)S(1)}, bf16[272,128]{1,0:T(8,128)(2,1)S(1)}, u32[]{:S(2)}, u32[]{:S(2)}) collective-permute-start(bf16[272,128]{1,0:T(8,128)(2,1)S(1)} %get-tuple-element.34), channel_id=1, source_target_pairs={{4,8},{8,4},{12,16},{16,12},{20,24},{24,20},{28,32},{32,28},{36,40... | collective-permute-start | bytes 208904 | tf_op jit(solution)/shard_map/ppermute | solution.py:330
  19.1 5.5 %collective-permute-start.6 = (bf16[256,128]{1,0:T(8,128)(2,1)S(1)}, bf16[256,128]{1,0:T(8,128)(2,1)S(1)}, u32[]{:S(2)}, u32[]{:S(2)}) collective-permute-start(bf16[256,128]{1,0:T(8,128)(2,1)S(1)} %get-tuple-element.35), channel_id=1, source_target_pairs={{0,1},{1,0},{2,3},{3,2},{4,5},{5,4},{6,7},{7,6},{8,9},{9,8},{10,11... | collective-permute-start | bytes 196616 | tf_op jit(solution)/shard_map/ppermute | solution.py:331
  24.5 0.7 collective-permute-start.7
  25.2 1.9 %collective-permute-start.4 = (bf16[64,128]{1,0:T(8,128)(2,1)S(1)}, bf16[64,128]{1,0:T(8,128)(2,1)S(1)}, u32[]{:S(2)}, u32[]{:S(2)}) collective-permute-start(bf16[64,128]{1,0:T(8,128)(2,1)S(1)} %get-tuple-element.33), channel_id=1, source_target_pairs={{0,4},{4,0},{8,12},{12,8},{16,20},{20,16},{24,28},{28,24},{32,36},... | collective-permute-start | bytes 49160 | tf_op jit(solution)/shard_map/ppermute | solution.py:331
  27.1 0.7 shard_map.71.base
  27.8 0.5 collective-permute-done.4.d1
  28.3 0.0 collective-permute-done.6.t1
  28.3 0.0 collective-permute-done.7.t2
  28.3 0.0 collective-permute-done.5.d2
  28.3 1.2 %shard_map.72 = f32[128,128]{1,0:T(8,128)S(1)} custom-call(f32[512,128]{1,0:T(8,128)S(1)} %get-tuple-element.30.ap.v, f32[512,128]{1,0:T(8,128)S(1)} %get-tuple-element.32.u, bf16[1024,128]{1,0:T(8,128)(2,1)S(1)} %get-tuple-element.24.sh, bf16[1024,128]{1,0:T(8,128)(2,1)S(1)} %get-tuple-element.25.sl, f32[16,64]{1,0:T(8,128)S(1)} %copy-done, ...), custom_call_target="tpu_custom_call" | custom-call | flops 1000000 | bytes 1048576 | tf_op jit(solution)/shard_map/pallas_call | solution.py:310
  29.5 21.6 %all_to_all.20 = f32[32,4,128]{2,1,0:T(4,128)S(1)} all-to-all(f32[32,4,128]{2,1,0:T(4,128)S(1)} %bitcast.7), channel_id=1, replica_groups={{0,1,2,3,4,5,6,7,128,129,130,131,132,133,134,135,256,257,258,259,260,26..., dimensions={0} | all-to-all | bytes 131072 | tf_op jit(solution)/shard_map/all_to_all | solution.py:361
  51.1 18.9 %all_to_all.21 = f32[16,4,128]{2,1,0:T(4,128)S(1)} all-to-all(f32[16,4,128]{2,1,0:T(4,128)S(1)} %broadcast_in_dim.4), channel_id=1, replica_groups={{0,8,16,24,32,40,48,56,64,72,80,88,96,104,112,120},{1,9,17,25,33,41,49,..., dimensions={0} | all-to-all | bytes 65536 | tf_op jit(solution)/shard_map/all_to_all | solution.py:361
  70.0 0.6 broadcast_in_dim.5
  70.7 5.4 %all-to-all-start.2 = ((f32[32,4,128]{2,1,0:T(4,128)}), f32[32,4,128]{2,1,0:T(4,128)S(1)}, u32[]{:S(2)}, u32[]{:S(2)}) async-start(f32[32,4,128]{2,1,0:T(4,128)} %broadcast_in_dim.5), calls=%async_computation.2 | async-start | bytes 131072 | tf_op jit(solution)/shard_map/all_to_all | solution.py:361
  76.1 0.0 copy-done.1
  76.1 1.9 %shard_map.70 = (bf16[1024,256]{1,0:T(8,128)(2,1)S(1)}, bf16[32,512]{1,0:T(8,128)(2,1)S(1)}) custom-call(s32[1,1024]{1,0:T(1,128)S(1)} %copy-done.2, f32[512,128]{1,0:T(8,128)S(1)} %get-tuple-element.22.v.p, f32[512,128]{1,0:T(8,128)S(1)} %get-tuple-element.30.ap.v, bf16[16,1024]{1,0:T(8,128)(2,1)S(1)} %copy-done.1), custom_call_target="tpu_custom_call" | custom-call | flops 99999997952 | bytes 1048576 | tf_op jit(solution)/shard_map/pallas_call | solution.py:310
  78.0 5.4 %all-to-all-done.2 = f32[32,4,128]{2,1,0:T(4,128)S(1)} async-done(((f32[32,4,128]{2,1,0:T(4,128)}), f32[32,4,128]{2,1,0:T(4,128)S(1)}, u32[]{:S(2)}, u32[]{:S(2)}) %all-to-all-start.2) | async-done | bytes 65568 | tf_op jit(solution)/shard_map/all_to_all | solution.py:361
  83.4 5.3 %shard_map.73 = (f32[512,128]{1,0:T(8,128)S(1)}, f32[1,64]{1,0:T(1,128)S(1)}, f32[128,64]{1,0:T(8,128)S(1)}, f32[64,128]{1,0:T(8,128)S(1)}) custom-call(f32[128,128]{1,0:T(8,128)S(1)} %bitcast.5, bf16[1024,256]{1,0:T(8,128)(2,1)S(1)} %get-tuple-element.37.refs_1_), custom_call_target="tpu_custom_call" | custom-call | flops 1000000 | bytes 1048576 | tf_op jit(solution)/shard_map/pallas_call | solution.py:310
  88.8 22.3 %all_to_all.22 = f16[128,4,128]{2,1,0:T(4,128)(2,1)S(1)} all-to-all(f16[128,4,128]{2,1,0:T(4,128)(2,1)S(1)} %bitcast.8), channel_id=1, replica_groups=mesh['dom'=128,'tile'=4] {'dom'}, dimensions={0} | all-to-all | bytes 262144 | tf_op jit(solution)/shard_map/all_to_all | solution.py:410
  111.1 1.2 %shard_map.74 = (f32[16,64]{1,0:T(8,128)}, f32[64,64]{1,0:T(8,128)}) custom-call(bf16[32,512]{1,0:T(8,128)(2,1)S(1)} %get-tuple-element.31.refs_0_, f32[512,128]{1,0:T(8,128)S(1)} %convert.1.refs_1_, f32[1,64]{1,0:T(1,128)S(1)} %get-tuple-element.39.refs_2_, f32[128,128]{1,0:T(8,128)S(1)} %bitcast.6, f32[128,64]{1,0:T(8,128)S(1)} %get-tuple-element.40.refs_4_, ...), custom_call_target="tpu_custom_call" | custom-call | flops 1000000 | bytes 1048576 | tf_op jit(solution)/shard_map/pallas_call | solution.py:310
  (8 shorter events, 0.1 us)
Async XLA Ops:
  2.5 12.9 %copy-start = (f32[16,64]{1,0:T(8,128)S(1)}, f32[16,64]{1,0:T(8,128)}, u32[]{:S(2)}) copy-start(f32[16,64]{1,0:T(8,128)} %stor.3) | copy-start | bytes 12292
  2.5 12.9 %collective-permute-start.1 = (bf16[272,128]{1,0:T(8,128)(2,1)S(1)}, bf16[272,128]{1,0:T(8,128)(2,1)S(1)}, u32[]{:S(2)}, u32[]{:S(2)}) collective-permute-start(bf16[272,128]{1,0:T(8,128)(2,1)S(1)} %get-tuple-element.27), channel_id=1, source_target_pairs={{4,8},{8,4},{12,16},{16,12},{20,24},{24,20},{28,32},{32,28},{36,40... | collective-permute-start | bytes 208904 | tf_op jit(solution)/shard_map/ppermute | solution.py:330
  7.5 7.9 %collective-permute-start.2 = (bf16[256,128]{1,0:T(8,128)(2,1)S(1)}, bf16[256,128]{1,0:T(8,128)(2,1)S(1)}, u32[]{:S(2)}, u32[]{:S(2)}) collective-permute-start(bf16[256,128]{1,0:T(8,128)(2,1)S(1)} %get-tuple-element.28), channel_id=1, source_target_pairs={{0,1},{1,0},{2,3},{3,2},{4,5},{5,4},{6,7},{7,6},{8,9},{9,8},{10,11... | collective-permute-start | bytes 196616 | tf_op jit(solution)/shard_map/ppermute | solution.py:331
  10.7 4.7 %collective-permute-start.3 = (bf16[256,128]{1,0:T(8,128)(2,1)S(1)}, bf16[256,128]{1,0:T(8,128)(2,1)S(1)}, u32[]{:S(2)}, u32[]{:S(2)}) collective-permute-start(bf16[256,128]{1,0:T(8,128)(2,1)S(1)} %get-tuple-element.29), channel_id=1, source_target_pairs={{1,2},{2,1},{5,6},{6,5},{9,10},{10,9},{13,14},{14,13},{17,18},{18,... | collective-permute-start | bytes 196616 | tf_op jit(solution)/shard_map/ppermute | solution.py:330
  11.3 4.1 %collective-permute-start = (bf16[64,128]{1,0:T(8,128)(2,1)S(1)}, bf16[64,128]{1,0:T(8,128)(2,1)S(1)}, u32[]{:S(2)}, u32[]{:S(2)}) collective-permute-start(bf16[64,128]{1,0:T(8,128)(2,1)S(1)} %get-tuple-element.26), channel_id=1, source_target_pairs={{0,4},{4,0},{8,12},{12,8},{16,20},{20,16},{24,28},{28,24},{32,36},... | collective-permute-start | bytes 49160 | tf_op jit(solution)/shard_map/ppermute | solution.py:331
  16.4 11.8 %collective-permute-start.5 = (bf16[272,128]{1,0:T(8,128)(2,1)S(1)}, bf16[272,128]{1,0:T(8,128)(2,1)S(1)}, u32[]{:S(2)}, u32[]{:S(2)}) collective-permute-start(bf16[272,128]{1,0:T(8,128)(2,1)S(1)} %get-tuple-element.34), channel_id=1, source_target_pairs={{4,8},{8,4},{12,16},{16,12},{20,24},{24,20},{28,32},{32,28},{36,40... | collective-permute-start | bytes 208904 | tf_op jit(solution)/shard_map/ppermute | solution.py:330
  19.1 9.2 %collective-permute-start.6 = (bf16[256,128]{1,0:T(8,128)(2,1)S(1)}, bf16[256,128]{1,0:T(8,128)(2,1)S(1)}, u32[]{:S(2)}, u32[]{:S(2)}) collective-permute-start(bf16[256,128]{1,0:T(8,128)(2,1)S(1)} %get-tuple-element.35), channel_id=1, source_target_pairs={{0,1},{1,0},{2,3},{3,2},{4,5},{5,4},{6,7},{7,6},{8,9},{9,8},{10,11... | collective-permute-start | bytes 196616 | tf_op jit(solution)/shard_map/ppermute | solution.py:331
  24.5 3.8 %collective-permute-start.7 = (bf16[256,128]{1,0:T(8,128)(2,1)S(1)}, bf16[256,128]{1,0:T(8,128)(2,1)S(1)}, u32[]{:S(2)}, u32[]{:S(2)}) collective-permute-start(bf16[256,128]{1,0:T(8,128)(2,1)S(1)} %get-tuple-element.36), channel_id=1, source_target_pairs={{1,2},{2,1},{5,6},{6,5},{9,10},{10,9},{13,14},{14,13},{17,18},{18,... | collective-permute-start | bytes 196616 | tf_op jit(solution)/shard_map/ppermute | solution.py:330
  25.2 3.1 %collective-permute-start.4 = (bf16[64,128]{1,0:T(8,128)(2,1)S(1)}, bf16[64,128]{1,0:T(8,128)(2,1)S(1)}, u32[]{:S(2)}, u32[]{:S(2)}) collective-permute-start(bf16[64,128]{1,0:T(8,128)(2,1)S(1)} %get-tuple-element.33), channel_id=1, source_target_pairs={{0,4},{4,0},{8,12},{12,8},{16,20},{20,16},{24,28},{28,24},{32,36},... | collective-permute-start | bytes 49160 | tf_op jit(solution)/shard_map/ppermute | solution.py:331
  70.7 5.4 %copy-start.1 = (bf16[16,1024]{1,0:T(8,128)(2,1)S(1)}, bf16[16,1024]{1,0:T(8,128)(2,1)}, u32[]{:S(2)}) copy-start(bf16[16,1024]{1,0:T(8,128)(2,1)} %kriging.1) | copy-start | bytes 98308
  70.7 5.4 %copy-start.2 = (s32[1,1024]{1,0:T(1,128)S(1)}, s32[1,1024]{1,0:T(1,128)}, u32[]{:S(2)}) copy-start(s32[1,1024]{1,0:T(1,128)} %order.1) | copy-start | bytes 12292
  70.7 12.8 %all-to-all-start.2 = ((f32[32,4,128]{2,1,0:T(4,128)}), f32[32,4,128]{2,1,0:T(4,128)S(1)}, u32[]{:S(2)}, u32[]{:S(2)}) async-start(f32[32,4,128]{2,1,0:T(4,128)} %broadcast_in_dim.5), calls=%async_computation.2 | async-start | bytes 131072 | tf_op jit(solution)/shard_map/all_to_all | solution.py:361

commit v14 on v13

--- a/solution.py
+++ b/solution.py
@@ -397,7 +397,6 @@
         (((FX * LANE, 4 * RHS), BF16), ((2 * PILOT, FX * LANE // 2), BF16)),
         *(tile_order, p, ap, kriging),
         scratch=(pltpu.VMEM((4 * RHS, FX * LANE), BF16),),
-        flops=LONG,
     )
     packed = reduce_all(packed)
     heads, scale, weights, later = call(

time: 113 us -> 113 us (level)
  no operation moved by 1% of the time
where the time goes in v14:
time: 113 us; the launch traced here: 112 us
  blocking collectives  62.8 us (56%)
  starting transfers between devices  28.1 us (25%)
  Pallas kernels  13.1 us (12%)
  waiting for transfers between devices  6.72 us (6%)
    all_to_all x2, blocking collectives, trade(): lax.all_to_all(array, axes, 0, 0, axis_index_groups=groups, tiled=True)  40.5 us
    all_to_all x1, blocking collectives, shards(): lax.all_to_all(heads, 'dom', 0, 0, tiled=True).reshape(-1, LANE).astype(F32)  22.3 us
    ppermute x4, starting transfers between devices, along(): return (lax.ppermute(one, axis, first), two)  13.8 us
    pallas_call x7, Pallas kernels, call(): pl.pallas_call(kernel, out_shape=[jax.ShapeDtypeStruct(shape, kind) for s...  13.1 us
    ppermute x4, starting transfers between devices, along(): two = lax.ppermute(two, axis, second)  8.88 us
    all_to_all x1, starting transfers between devices, trade(): lax.all_to_all(array, axes, 0, 0, axis_index_groups=groups, tiled=True)  5.41 us
    all_to_all x1, waiting for transfers between devices, trade(): lax.all_to_all(array, axes, 0, 0, axis_index_groups=groups, tiled=True)  5.41 us
  transfers between devices with their start and end apart: 9, of which 3 were waited for; matrix products, arithmetic and copies ran while one was open for 0% of the time, Pallas kernels for 2%

profile of v14, /device:TPU:1, one launch (start us, length us, event | category | flops | bytes accessed | tf_op | source)
XLA Modules:
  0.0 112.3 jit_solution(9667093104708280427)
XLA Ops:
  0.6 1.9 %shard_map.68 = (f32[512,128]{1,0:T(8,128)S(1)}, bf16[1024,128]{1,0:T(8,128)(2,1)S(1)}, bf16[1024,128]{1,0:T(8,128)(2,1)S(1)}, f32[512,128]{1,0:T(8,128)S(1)}, b...) custom-call(f32[16,4096]{1,0:T(8,128)} %pump_hbm.1, ...), custom_call_target="tpu_custom_call" | custom-call | flops 1000000 | bytes 1048576 | tf_op jit(solution)/shard_map/pallas_call | solution.py:310
  2.5 0.0 copy-start
  2.5 4.9 %collective-permute-start.1 = (bf16[272,128]{1,0:T(8,128)(2,1)S(1)}, bf16[272,128]{1,0:T(8,128)(2,1)S(1)}, u32[]{:S(2)}, u32[]{:S(2)}) collective-permute-start(bf16[272,128]{1,0:T(8,128)(2,1)S(1)} %get-tuple-element.27), channel_id=1, source_target_pairs={{4,8},{8,4},{12,16},{16,12},{20,24},{24,20},{28,32},{32,28},{36,40... | collective-permute-start | bytes 208904 | tf_op jit(solution)/shard_map/ppermute | solution.py:330
  7.5 3.2 %collective-permute-start.2 = (bf16[256,128]{1,0:T(8,128)(2,1)S(1)}, bf16[256,128]{1,0:T(8,128)(2,1)S(1)}, u32[]{:S(2)}, u32[]{:S(2)}) collective-permute-start(bf16[256,128]{1,0:T(8,128)(2,1)S(1)} %get-tuple-element.28), channel_id=1, source_target_pairs={{0,1},{1,0},{2,3},{3,2},{4,5},{5,4},{6,7},{7,6},{8,9},{9,8},{10,11... | collective-permute-start | bytes 196616 | tf_op jit(solution)/shard_map/ppermute | solution.py:331
  10.7 0.7 collective-permute-start.3
  11.3 3.2 %collective-permute-start = (bf16[64,128]{1,0:T(8,128)(2,1)S(1)}, bf16[64,128]{1,0:T(8,128)(2,1)S(1)}, u32[]{:S(2)}, u32[]{:S(2)}) collective-permute-start(bf16[64,128]{1,0:T(8,128)(2,1)S(1)} %get-tuple-element.26), channel_id=1, source_target_pairs={{0,4},{4,0},{8,12},{12,8},{16,20},{20,16},{24,28},{28,24},{32,36},... | collective-permute-start | bytes 49160 | tf_op jit(solution)/shard_map/ppermute | solution.py:331
  14.6 0.8 collective-permute-done.d1
  15.4 0.0 collective-permute-done.2.t1
  15.4 0.0 collective-permute-done.3.t2
  15.4 0.0 collective-permute-done.1.d2
  15.4 0.0 copy-done
  15.4 1.0 shard_map.69
  16.4 2.6 %collective-permute-start.5 = (bf16[272,128]{1,0:T(8,128)(2,1)S(1)}, bf16[272,128]{1,0:T(8,128)(2,1)S(1)}, u32[]{:S(2)}, u32[]{:S(2)}) collective-permute-start(bf16[272,128]{1,0:T(8,128)(2,1)S(1)} %get-tuple-element.34), channel_id=1, source_target_pairs={{4,8},{8,4},{12,16},{16,12},{20,24},{24,20},{28,32},{32,28},{36,40... | collective-permute-start | bytes 208904 | tf_op jit(solution)/shard_map/ppermute | solution.py:330
  19.1 5.5 %collective-permute-start.6 = (bf16[256,128]{1,0:T(8,128)(2,1)S(1)}, bf16[256,128]{1,0:T(8,128)(2,1)S(1)}, u32[]{:S(2)}, u32[]{:S(2)}) collective-permute-start(bf16[256,128]{1,0:T(8,128)(2,1)S(1)} %get-tuple-element.35), channel_id=1, source_target_pairs={{0,1},{1,0},{2,3},{3,2},{4,5},{5,4},{6,7},{7,6},{8,9},{9,8},{10,11... | collective-permute-start | bytes 196616 | tf_op jit(solution)/shard_map/ppermute | solution.py:331
  24.5 0.7 collective-permute-start.7
  25.2 1.9 %collective-permute-start.4 = (bf16[64,128]{1,0:T(8,128)(2,1)S(1)}, bf16[64,128]{1,0:T(8,128)(2,1)S(1)}, u32[]{:S(2)}, u32[]{:S(2)}) collective-permute-start(bf16[64,128]{1,0:T(8,128)(2,1)S(1)} %get-tuple-element.33), channel_id=1, source_target_pairs={{0,4},{4,0},{8,12},{12,8},{16,20},{20,16},{24,28},{28,24},{32,36},... | collective-permute-start | bytes 49160 | tf_op jit(solution)/shard_map/ppermute | solution.py:331
  27.1 0.7 shard_map.71.base
  27.8 0.5 collective-permute-done.4.d1
  28.3 0.0 collective-permute-done.6.t1
  28.3 0.0 collective-permute-done.7.t2
  28.3 0.0 collective-permute-done.5.d2
  28.3 1.2 %shard_map.72 = f32[128,128]{1,0:T(8,128)S(1)} custom-call(f32[512,128]{1,0:T(8,128)S(1)} %get-tuple-element.30.ap.v, f32[512,128]{1,0:T(8,128)S(1)} %get-tuple-element.32.u, bf16[1024,128]{1,0:T(8,128)(2,1)S(1)} %get-tuple-element.24.sh, bf16[1024,128]{1,0:T(8,128)(2,1)S(1)} %get-tuple-element.25.sl, f32[16,64]{1,0:T(8,128)S(1)} %copy-done, ...), custom_call_target="tpu_custom_call" | custom-call | flops 1000000 | bytes 1048576 | tf_op jit(solution)/shard_map/pallas_call | solution.py:310
  29.5 21.6 %all_to_all.20 = f32[32,4,128]{2,1,0:T(4,128)S(1)} all-to-all(f32[32,4,128]{2,1,0:T(4,128)S(1)} %bitcast.7), channel_id=1, replica_groups={{0,1,2,3,4,5,6,7,128,129,130,131,132,133,134,135,256,257,258,259,260,26..., dimensions={0} | all-to-all | bytes 131072 | tf_op jit(solution)/shard_map/all_to_all | solution.py:361
  51.1 18.9 %all_to_all.21 = f32[16,4,128]{2,1,0:T(4,128)S(1)} all-to-all(f32[16,4,128]{2,1,0:T(4,128)S(1)} %broadcast_in_dim.4), channel_id=1, replica_groups={{0,8,16,24,32,40,48,56,64,72,80,88,96,104,112,120},{1,9,17,25,33,41,49,..., dimensions={0} | all-to-all | bytes 65536 | tf_op jit(solution)/shard_map/all_to_all | solution.py:361
  70.0 0.6 broadcast_in_dim.5
  70.7 5.4 %all-to-all-start.2 = ((f32[32,4,128]{2,1,0:T(4,128)}), f32[32,4,128]{2,1,0:T(4,128)S(1)}, u32[]{:S(2)}, u32[]{:S(2)}) async-start(f32[32,4,128]{2,1,0:T(4,128)} %broadcast_in_dim.5), calls=%async_computation.2 | async-start | bytes 131072 | tf_op jit(solution)/shard_map/all_to_all | solution.py:361
  76.1 0.0 copy-done.1
  76.1 1.9 %shard_map.70 = (bf16[1024,256]{1,0:T(8,128)(2,1)S(1)}, bf16[32,512]{1,0:T(8,128)(2,1)S(1)}) custom-call(s32[1,1024]{1,0:T(1,128)S(1)} %copy-done.2, f32[512,128]{1,0:T(8,128)S(1)} %get-tuple-element.22.v.p, f32[512,128]{1,0:T(8,128)S(1)} %get-tuple-element.30.ap.v, bf16[16,1024]{1,0:T(8,128)(2,1)S(1)} %copy-done.1), custom_call_target="tpu_custom_call" | custom-call | flops 1000000 | bytes 1048576 | tf_op jit(solution)/shard_map/pallas_call | solution.py:310
  78.0 5.4 %all-to-all-done.2 = f32[32,4,128]{2,1,0:T(4,128)S(1)} async-done(((f32[32,4,128]{2,1,0:T(4,128)}), f32[32,4,128]{2,1,0:T(4,128)S(1)}, u32[]{:S(2)}, u32[]{:S(2)}) %all-to-all-start.2) | async-done | bytes 65568 | tf_op jit(solution)/shard_map/all_to_all | solution.py:361
  83.4 5.3 %shard_map.73 = (f32[512,128]{1,0:T(8,128)S(1)}, f32[1,64]{1,0:T(1,128)S(1)}, f32[128,64]{1,0:T(8,128)S(1)}, f32[64,128]{1,0:T(8,128)S(1)}) custom-call(f32[128,128]{1,0:T(8,128)S(1)} %bitcast.5, bf16[1024,256]{1,0:T(8,128)(2,1)S(1)} %get-tuple-element.37.refs_1_), custom_call_target="tpu_custom_call" | custom-call | flops 1000000 | bytes 1048576 | tf_op jit(solution)/shard_map/pallas_call | solution.py:310
  88.8 22.3 %all_to_all.22 = f16[128,4,128]{2,1,0:T(4,128)(2,1)S(1)} all-to-all(f16[128,4,128]{2,1,0:T(4,128)(2,1)S(1)} %bitcast.8), channel_id=1, replica_groups=mesh['dom'=128,'tile'=4] {'dom'}, dimensions={0} | all-to-all | bytes 262144 | tf_op jit(solution)/shard_map/all_to_all | solution.py:409
  111.1 1.2 %shard_map.74 = (f32[16,64]{1,0:T(8,128)}, f32[64,64]{1,0:T(8,128)}) custom-call(bf16[32,512]{1,0:T(8,128)(2,1)S(1)} %get-tuple-element.31.refs_0_, f32[512,128]{1,0:T(8,128)S(1)} %convert.1.refs_1_, f32[1,64]{1,0:T(1,128)S(1)} %get-tuple-element.39.refs_2_, f32[128,128]{1,0:T(8,128)S(1)} %bitcast.6, f32[128,64]{1,0:T(8,128)S(1)} %get-tuple-element.40.refs_4_, ...), custom_call_target="tpu_custom_call" | custom-call | flops 1000000 | bytes 1048576 | tf_op jit(solution)/shard_map/pallas_call | solution.py:310
  (8 shorter events, 0.1 us)
Async XLA Ops:
  2.5 12.9 %copy-start = (f32[16,64]{1,0:T(8,128)S(1)}, f32[16,64]{1,0:T(8,128)}, u32[]{:S(2)}) copy-start(f32[16,64]{1,0:T(8,128)} %stor.3) | copy-start | bytes 12292
  2.5 12.9 %collective-permute-start.1 = (bf16[272,128]{1,0:T(8,128)(2,1)S(1)}, bf16[272,128]{1,0:T(8,128)(2,1)S(1)}, u32[]{:S(2)}, u32[]{:S(2)}) collective-permute-start(bf16[272,128]{1,0:T(8,128)(2,1)S(1)} %get-tuple-element.27), channel_id=1, source_target_pairs={{4,8},{8,4},{12,16},{16,12},{20,24},{24,20},{28,32},{32,28},{36,40... | collective-permute-start | bytes 208904 | tf_op jit(solution)/shard_map/ppermute | solution.py:330
  7.5 7.9 %collective-permute-start.2 = (bf16[256,128]{1,0:T(8,128)(2,1)S(1)}, bf16[256,128]{1,0:T(8,128)(2,1)S(1)}, u32[]{:S(2)}, u32[]{:S(2)}) collective-permute-start(bf16[256,128]{1,0:T(8,128)(2,1)S(1)} %get-tuple-element.28), channel_id=1, source_target_pairs={{0,1},{1,0},{2,3},{3,2},{4,5},{5,4},{6,7},{7,6},{8,9},{9,8},{10,11... | collective-permute-start | bytes 196616 | tf_op jit(solution)/shard_map/ppermute | solution.py:331
  10.7 4.7 %collective-permute-start.3 = (bf16[256,128]{1,0:T(8,128)(2,1)S(1)}, bf16[256,128]{1,0:T(8,128)(2,1)S(1)}, u32[]{:S(2)}, u32[]{:S(2)}) collective-permute-start(bf16[256,128]{1,0:T(8,128)(2,1)S(1)} %get-tuple-element.29), channel_id=1, source_target_pairs={{1,2},{2,1},{5,6},{6,5},{9,10},{10,9},{13,14},{14,13},{17,18},{18,... | collective-permute-start | bytes 196616 | tf_op jit(solution)/shard_map/ppermute | solution.py:330
  11.3 4.1 %collective-permute-start = (bf16[64,128]{1,0:T(8,128)(2,1)S(1)}, bf16[64,128]{1,0:T(8,128)(2,1)S(1)}, u32[]{:S(2)}, u32[]{:S(2)}) collective-permute-start(bf16[64,128]{1,0:T(8,128)(2,1)S(1)} %get-tuple-element.26), channel_id=1, source_target_pairs={{0,4},{4,0},{8,12},{12,8},{16,20},{20,16},{24,28},{28,24},{32,36},... | collective-permute-start | bytes 49160 | tf_op jit(solution)/shard_map/ppermute | solution.py:331
  16.4 11.8 %collective-permute-start.5 = (bf16[272,128]{1,0:T(8,128)(2,1)S(1)}, bf16[272,128]{1,0:T(8,128)(2,1)S(1)}, u32[]{:S(2)}, u32[]{:S(2)}) collective-permute-start(bf16[272,128]{1,0:T(8,128)(2,1)S(1)} %get-tuple-element.34), channel_id=1, source_target_pairs={{4,8},{8,4},{12,16},{16,12},{20,24},{24,20},{28,32},{32,28},{36,40... | collective-permute-start | bytes 208904 | tf_op jit(solution)/shard_map/ppermute | solution.py:330
  19.1 9.2 %collective-permute-start.6 = (bf16[256,128]{1,0:T(8,128)(2,1)S(1)}, bf16[256,128]{1,0:T(8,128)(2,1)S(1)}, u32[]{:S(2)}, u32[]{:S(2)}) collective-permute-start(bf16[256,128]{1,0:T(8,128)(2,1)S(1)} %get-tuple-element.35), channel_id=1, source_target_pairs={{0,1},{1,0},{2,3},{3,2},{4,5},{5,4},{6,7},{7,6},{8,9},{9,8},{10,11... | collective-permute-start | bytes 196616 | tf_op jit(solution)/shard_map/ppermute | solution.py:331
  24.5 3.8 %collective-permute-start.7 = (bf16[256,128]{1,0:T(8,128)(2,1)S(1)}, bf16[256,128]{1,0:T(8,128)(2,1)S(1)}, u32[]{:S(2)}, u32[]{:S(2)}) collective-permute-start(bf16[256,128]{1,0:T(8,128)(2,1)S(1)} %get-tuple-element.36), channel_id=1, source_target_pairs={{1,2},{2,1},{5,6},{6,5},{9,10},{10,9},{13,14},{14,13},{17,18},{18,... | collective-permute-start | bytes 196616 | tf_op jit(solution)/shard_map/ppermute | solution.py:330
  25.2 3.1 %collective-permute-start.4 = (bf16[64,128]{1,0:T(8,128)(2,1)S(1)}, bf16[64,128]{1,0:T(8,128)(2,1)S(1)}, u32[]{:S(2)}, u32[]{:S(2)}) collective-permute-start(bf16[64,128]{1,0:T(8,128)(2,1)S(1)} %get-tuple-element.33), channel_id=1, source_target_pairs={{0,4},{4,0},{8,12},{12,8},{16,20},{20,16},{24,28},{28,24},{32,36},... | collective-permute-start | bytes 49160 | tf_op jit(solution)/shard_map/ppermute | solution.py:331
  70.7 5.4 %copy-start.1 = (bf16[16,1024]{1,0:T(8,128)(2,1)S(1)}, bf16[16,1024]{1,0:T(8,128)(2,1)}, u32[]{:S(2)}) copy-start(bf16[16,1024]{1,0:T(8,128)(2,1)} %kriging.1) | copy-start | bytes 98308
  70.7 5.4 %copy-start.2 = (s32[1,1024]{1,0:T(1,128)S(1)}, s32[1,1024]{1,0:T(1,128)}, u32[]{:S(2)}) copy-start(s32[1,1024]{1,0:T(1,128)} %order.1) | copy-start | bytes 12292
  70.7 12.8 %all-to-all-start.2 = ((f32[32,4,128]{2,1,0:T(4,128)}), f32[32,4,128]{2,1,0:T(4,128)S(1)}, u32[]{:S(2)}, u32[]{:S(2)}) async-start(f32[32,4,128]{2,1,0:T(4,128)} %broadcast_in_dim.5), calls=%async_computation.2 | async-start | bytes 131072 | tf_op jit(solution)/shard_map/all_to_all | solution.py:361
